TPU v7x, 32 devices: a whole 2x2x4 slice. The times are simulated.
32 devices in a mesh: dp: 2 (over x), fsdp: 16 (over z, y, core).
Axes of the slice: x: 2, y: 2, z: 4, core: 2. Of those that a mesh axis runs over, the one named last changes fastest.
Arguments:
- hidden: bfloat16 [64, 64, 768], P(('dp', 'fsdp')), may hold values from -6 to 6
- lengths: int32 [64], P(('dp', 'fsdp')), may hold values from 5 to 32, as said below
- features: bfloat16 [64, 257, 1408], P(('dp', 'fsdp')), may hold values from -6 to 6
- cotangent: bfloat16 [64, 64, 768], P(('dp', 'fsdp')), may hold values from -6 to 6
- self_params: bfloat16 [2363392], P('fsdp')
- cross_params: bfloat16 [3346432], P('fsdp')
- ffn_params: bfloat16 [9449472], P('fsdp')
Outputs:
- mixed: bfloat16 [64, 64, 768], P(('dp', 'fsdp'))
- hidden_grad: bfloat16 [64, 64, 768], P(('dp', 'fsdp'))
- self_grad: float32 [2363392], P('fsdp')
- cross_grad: float32 [3346432], P('fsdp')
- ffn_grad: float32 [9449472], P('fsdp')
Inputs may be any that keep to these rules, and one draw needn't show every extreme that they name: lengths lie between 5 and 32; some item of every draw has 32.
All inputs are finite; a program needn't handle non-finite values.
Results may differ from a plain program's by a relative error of at most 0.017.
Values may be sent and summed in bfloat16 or wider, within the bound.
A program may use at most 384 MiB of HBM per device.

v0:
```python
from functools import partial
import math

import jax
import jax.numpy as jnp
from jax import lax
from jax.sharding import PartitionSpec as P

D = 768
HEADS = 12
HDIM = 64
F = 3072
E = 1408
NQ = 32


EPS = 1e-06
SCALE = 0.125


def self_layout():
    return [(D, D)] * 4 + [(D,)] * 5


def cross_layout():
    return [(D, D), (E, D), (E, D), (D, D)] + [(D,)] * 5


def ffn_layout():
    return [(D, F), (F,), (F, D), (D,), (D,), (D,)] * 2


def split_flat(flat_vec, layouts):
    pieces = []
    offset = 0
    for layout in layouts:
        amount = math.prod(layout)
        pieces.append(flat_vec[offset : offset + amount].reshape(layout))
        offset = offset + amount
    return pieces


def join_flat(pieces, length):
    flat_vec = jnp.concatenate([piece.reshape(-1) for piece in pieces])
    return jnp.pad(flat_vec, (0, length - flat_vec.shape[0]))


def regroup(flat_vec):
    groups = lax.axis_size("fsdp")
    replicas = lax.axis_size("dp")
    return flat_vec.reshape(groups, replicas, -1).transpose(1, 0, 2).reshape(-1)


def matmul(left, right):
    return jnp.dot(left, right, preferred_element_type=jnp.float32)


def matmul_left(left, right):
    return lax.dot_general(
        left, right, (((0,), (0,)), ((), ())), preferred_element_type=jnp.float32
    )


def matmul_right(left, right):
    return lax.dot_general(
        left, right, (((1,), (1,)), ((), ())), preferred_element_type=jnp.float32
    )


def column_sum(values):
    return jnp.sum(values.astype(jnp.float32), 0)


def layer_norm(values, gain, shift):
    average = jnp.mean(values, -1, keepdims=True)
    centered = values - average
    variance = jnp.mean(centered * centered, -1, keepdims=True)
    return centered * lax.rsqrt(variance + EPS) * gain + shift


def norm_backward(summed, gain, shift, grad_out):
    _, norm_pull = jax.vjp(layer_norm, summed, gain.astype(jnp.float32), shift.astype(jnp.float32))
    return norm_pull(grad_out)


def heads(rows, items):
    return rows.reshape(items, -1, HEADS, HDIM)


def score_block(query, keys, mask):
    scores = jnp.einsum("iqhd,ikhd->ihqk", query, keys, preferred_element_type=jnp.float32) * SCALE
    if mask is not None:
        scores = jnp.where(mask, scores, -1e30)
    return scores


def attend(query, keys, values, mask):
    scores = score_block(query, keys, mask)
    top_sum = jax.nn.logsumexp(scores, axis=-1)
    probs = jnp.exp(scores - top_sum[..., None]).astype(jnp.bfloat16)
    context = jnp.einsum("ihqk,ikhd->iqhd", probs, values, preferred_element_type=jnp.float32)
    return (context, top_sum)


def attend_back(query, keys, values, mask, top_sum, grad_context):
    probs = jnp.exp(score_block(query, keys, mask) - top_sum[..., None])
    grad_probs = jnp.einsum(
        "iqhd,ikhd->ihqk", grad_context, values, preferred_element_type=jnp.float32
    )
    inner = jnp.sum(probs * grad_probs, -1, keepdims=True)
    grad_scores = (probs * (grad_probs - inner)).astype(jnp.bfloat16)
    grad_query = (
        jnp.einsum("ihqk,ikhd->iqhd", grad_scores, keys, preferred_element_type=jnp.float32) * SCALE
    )
    grad_keys = (
        jnp.einsum("ihqk,iqhd->ikhd", grad_scores, query, preferred_element_type=jnp.float32)
        * SCALE
    )
    grad_values = jnp.einsum(
        "ihqk,iqhd->ikhd",
        probs.astype(jnp.bfloat16),
        grad_context,
        preferred_element_type=jnp.float32,
    )
    return (grad_query, grad_keys, grad_values)


def linear_back(inputs, weight, grad_out):
    return (matmul_left(inputs, grad_out), column_sum(grad_out), matmul_right(grad_out, weight))


def ffn_forward(rows, params):
    w_in, b_in, w_out, b_out, gain, shift = params
    rows_low = rows.astype(jnp.bfloat16)
    hidden_pre = matmul(rows_low, w_in) + b_in
    activated = jax.nn.gelu(hidden_pre, approximate=True).astype(jnp.bfloat16)
    summed = rows + (matmul(activated, w_out) + b_out)
    final = layer_norm(summed, gain.astype(jnp.float32), shift.astype(jnp.float32))
    return (final, (rows_low, hidden_pre, activated, summed))


def ffn_backward(grad_out, kept, params):
    w_in, b_in, w_out, b_out, gain, shift = params
    rows_low, hidden_pre, activated, summed = kept
    grad_sum, grad_gain, grad_shift = norm_backward(summed, gain, shift, grad_out)
    grad_branch = grad_sum.astype(jnp.bfloat16)
    grad_w_out, grad_b_out, grad_act = linear_back(activated, w_out, grad_branch)
    _, gelu_pull = jax.vjp(partial(jax.nn.gelu, approximate=True), hidden_pre)
    grad_pre = gelu_pull(grad_act)[0].astype(jnp.bfloat16)
    grad_w_in, grad_b_in, grad_rows = linear_back(rows_low, w_in, grad_pre)
    return (
        grad_sum + grad_rows,
        [grad_w_in, grad_b_in, grad_w_out, grad_b_out, grad_gain, grad_shift],
    )


def per_device(hidden, lengths, features, cotangent, self_params, cross_params, ffn_params):
    items, seq, width = hidden.shape
    self_full = lax.all_gather(self_params, "fsdp", axis=0, tiled=True)
    self_parts = split_flat(self_full, self_layout())
    w_q, w_k, w_v, w_o, b_q, b_v, b_o, gain_one, shift_one = self_parts
    positions = jnp.arange(seq)
    rows_at = positions[:, None]
    cols_at = positions[None, :]
    allowed = (cols_at < NQ)[None] | ((rows_at >= NQ) & (cols_at <= rows_at))[None] & (
        cols_at[None] < NQ + lengths[:, None, None]
    )
    allowed = allowed[:, None]
    inputs = hidden.reshape(-1, width)
    query_low = (matmul(inputs, w_q) + b_q).astype(jnp.bfloat16)
    key_low = matmul(inputs, w_k).astype(jnp.bfloat16)
    value_low = (matmul(inputs, w_v) + b_v).astype(jnp.bfloat16)
    context, self_top = attend(
        heads(query_low, items), heads(key_low, items), heads(value_low, items), allowed
    )
    context_low = context.reshape(-1, width).astype(jnp.bfloat16)
    summed_one = inputs.astype(jnp.float32) + (matmul(context_low, w_o) + b_o)
    first = layer_norm(summed_one, gain_one.astype(jnp.float32), shift_one.astype(jnp.float32))
    first_items = first.reshape(items, seq, width)
    query_rows = first_items[:, :NQ].reshape(-1, width)
    text_rows = first_items[:, NQ:].reshape(-1, width)
    cross_full = lax.all_gather(cross_params, "fsdp", axis=0, tiled=True)
    cross_parts = split_flat(cross_full, cross_layout())
    cross_wq, cross_wk, cross_wv, cross_wo, cross_bq, cross_bv, cross_bo, gain_two, shift_two = (
        cross_parts
    )
    query_in = query_rows.astype(jnp.bfloat16)
    image_rows = features.reshape(-1, features.shape[-1])
    cross_query = (matmul(query_in, cross_wq) + cross_bq).astype(jnp.bfloat16)
    cross_key = matmul(image_rows, cross_wk).astype(jnp.bfloat16)
    cross_value = (matmul(image_rows, cross_wv) + cross_bv).astype(jnp.bfloat16)
    cross_context, cross_top = attend(
        heads(cross_query, items), heads(cross_key, items), heads(cross_value, items), None
    )
    cross_low = cross_context.reshape(-1, width).astype(jnp.bfloat16)
    summed_two = query_rows + (matmul(cross_low, cross_wo) + cross_bo)
    second = layer_norm(summed_two, gain_two.astype(jnp.float32), shift_two.astype(jnp.float32))
    ffn_full = lax.all_gather(ffn_params, "fsdp", axis=0, tiled=True)
    ffn_parts = split_flat(ffn_full, ffn_layout())
    query_final, query_kept = ffn_forward(second, ffn_parts[:6])
    text_final, text_kept = ffn_forward(text_rows, ffn_parts[6:])
    mixed = jnp.concatenate(
        [query_final.reshape(items, NQ, width), text_final.reshape(items, -1, width)], 1
    ).astype(jnp.bfloat16)
    grad_items = cotangent.astype(jnp.float32)
    grad_query_final = grad_items[:, :NQ].reshape(-1, width)
    grad_text_final = grad_items[:, NQ:].reshape(-1, width)
    ffn_back = split_flat(lax.all_gather(ffn_params, "fsdp", axis=0, tiled=True), ffn_layout())
    grad_second, query_grads = ffn_backward(grad_query_final, query_kept, ffn_back[:6])
    grad_text, text_grads = ffn_backward(grad_text_final, text_kept, ffn_back[6:])
    ffn_flat_grad = join_flat(query_grads + text_grads, ffn_full.shape[0])
    ffn_grad = lax.psum_scatter(
        regroup(ffn_flat_grad), ("dp", "fsdp"), scatter_dimension=0, tiled=True
    )
    cross_back = split_flat(
        lax.all_gather(cross_params, "fsdp", axis=0, tiled=True), cross_layout()
    )
    grad_summed_two, grad_gain_two, grad_shift_two = norm_backward(
        summed_two, cross_back[7], cross_back[8], grad_second
    )
    grad_cross_out = grad_summed_two.astype(jnp.bfloat16)
    grad_cross_wo, grad_cross_bo, grad_cross_ctx = linear_back(
        cross_low, cross_back[3], grad_cross_out
    )
    grad_cq, grad_ck, grad_cv = attend_back(
        heads(cross_query, items),
        heads(cross_key, items),
        heads(cross_value, items),
        None,
        cross_top,
        heads(grad_cross_ctx.astype(jnp.bfloat16), items),
    )
    grad_cq = grad_cq.reshape(-1, width).astype(jnp.bfloat16)
    grad_ck = grad_ck.reshape(-1, width).astype(jnp.bfloat16)
    grad_cv = grad_cv.reshape(-1, width).astype(jnp.bfloat16)
    grad_cross_wq, grad_cross_bq, grad_query_in = linear_back(query_in, cross_back[0], grad_cq)
    grad_cross_wk = matmul_left(image_rows, grad_ck)
    grad_cross_wv = matmul_left(image_rows, grad_cv)
    grad_cross_bv = column_sum(grad_cv)
    grad_query_rows = grad_summed_two + grad_query_in
    cross_list = [
        grad_cross_wq,
        grad_cross_wk,
        grad_cross_wv,
        grad_cross_wo,
        grad_cross_bq,
        grad_cross_bv,
        grad_cross_bo,
        grad_gain_two,
        grad_shift_two,
    ]
    cross_flat_grad = join_flat(cross_list, cross_full.shape[0])
    cross_grad = lax.psum_scatter(
        regroup(cross_flat_grad), ("dp", "fsdp"), scatter_dimension=0, tiled=True
    )
    self_back = split_flat(lax.all_gather(self_params, "fsdp", axis=0, tiled=True), self_layout())
    grad_first = jnp.concatenate(
        [grad_query_rows.reshape(items, NQ, width), grad_text.reshape(items, -1, width)], 1
    ).reshape(-1, width)
    grad_summed_one, grad_gain_one, grad_shift_one = norm_backward(
        summed_one, self_back[7], self_back[8], grad_first
    )
    grad_attn = grad_summed_one.astype(jnp.bfloat16)
    grad_w_o, grad_b_o, grad_ctx = linear_back(context_low, self_back[3], grad_attn)
    grad_q, grad_k, grad_v = attend_back(
        heads(query_low, items),
        heads(key_low, items),
        heads(value_low, items),
        allowed,
        self_top,
        heads(grad_ctx.astype(jnp.bfloat16), items),
    )
    grad_q = grad_q.reshape(-1, width).astype(jnp.bfloat16)
    grad_k = grad_k.reshape(-1, width).astype(jnp.bfloat16)
    grad_v = grad_v.reshape(-1, width).astype(jnp.bfloat16)
    grad_w_q, grad_b_q, input_from_q = linear_back(inputs, self_back[0], grad_q)
    grad_w_k = matmul_left(inputs, grad_k)
    input_from_k = matmul_right(grad_k, self_back[1])
    grad_w_v, grad_b_v, input_from_v = linear_back(inputs, self_back[2], grad_v)
    hidden_grad = (
        (grad_summed_one + input_from_q + input_from_k + input_from_v)
        .reshape(items, seq, width)
        .astype(jnp.bfloat16)
    )
    self_list = [
        grad_w_q,
        grad_w_k,
        grad_w_v,
        grad_w_o,
        grad_b_q,
        grad_b_v,
        grad_b_o,
        grad_gain_one,
        grad_shift_one,
    ]
    self_flat_grad = join_flat(self_list, self_full.shape[0])
    self_grad = lax.psum_scatter(
        regroup(self_flat_grad), ("dp", "fsdp"), scatter_dimension=0, tiled=True
    )
    self_grad, cross_grad, ffn_grad = (
        lax.all_gather(self_grad.astype(jnp.bfloat16), "dp", axis=0, tiled=True).astype(
            self_grad.dtype
        ),
        lax.all_gather(cross_grad.astype(jnp.bfloat16), "dp", axis=0, tiled=True).astype(
            cross_grad.dtype
        ),
        lax.all_gather(ffn_grad.astype(jnp.bfloat16), "dp", axis=0, tiled=True).astype(
            ffn_grad.dtype
        ),
    )
    return (mixed, hidden_grad, self_grad, cross_grad, ffn_grad)


def solution(mesh):
    return jax.shard_map(
        per_device,
        mesh=mesh,
        in_specs=(
            P(("dp", "fsdp"), None, None),
            P(("dp", "fsdp")),
            P(("dp", "fsdp"), None, None),
            P(("dp", "fsdp"), None, None),
            P("fsdp"),
            P("fsdp"),
            P("fsdp"),
        ),
        out_specs=(
            P(("dp", "fsdp"), None, None),
            P(("dp", "fsdp"), None, None),
            P("fsdp"),
            P("fsdp"),
            P("fsdp"),
        ),
        check_vma=False,
    )
```

profile of v0, /device:TPU:0, one launch (start us, length us, event | category | flops | bytes accessed | tf_op | source)
XLA Modules:
  0.0 2604.6 jit_solution(10896527017699016095)
XLA Ops:
  17.5 14.2 reshape.500
  35.5 60.6 %all-gather.11.cloned.1.call-done = bf16[16,1,147712]{2,1,0:T(2,128)(2,1)} async-done(((bf16[1,1,147712]{2,1,0:T(2,128)(2,1)}), bf16[16,1,147712]{2,1,0:T(2,128)(2,1)}) %all-gather.11.cloned.1.call-update) | async-done | bytes 4726800 | tf_op jit(solution)/shard_map/all_gather | solution.py:159
  96.1 78.1 %reduce.11 = bf16[16,147712]{1,0:T(8,128)(2,1)} reduce(bf16[16,1,147712]{2,1,0:T(2,128)(2,1)} %all-gather.11.cloned.1.call-done, bf16[]{:T(256)} %constant.79), dimensions={1}, to_apply=%all-gather.reduce_sub_computation | reduce | bytes 9453570 | tf_op jit(solution)/shard_map/all_gather | solution.py:159
  174.2 10.1 reshape.497
  209.2 141.5 %reduce.12 = bf16[16,209152]{1,0:T(8,128)(2,1)} reduce(bf16[16,1,209152]{2,1,0:T(2,128)(2,1)} %all-gather.13.cloned.1.call-done, bf16[]{:T(256)} %constant.79), dimensions={1}, to_apply=%all-gather.1.reduce_sub_computation | reduce | bytes 13385730 | tf_op jit(solution)/shard_map/all_gather | solution.py:182
  350.8 14.0 reshape.499
  420.2 400.6 %reduce.13 = bf16[16,590592]{1,0:T(8,128)(2,1)} reduce(bf16[16,1,590592]{2,1,0:T(2,128)(2,1)} %all-gather.15.cloned.1.call-done, bf16[]{:T(256)} %constant.79), dimensions={1}, to_apply=%all-gather.2.reduce_sub_computation | reduce | bytes 37797888 | tf_op jit(solution)/shard_map/all_gather | solution.py:198
  820.8 43.1 %reshape.501 = bf16[9449472]{0:T(1024)(128)(2,1)} reshape(bf16[16,590592]{1,0:T(8,128)(2,1)} %reduce.13) | data formatting | bytes 37797888
  863.9 14.0 fusion.71
  1047.3 10.3 reshape.482
  1148.6 13.4 reshape.488
  1162.0 10.4 copy.156
  1192.0 10.8 reshape.491
  1210.0 10.8 reshape.493
  1233.6 80.5 %dynamic-update-slice.6 = f32[9447936]{0:T(1024)} dynamic-update-slice(f32[9447936]{0:T(1024)} %constant_dynamic-update-slice_fusion.25, f32[2359296]{0:T(1024)} %bitcast.168, s32[]{} %constant.91) | dynamic-update-slice | bytes 18874372
  1315.4 80.5 %dynamic-update-slice.8 = f32[9447936]{0:T(1024)} dynamic-update-slice(f32[9447936]{0:T(1024)} %constant_dynamic-update-slice_fusion.24, f32[2359296]{0:T(1024)} %reshape.493, s32[]{} %constant.93) | dynamic-update-slice | bytes 18874372
  1399.8 27.1 %pad.14 = f32[9449472]{0:T(1024)} pad(f32[9447936]{0:T(1024)} %constant_dynamic-update-slice_fusion.21, f32[]{:T(128)} %constant.23.clone.1), padding=0_1536 | pad | bytes 75589632 | tf_op jit(solution)/shard_map/jit(_pad)/pad | solution.py:45
  1426.9 59.6 %reshape.494 = f32[16,2,295296]{2,1,0:T(2,128)} reshape(f32[9449472]{0:T(1024)} %pad.14) | data formatting | bytes 75595776 | tf_op jit(solution)/shard_map/reshape | solution.py:51
  1486.5 29.9 %copy.157 = f32[2,16,295296]{2,1,0:T(8,128)} copy(f32[2,16,295296]{2,0,1:T(2,128)} %bitcast.161) | data formatting | bytes 75595776 | tf_op jit(solution)/shard_map/transpose | solution.py:51
  1516.4 31.6 %reshape.495 = f32[9449472]{0:T(1024)} reshape(f32[2,16,295296]{2,1,0:T(8,128)} %copy.157) | data formatting | bytes 75595776 | tf_op jit(solution)/shard_map/reshape | solution.py:51
  1548.0 960.9 %all-reduce.8 = (bf16[2363392]{0:T(1024)(128)(2,1)}, bf16[3346432]{0:T(1024)(128)(2,1)}, bf16[9449472]{0:T(1024)(128)(2,1)}) all-reduce(f32[2363392]{0:T(1024)} %reshape.483, f32[3346432]{0:T(1024)} %reshape.489, f32[9449472]{0:T(1024)} %reshape.495), channel_id=2, replica_groups=mesh['dp'=2,'fsdp'=16] {'dp','fsdp'}, use_global_device_ids=true, to_apply=%region_28.29.clone | all-reduce | flops 15159296 | bytes 90955776
  2531.3 14.9 all-gather.4
  2557.1 10.7 all-gather.17.cloned.1.call-done
  2567.8 26.9 %convert_reduce_fusion = f32[2,295296]{1,0:T(2,128)S(1)} fusion(bf16[2,1,295296]{2,1,0:T(2,128)(2,1)} %all-gather.17.cloned.1.call-done), kind=kLoop, calls=%fused_computation.6 | loop fusion | flops 590592 | bytes 3543552 | tf_op jit(solution)/shard_map/convert_element_type | solution.py:307
  (496 shorter events, 434.8 us)
Async XLA Ops:
  7.2 10.3 copy-start.56
  7.2 88.9 %all-gather.11.cloned.1.call-start = ((), (), s32[]{:S(2)}) async-start(), calls=%async_computation | async-start | bytes 10044416 | tf_op jit(solution)/shard_map/all_gather | solution.py:159
  11.7 197.5 %all-gather.13.cloned.1.call-start = ((), (), s32[]{:S(2)}) async-start(), calls=%async_computation.1 | async-start | bytes 14222336 | tf_op jit(solution)/shard_map/all_gather | solution.py:182
  17.4 14.4 copy-start.34
  17.4 402.8 %all-gather.15.cloned.1.call-start = ((), (), s32[]{:S(2)}) async-start(), calls=%async_computation.2 | async-start | bytes 40160256 | tf_op jit(solution)/shard_map/all_gather | solution.py:198
  31.7 2536.1 %all-gather.17.cloned.1.call-start = ((), (), s32[]{:S(2)}) async-start(), calls=%async_computation.3 | async-start | bytes 3543552 | tf_op jit(solution)/shard_map/all_gather | solution.py:307
  204.9 145.9 %copy-start.7 = (bf16[768,768]{1,0:T(8,128)(2,1)}, bf16[768,768]{1,0:T(8,128)(2,1)S(1)}, u32[]{:S(2)}) copy-start(bf16[768,768]{1,0:T(8,128)(2,1)S(1)} %reshape.456) | copy-start | bytes 3538948
  207.8 143.0 %copy-start.44 = (f32[2,32,768]{2,1,0:T(8,128)}, f32[2,32,768]{2,1,0:T(8,128)S(1)}, u32[]{:S(2)}) copy-start(f32[2,32,768]{2,1,0:T(8,128)S(1)} %get-tuple-element.72) | copy-start | bytes 589828
  208.6 196.8 %copy-start.59 = (bf16[2,32,768]{2,1,0:T(8,128)(2,1)}, bf16[2,32,768]{2,1,0:T(8,128)(2,1)S(1)}, u32[]{:S(2)}) copy-start(bf16[2,32,768]{2,1,0:T(8,128)(2,1)S(1)} %get-tuple-element.69) | copy-start | bytes 294916
  898.2 12.2 slice-start.2
  901.8 8.5 slice-start.3
  992.6 12.9 copy-start.40
  994.2 19.5 copy-start.46
  1192.0 10.8 copy-start.51
  1192.0 10.8 copy-start.64
  1210.0 10.8 copy-start.113
  1221.4 9.6 copy-start.102
  1221.4 11.0 copy-start.101
  1233.6 80.5 %copy-start.114 = (f32[3072]{0:T(1024)S(1)}, f32[3072]{0:T(1024)}, u32[]{:S(2)}) copy-start(f32[3072]{0:T(1024)} %get-tuple-element.21) | copy-start | bytes 36868
  1315.4 80.5 %copy-start.105 = (f32[768]{0:T(1024)S(1)}, f32[768]{0:T(1024)}, u32[]{:S(2)}) copy-start(f32[768]{0:T(1024)} %get-tuple-element.19) | copy-start | bytes 9220
  1315.4 81.8 %copy-start.104 = (f32[768]{0:T(1024)S(1)}, f32[768]{0:T(1024)}, u32[]{:S(2)}) copy-start(f32[768]{0:T(1024)} %get-tuple-element.7) | copy-start | bytes 9220
  1315.4 83.1 %copy-start.100 = (f32[768]{0:T(1024)S(1)}, f32[768]{0:T(1024)}, u32[]{:S(2)}) copy-start(f32[768]{0:T(1024)} %get-tuple-element.13) | copy-start | bytes 9220
  2546.2 8.5 copy-start.39
  2546.2 8.5 copy-start.122
  (115 other events, 385.5 us)
Sparse Core Ops, SparseCore 0:
  11.8 84.2 all-gather.10
  98.9 103.9 all-gather.12
  205.1 186.1 all-gather.14
  2531.4 36.2 all-gather.16
where the time goes:
time: 2630 us; the launch traced here: 2600 us
  blocking collectives  984 us (37%)
  local copies, waits for them, and re-layouts  767 us (29%)
  other arithmetic  672 us (26%)
  matrix products  94.1 us (4%)
  waiting for transfers between devices  71.3 us (3%)
    unnamed x1, blocking collectives  961 us
    all_gather x1, other arithmetic, per_device(): ffn_full = lax.all_gather(ffn_params, 'fsdp', axis=0, tiled=True)  401 us
    unnamed x312, local copies, waits for them, and re-layouts  337 us
    all_gather x1, other arithmetic, per_device(): cross_full = lax.all_gather(cross_params, 'fsdp', axis=0, tiled=True)  142 us
    reshape x6, local copies, waits for them, and re-layouts, regroup(): return flat_vec.reshape(groups, replicas, -1).transpose(1, 0, 2).reshape(-1)  133 us
    all_gather x1, other arithmetic, per_device(): self_full = lax.all_gather(self_params, 'fsdp', axis=0, tiled=True)  78.1 us
    all_gather x1, waiting for transfers between devices, per_device(): self_full = lax.all_gather(self_params, 'fsdp', axis=0, tiled=True)  60.6 us
  transfers between devices with their start and end apart: 4, of which 2 were waited for; matrix products, arithmetic and copies ran while one was open for 14% of the time, Pallas kernels for 0%

commit v1 on v0

--- a/solution.py
+++ b/solution.py
@@ -4,6 +4,8 @@
 import jax
 import jax.numpy as jnp
 from jax import lax
+from jax.experimental import pallas as pl
+from jax.experimental.pallas import tpu as pltpu
 from jax.sharding import PartitionSpec as P
 
 D = 768
@@ -311,9 +313,743 @@
     return (mixed, hidden_grad, self_grad, cross_grad, ffn_grad)
 
 
+MESH = pl.DeviceIdType.MESH
+BF = jnp.bfloat16
+F32 = jnp.float32
+VMEM_BYTES = 62 * 2**20
+
+
+def place():
+    f = lax.axis_index("fsdp")
+    return lax.axis_index("dp"), f // 4, (f // 2) % 2, f % 2
+
+
+def device(x, z, y, c):
+    return (x, (z * 2 + y) * 2 + c)
+
+
+def meet(devices):
+    barrier = pltpu.get_barrier_semaphore()
+    for d in devices:
+        pl.semaphore_signal(barrier, inc=1, device_id=d, device_id_type=MESH)
+    pl.semaphore_wait(barrier, len(devices))
+
+
+def neighbours(x, z, y, c):
+    return [
+        device(x, z, y, 1 - c),
+        device(1 - x, z, y, c),
+        device(x, z, 1 - y, c),
+        device(x, (z + 1) % 4, y, c),
+        device(x, (z + 2) % 4, y, c),
+        device(x, (z + 3) % 4, y, c),
+    ]
+
+
+def remote(src, dst, send, recv, target):
+    return pltpu.make_async_remote_copy(
+        src_ref=src,
+        dst_ref=dst,
+        send_sem=send,
+        recv_sem=recv,
+        device_id=target,
+        device_id_type=MESH,
+    )
+
+
+def gather_kernel(own_s, own_c, own_f, all_s, all_c, all_f, block_f, loc, *sems):
+    x, z, y, c = place()
+    core, xn, yn = device(x, z, y, 1 - c), device(1 - x, z, y, c), device(x, z, 1 - y, c)
+    meet(neighbours(x, z, y, c))
+
+    def part_s(zz, yy, cc, h):
+        rows = pl.ds(pl.multiple_of(192 * (2 * yy + cc), 192), 192)
+        if h is None:
+            return all_s.at[zz, rows]
+        return all_s.at[zz, rows, pl.ds(pl.multiple_of(384 * h, 384), 384)]
+
+    def part_c(zz, yy, cc, h):
+        rows = pl.ds(pl.multiple_of(272 * ((zz * 2 + yy) * 2 + cc), 16), 272)
+        if h is None:
+            return all_c.at[rows]
+        return all_c.at[rows, pl.ds(pl.multiple_of(384 * h, 384), 384)]
+
+    def part_f(zz, yy):
+        return all_f.at[zz, pl.ds(pl.multiple_of(384 * yy, 384), 384)]
+
+    sent = []
+    (zs, zr, ys, yr, xs, xr, cs, cr) = sems
+
+    def go(src, dst, send, recv, target):
+        copy = remote(src, dst, send, recv, target)
+        copy.start()
+        sent.append(copy)
+
+    def arrived(view, recv):
+        remote(view, view, recv, recv, core).wait_recv()
+
+    half = pl.ds(pl.multiple_of(384 * x, 384), 384)
+    groups = [(0, own_s, part_s), (1, own_c, part_c)]
+
+    fb = pl.ds(pl.multiple_of(192 * c, 192), 192)
+    w1 = z % 2 == 0
+
+    def start_own(g, own, part):
+        for k in (1, 2, 3):
+            go(own.at[:, half], part(z, y, c, x), zs.at[g, k], zr.at[g, k], device(x, (z + k) % 4, y, c))
+        go(own.at[:, half], part(z, y, c, x), ys.at[g, 0], yr.at[g, 0], yn)
+        go(own, part(z, y, c, None), cs.at[g, 0], cr.at[g, 0], core)
+
+    locals_ = []
+    for g, own, part in groups:
+        start_own(g, own, part)
+        copy = pltpu.make_async_copy(own, part(z, y, c, None), loc.at[g])
+        copy.start()
+        locals_.append(copy)
+
+    @pl.when(w1)
+    def _():
+        copy = remote(own_f.at[1], block_f.at[fb], cs.at[2, 0], cr.at[2, 0], core)
+        copy.start()
+        mine = pltpu.make_async_copy(own_f.at[0], block_f.at[fb], loc.at[2])
+        mine.start()
+        mine.wait()
+        copy.wait()
+
+    @pl.when(jnp.logical_not(w1))
+    def _():
+        for j in range(2):
+            mine = pltpu.make_async_copy(own_f.at[j], block_f.at[pl.ds(192 * j, 192)], loc.at[2])
+            mine.start()
+            mine.wait()
+
+    for k in (1, 2, 3):
+        go(block_f, part_f(z, y), zs.at[2, k], zr.at[2, k], device(x, (z + k) % 4, y, c))
+    go(block_f, part_f(z, y), ys.at[2, 0], yr.at[2, 0], yn)
+    copy = pltpu.make_async_copy(block_f, part_f(z, y), loc.at[2])
+    copy.start()
+    locals_.append(copy)
+
+    def z_arrivals(g, part):
+        for k in (1, 2, 3):
+            view = part((z - k) % 4, y, c, x)
+            arrived(view, zr.at[g, k])
+            go(view, view, ys.at[g, k], yr.at[g, k], yn)
+            go(view, view, xs.at[g, k - 1], xr.at[g, k - 1], xn)
+            go(view, view, cs.at[g, k], cr.at[g, k], core)
+
+    def y_arrivals(g, part):
+        for j in range(4):
+            view = part((z - j) % 4, 1 - y, c, x)
+            arrived(view, yr.at[g, j])
+            go(view, view, xs.at[g, 3 + j], xr.at[g, 3 + j], xn)
+            go(view, view, cs.at[g, 4 + j], cr.at[g, 4 + j], core)
+
+    def x_arrivals(g, part):
+        for j in range(7):
+            view = part((z - j - 1) % 4, y, c, 1 - x) if j < 3 else part((z - j + 3) % 4, 1 - y, c, 1 - x)
+            arrived(view, xr.at[g, j])
+            go(view, view, cs.at[g, 8 + j], cr.at[g, 8 + j], core)
+
+    def core_arrivals(g, part):
+        for j in range(15):
+            if j == 0:
+                view = part(z, y, 1 - c, None)
+            elif j < 4:
+                view = part((z - j) % 4, y, 1 - c, x)
+            elif j < 8:
+                view = part((z - j + 4) % 4, 1 - y, 1 - c, x)
+            elif j < 11:
+                view = part((z - j + 7) % 4, y, 1 - c, 1 - x)
+            else:
+                view = part((z - j + 11) % 4, 1 - y, 1 - c, 1 - x)
+            arrived(view, cr.at[g, j])
+
+    z_arrivals(0, part_s)
+    z_arrivals(1, part_c)
+    y_arrivals(0, part_s)
+    for k in (1, 2, 3):
+        view = part_f((z - k) % 4, y)
+        arrived(view, zr.at[2, k])
+        go(view, view, ys.at[2, k], yr.at[2, k], yn)
+    y_arrivals(1, part_c)
+    x_arrivals(0, part_s)
+    x_arrivals(1, part_c)
+    for j in range(4):
+        arrived(part_f((z - j) % 4, 1 - y), yr.at[2, j])
+    core_arrivals(0, part_s)
+    core_arrivals(1, part_c)
+    for copy in locals_:
+        copy.wait()
+    for copy in sent:
+        copy.wait_send()
+
+
+def gather_weights(own_s, own_c, own_f):
+    dma = pltpu.SemaphoreType.DMA
+    anywhere = pl.BlockSpec(memory_space=pl.ANY)
+    return pl.pallas_call(
+        gather_kernel,
+        out_shape=(
+            jax.ShapeDtypeStruct((4, D, D), BF),
+            jax.ShapeDtypeStruct((4352, D), BF),
+            jax.ShapeDtypeStruct((4, D, D), BF),
+            jax.ShapeDtypeStruct((384, D), BF),
+        ),
+        in_specs=[anywhere] * 3,
+        out_specs=[anywhere] * 4,
+        scratch_shapes=[
+            dma((3,)),
+            dma((3, 4)),
+            dma((3, 4)),
+            dma((3, 4)),
+            dma((3, 4)),
+            dma((2, 7)),
+            dma((2, 7)),
+            dma((3, 15)),
+            dma((3, 15)),
+        ],
+        compiler_params=pltpu.CompilerParams(collective_id=0, has_side_effects=True),
+    )(own_s, own_c, own_f)[:3]
+
+
+def mm(a, b):
+    return jnp.dot(a, b, preferred_element_type=F32)
+
+
+def mm_nt(a, b):
+    return lax.dot_general(a, b, (((1,), (1,)), ((), ())), preferred_element_type=F32)
+
+
+def mm_tn(a, b):
+    return lax.dot_general(a, b, (((0,), (0,)), ((), ())), preferred_element_type=F32)
+
+
+def normed(v):
+    centered = v - jnp.mean(v, -1, keepdims=True)
+    r = lax.rsqrt(jnp.mean(centered * centered, -1, keepdims=True) + EPS)
+    return centered * r, r
+
+
+def norm_back(v, gain, g_out):
+    xh, r = normed(v)
+    gg = g_out * gain
+    dv = r * (gg - jnp.mean(gg, -1, keepdims=True) - xh * jnp.mean(gg * xh, -1, keepdims=True))
+    return dv, jnp.sum(g_out * xh, 0, keepdims=True), jnp.sum(g_out, 0, keepdims=True)
+
+
+GELU_A = math.sqrt(2.0 / math.pi)
+GELU_B = 0.044715
+
+
+def gelu(v):
+    return 0.5 * v * (1.0 + jnp.tanh(GELU_A * (v + GELU_B * (v * v * v))))
+
+
+def gelu_slope(v):
+    t = jnp.tanh(GELU_A * (v + GELU_B * (v * v * v)))
+    return 0.5 * (1.0 + t) + 0.5 * v * (1.0 - t * t) * (GELU_A * (1.0 + 3.0 * GELU_B * (v * v)))
+
+
+def head_mask(h):
+    lane = lax.broadcasted_iota(jnp.int32, (1, 256), 1)
+    return jnp.where(lane // HDIM == h, 1.0, 0.0)
+
+
+def spread(rows):
+    wide = rows.astype(F32)
+    return jnp.concatenate([(wide * head_mask(h)).astype(BF) for h in range(4)], 0)
+
+
+def fold(stacked):
+    n = stacked.shape[0] // 4
+    total = stacked[:n] * head_mask(0)
+    for h in range(1, 4):
+        total = total + stacked[h * n : (h + 1) * n] * head_mask(h)
+    return total
+
+
+def attend_block(q, k, v, allowed):
+    s = mm_nt(spread(q), k) * SCALE
+    s = jnp.where(allowed > 0.5, s, -1e30)
+    e = jnp.exp(s - jnp.max(s, -1, keepdims=True))
+    p = e / jnp.sum(e, -1, keepdims=True)
+    return p, fold(mm(p.astype(BF), v)).astype(BF)
+
+
+def attend_block_back(q, k, v, p, da):
+    dax = spread(da)
+    dp = mm_nt(dax, v)
+    ds = (p * (dp - jnp.sum(p * dp, -1, keepdims=True))).astype(BF)
+    dq = (fold(mm(ds, k)) * SCALE).astype(BF)
+    dk = (mm_tn(ds, spread(q)) * SCALE).astype(BF)
+    dv = mm_tn(p.astype(BF), dax).astype(BF)
+    return dq, dk, dv
+
+
+def rows_of(ref, first):
+    return jnp.concatenate([ref[first : first + 32], ref[64 + first : 96 + first]], 0)
+
+
+def compute_kernel(
+    hid, allowed, feat, cot, vec, ws, wc, wf,
+    mixed, hgrad, gs, gc, gf, vg,
+    q_s, k_s, v_s, a_s, p_s, sum1, first,
+    cq_s, ck_s, cv_s, ca_s, p_c, sum2, second,
+    xg, pre, act, part, send_p, recv_p, send_x, recv_x, sum3, gb, dsum3, dfirst,
+    dq_s, dk_s, dv_s, dck, dcv, ex_s, ex_r, rs_s, rs_r,
+):
+    x, z, y, c = place()
+    core, xn = device(x, z, y, 1 - c), device(1 - x, z, y, c)
+    meet([core, xn])
+
+    def slot(xx, cc):
+        return 2 * cc + xx
+
+    def exchange(phase, buf):
+        me, xs_, ps_, ds_ = slot(x, c), slot(1 - x, c), slot(x, 1 - c), slot(1 - x, 1 - c)
+        to_x = remote(buf.at[me], buf.at[me], ex_s.at[phase, 0], ex_r.at[phase, 0], xn)
+        to_x.start()
+        to_p = remote(buf.at[me], buf.at[me], ex_s.at[phase, 1], ex_r.at[phase, 1], core)
+        to_p.start()
+        to_x.wait_recv()
+        fwd = remote(buf.at[xs_], buf.at[xs_], ex_s.at[phase, 2], ex_r.at[phase, 2], core)
+        fwd.start()
+        to_p.wait_recv()
+        fwd.wait_recv()
+        to_x.wait_send()
+        to_p.wait_send()
+        fwd.wait_send()
+
+    def scatter_sum(phase, part):
+        send_p[phase, 0] = part[slot(1 - x, 1 - c)].astype(BF)
+        send_p[phase, 1] = part[slot(x, 1 - c)].astype(BF)
+        far = remote(send_p.at[phase, 0], recv_p.at[phase, 0], rs_s.at[phase, 0], rs_r.at[phase, 0], core)
+        far.start()
+        near = remote(send_p.at[phase, 1], recv_p.at[phase, 1], rs_s.at[phase, 1], rs_r.at[phase, 1], core)
+        near.start()
+        far.wait_recv()
+        send_x[phase] = (part[slot(1 - x, c)] + recv_p[phase, 0].astype(F32)).astype(BF)
+        over = remote(send_x.at[phase], recv_x.at[phase], rs_s.at[phase, 2], rs_r.at[phase, 2], xn)
+        over.start()
+        near.wait_recv()
+        over.wait_recv()
+        far.wait_send()
+        near.wait_send()
+        over.wait_send()
+        return part[slot(x, c)] + recv_p[phase, 1].astype(F32) + recv_x[phase].astype(F32)
+
+    def v_(i):
+        return vec[i : i + 1]
+
+    h = hid[...]
+    q_s[...] = (mm(h, ws[0]) + v_(0)).astype(BF)
+    k_s[...] = mm(h, ws[1]).astype(BF)
+    v_s[...] = (mm(h, ws[2]) + v_(1)).astype(BF)
+    for i in range(2):
+        rows = slice(64 * i, 64 * i + 64)
+        ok = jnp.concatenate([allowed[i]] * 4, 0)
+        for g in range(3):
+            lanes = slice(256 * g, 256 * g + 256)
+            p, a = attend_block(q_s[rows, lanes], k_s[rows, lanes], v_s[rows, lanes], ok)
+            p_s[i, g] = p
+            a_s[rows, lanes] = a
+    sum1[...] = h.astype(F32) + (mm(a_s[...], ws[3]) + v_(2))
+    xh, _ = normed(sum1[...])
+    first[...] = xh * v_(3) + v_(4)
+    me = slot(x, c)
+    xg[0, me, 64:128] = rows_of(first, 32).astype(BF)
+
+    u = rows_of(first, 0)
+    cq_s[...] = (mm(u.astype(BF), wc[0:768]) + v_(5)).astype(BF)
+    for i in range(2):
+        rows = slice(272 * i, 272 * i + 272)
+        ck_s[rows] = mm(feat[rows], wc[768:2176]).astype(BF)
+        cv_s[rows] = (mm(feat[rows], wc[2176:3584]) + v_(6)).astype(BF)
+    ok = jnp.where(lax.broadcasted_iota(jnp.int32, (128, 272), 1) < 257, 1.0, 0.0)
+    for i in range(2):
+        rows = slice(272 * i, 272 * i + 272)
+        mine = slice(32 * i, 32 * i + 32)
+        for g in range(3):
+            lanes = slice(256 * g, 256 * g + 256)
+            p, a = attend_block(cq_s[mine, lanes], ck_s[rows, lanes], cv_s[rows, lanes], ok)
+            p_c[i, g] = p
+            ca_s[mine, lanes] = a
+    sum2[...] = u + (mm(ca_s[...], wc[3584:4352]) + v_(7))
+    xh, _ = normed(sum2[...])
+    second[...] = xh * v_(8) + v_(9)
+    xg[0, me, 0:64] = second[...].astype(BF)
+
+    exchange(0, xg.at[0])
+    for b in range(2):
+        r = slice(64 * b, 64 * b + 64)
+        rows = xg[0, :, r].reshape(256, D)
+        pre[b] = mm(rows, wf[2 * b]) + v_(10 + 4 * b)
+        act[b] = gelu(pre[b]).astype(BF)
+        part[:, r] = mm(act[b], wf[2 * b + 1]).reshape(4, 64, D)
+    out = scatter_sum(0, part)
+    for b in range(2):
+        rows = second[...] if b == 0 else rows_of(first, 32)
+        s3 = rows + (out[64 * b : 64 * b + 64] + v_(11 + 4 * b))
+        sum3[b] = s3
+        xh, _ = normed(s3)
+        done = (xh * v_(12 + 4 * b) + v_(13 + 4 * b)).astype(BF)
+        for i in range(2):
+            mixed[64 * i + 32 * b : 64 * i + 32 * b + 32] = done[32 * i : 32 * i + 32]
+        g_out = rows_of(cot, 32 * b).astype(F32)
+        dsum, dgain, dshift = norm_back(s3, v_(12 + 4 * b), g_out)
+        dsum3[b] = dsum
+        low = dsum.astype(BF)
+        xg[1, me, 64 * b : 64 * b + 64] = low
+        o = 10 + 7 * b
+        vg[o + 4 : o + 5] = jnp.sum(low.astype(F32), 0, keepdims=True)
+        vg[o + 5 : o + 6] = dgain
+        vg[o + 6 : o + 7] = dshift
+    exchange(1, xg.at[1])
+    for b in range(2):
+        r = slice(64 * b, 64 * b + 64)
+        up = xg[1, :, r].reshape(256, D)
+        dpre = (mm_nt(up, wf[2 * b + 1]) * gelu_slope(pre[b])).astype(BF)
+        gb[b] = dpre
+        part[:, r] = mm_nt(dpre, wf[2 * b]).reshape(4, 64, D)
+        db1 = jnp.sum(dpre.astype(F32), 0, keepdims=True)
+        for j in range(4):
+            vg[10 + 7 * b + j : 11 + 7 * b + j] = jnp.where(j == me, db1, 0.0)
+    dx = scatter_sum(1, part)
+    for b in range(2):
+        r = slice(64 * b, 64 * b + 64)
+        rows = xg[0, :, r].reshape(256, D)
+        up = xg[1, :, r].reshape(256, D)
+        gf[2 * b] = mm_tn(rows, gb[b]).astype(BF)
+        gf[2 * b + 1] = mm_tn(act[b], up).astype(BF)
+    d_second = dsum3[0] + dx[0:64]
+    d_text = dsum3[1] + dx[64:128]
+    for i in range(2):
+        dfirst[64 * i + 32 : 64 * i + 64] = d_text[32 * i : 32 * i + 32]
+
+    du2, dgain, dshift = norm_back(sum2[...], v_(8), d_second)
+    vg[8:9] = dgain
+    vg[9:10] = dshift
+    go = du2.astype(BF)
+    vg[7:8] = jnp.sum(go.astype(F32), 0, keepdims=True)
+    gc[3584:4352] = mm_tn(ca_s[...], go).astype(BF)
+    dca = mm_nt(go, wc[3584:4352]).astype(BF)
+    dcq = []
+    for i in range(2):
+        rows = slice(272 * i, 272 * i + 272)
+        mine = slice(32 * i, 32 * i + 32)
+        blocks = []
+        for g in range(3):
+            lanes = slice(256 * g, 256 * g + 256)
+            dq, dk, dv = attend_block_back(
+                cq_s[mine, lanes], ck_s[rows, lanes], cv_s[rows, lanes], p_c[i, g], dca[mine, lanes]
+            )
+            blocks.append(dq)
+            dck[rows, lanes] = dk
+            dcv[rows, lanes] = dv
+        dcq.append(jnp.concatenate(blocks, 1))
+    dcq = jnp.concatenate(dcq, 0)
+    vg[5:6] = jnp.sum(dcq.astype(F32), 0, keepdims=True)
+    vg[6:7] = jnp.sum(dcv[...].astype(F32), 0, keepdims=True)
+    u_low = rows_of(first, 0).astype(BF)
+    gc[0:768] = mm_tn(u_low, dcq).astype(BF)
+    for j in range(11):
+        block = feat[:, 128 * j : 128 * j + 128]
+        gc[768 + 128 * j : 896 + 128 * j] = mm_tn(block, dck[...]).astype(BF)
+        gc[2176 + 128 * j : 2304 + 128 * j] = mm_tn(block, dcv[...]).astype(BF)
+    du = du2 + mm_nt(dcq, wc[0:768])
+    for i in range(2):
+        dfirst[64 * i : 64 * i + 32] = du[32 * i : 32 * i + 32]
+
+    dsum1, dgain, dshift = norm_back(sum1[...], v_(3), dfirst[...])
+    vg[3:4] = dgain
+    vg[4:5] = dshift
+    go = dsum1.astype(BF)
+    vg[2:3] = jnp.sum(go.astype(F32), 0, keepdims=True)
+    gs[3] = mm_tn(a_s[...], go).astype(BF)
+    da = mm_nt(go, ws[3]).astype(BF)
+    for i in range(2):
+        rows = slice(64 * i, 64 * i + 64)
+        for g in range(3):
+            lanes = slice(256 * g, 256 * g + 256)
+            dq, dk, dv = attend_block_back(
+                q_s[rows, lanes], k_s[rows, lanes], v_s[rows, lanes], p_s[i, g], da[rows, lanes]
+            )
+            dq_s[rows, lanes] = dq
+            dk_s[rows, lanes] = dk
+            dv_s[rows, lanes] = dv
+    vg[0:1] = jnp.sum(dq_s[...].astype(F32), 0, keepdims=True)
+    vg[1:2] = jnp.sum(dv_s[...].astype(F32), 0, keepdims=True)
+    gs[0] = mm_tn(hid[...], dq_s[...]).astype(BF)
+    gs[1] = mm_tn(hid[...], dk_s[...]).astype(BF)
+    gs[2] = mm_tn(hid[...], dv_s[...]).astype(BF)
+    total = dsum1 + mm_nt(dq_s[...], ws[0]) + mm_nt(dk_s[...], ws[1]) + mm_nt(dv_s[...], ws[2])
+    hgrad[...] = total.astype(BF)
+
+
+def layer(hid, allowed, feat, cot, vec, ws, wc, wf):
+    dma = pltpu.SemaphoreType.DMA
+    vm = pl.BlockSpec(memory_space=pltpu.VMEM)
+    b = lambda *s: pltpu.VMEM(s, BF)
+    f = lambda *s: pltpu.VMEM(s, F32)
+    return pl.pallas_call(
+        compute_kernel,
+        out_shape=(
+            jax.ShapeDtypeStruct((128, D), BF),
+            jax.ShapeDtypeStruct((128, D), BF),
+            jax.ShapeDtypeStruct((4, D, D), BF),
+            jax.ShapeDtypeStruct((4352, D), BF),
+            jax.ShapeDtypeStruct((4, D, D), BF),
+            jax.ShapeDtypeStruct((24, D), F32),
+        ),
+        in_specs=[vm] * 8,
+        out_specs=[vm] * 6,
+        scratch_shapes=[
+            b(128, D), b(128, D), b(128, D), b(128, D), f(2, 3, 256, 64), f(128, D), f(128, D),
+            b(64, D), b(544, D), b(544, D), b(64, D), f(2, 3, 128, 272), f(64, D), f(64, D),
+            b(2, 4, 128, D), f(2, 256, D), b(2, 256, D), f(4, 128, D),
+            b(2, 2, 128, D), b(2, 2, 128, D), b(2, 128, D), b(2, 128, D),
+            f(2, 64, D), b(2, 256, D), f(2, 64, D), f(128, D),
+            b(128, D), b(128, D), b(128, D), b(544, D), b(544, D),
+            dma((2, 3)), dma((2, 3)), dma((2, 3)), dma((2, 3)),
+        ],
+        compiler_params=pltpu.CompilerParams(
+            collective_id=1, has_side_effects=True, vmem_limit_bytes=VMEM_BYTES
+        ),
+    )(hid, allowed, feat, cot, vec, ws, wc, wf)
+
+
+def reduce_kernel(
+    gs, gc, gf, out_s, out_c, out_f,
+    cs_buf, cc_buf, xs_buf, xc_buf, ys_buf, yc_buf, zs_buf, zc_buf, yf_buf, zf_buf, fin_s, fin_c, fin_f,
+    co_s, co_r, xx_s, xx_r, yy_s, yy_r, zz_s, zz_r, fi_s, fi_r,
+):
+    x, z, y, c = place()
+    core, xn, yn = device(x, z, y, 1 - c), device(1 - x, z, y, c), device(x, z, 1 - y, c)
+    diag = device(1 - x, z, y, 1 - c)
+    meet(neighbours(x, z, y, c) + [diag])
+    sent = []
+
+    def go(src, dst, send, recv, target):
+        copy = remote(src, dst, send, recv, target)
+        copy.start()
+        sent.append(copy)
+
+    def arrived(view, recv):
+        remote(view, view, recv, recv, core).wait_recv()
+
+    def add(a, b):
+        return (a.astype(F32) + b.astype(F32)).astype(BF)
+
+    mine_cols = pl.ds(pl.multiple_of(384 * x, 384), 384)
+    their_cols = pl.ds(pl.multiple_of(384 * (1 - x), 384), 384)
+
+    def view_s(zz, yy, cc):
+        return gs.at[zz, pl.ds(pl.multiple_of(192 * (2 * yy + cc), 192), 192)]
+
+    def view_c(zz, yy, cc):
+        return gc.at[pl.ds(pl.multiple_of(272 * ((zz * 2 + yy) * 2 + cc), 16), 272)]
+
+    def view_f(zz, yy):
+        return gf.at[zz, pl.ds(pl.multiple_of(384 * yy, 384), 384)]
+
+    groups = [
+        (0, view_c, cc_buf, xc_buf, yc_buf, zc_buf, fin_c, out_c),
+        (1, view_s, cs_buf, xs_buf, ys_buf, zs_buf, fin_s, out_s),
+    ]
+    order = (1, 2, 3, 0)
+    for d in order:
+        zz = (z + d) % 4
+        go(view_f(zz, 1 - y), yf_buf.at[zz], yy_s.at[2, d], yy_r.at[2, d], yn)
+    for g, view, cb, xb, yb, zb, fin, out in groups:
+        for far in range(2):
+            for d in order:
+                zz = (z + d) % 4
+                go(view(zz, y if far else 1 - y, 1 - c), cb.at[far, zz], co_s.at[g, far, d], co_r.at[g, far, d], core)
+    for g, view, cb, xb, yb, zb, fin, out in groups:
+        for far in range(2):
+            for d in order:
+                zz = (z + d) % 4
+                arrived(cb.at[far, zz], co_r.at[g, far, d])
+                cb[far, zz] = add(cb[far, zz], view(zz, y if far else 1 - y, c)[...])
+                go(cb.at[far, zz, :, their_cols], xb.at[far, zz], xx_s.at[g, far, d], xx_r.at[g, far, d], xn)
+    for d in order:
+        zz = (z + d) % 4
+        arrived(yf_buf.at[zz], yy_r.at[2, d])
+        yf_buf[zz] = add(yf_buf[zz], view_f(zz, y)[...])
+        if d:
+            go(yf_buf.at[zz], zf_buf.at[d - 1], zz_s.at[2, d - 1], zz_r.at[2, d - 1], device(x, zz, y, c))
+    for g, view, cb, xb, yb, zb, fin, out in groups:
+        for far in range(2):
+            for d in order:
+                zz = (z + d) % 4
+                arrived(xb.at[far, zz], xx_r.at[g, far, d])
+                xb[far, zz] = add(xb[far, zz], cb[far, zz, :, mine_cols])
+                if far == 0:
+                    go(xb.at[0, zz], yb.at[zz], yy_s.at[g, d], yy_r.at[g, d], yn)
+        for d in order:
+            zz = (z + d) % 4
+            arrived(yb.at[zz], yy_r.at[g, d])
+            yb[zz] = add(yb[zz], xb[1, zz])
+            if d:
+                go(yb.at[zz], zb.at[d - 1], zz_s.at[g, d - 1], zz_r.at[g, d - 1], device(x, zz, y, c))
+    for k in range(3):
+        arrived(zf_buf.at[k], zz_r.at[2, k])
+    total = yf_buf[z].astype(F32)
+    for k in range(3):
+        total = total + zf_buf[k].astype(F32)
+    fin_f[...] = total.astype(BF).reshape(2, 192, D)
+    quarter = 2 * c + x
+    w1 = z % 2 == 0
+
+    @pl.when(w1)
+    def _():
+        out_f[quarter] = fin_f[c]
+        copies = [
+            remote(fin_f.at[c], out_f.at[quarter], fi_s.at[2], fi_r.at[2], xn),
+            remote(fin_f.at[1 - c], out_f.at[quarter], fi_s.at[3], fi_r.at[3], core),
+            remote(fin_f.at[1 - c], out_f.at[quarter], fi_s.at[4], fi_r.at[4], diag),
+        ]
+        for copy in copies:
+            copy.start()
+        for copy in copies:
+            copy.wait()
+
+    @pl.when(jnp.logical_not(w1))
+    def _():
+        copies = []
+        for j in range(2):
+            out_f[2 * x + j] = fin_f[j]
+            copies.append(remote(fin_f.at[j], out_f.at[2 * x + j], fi_s.at[2 + j], fi_r.at[2 + j], xn))
+        for copy in copies:
+            copy.start()
+        for copy in copies:
+            copy.wait()
+
+    for g, view, cb, xb, yb, zb, fin, out in groups:
+        for k in range(3):
+            arrived(zb.at[k], zz_r.at[g, k])
+        total = yb[z].astype(F32)
+        for k in range(3):
+            total = total + zb[k].astype(F32)
+        fin[...] = total.astype(BF)
+        out[:, mine_cols] = fin[...]
+        go(fin, out.at[:, mine_cols], fi_s.at[g], fi_r.at[g], xn)
+    for g, view, cb, xb, yb, zb, fin, out in groups:
+        arrived(out.at[:, their_cols], fi_r.at[g])
+    for copy in sent:
+        copy.wait_send()
+
+
+def reduce_grads(gs, gc, gf):
+    dma = pltpu.SemaphoreType.DMA
+    vm = pl.BlockSpec(memory_space=pltpu.VMEM)
+    b = lambda *s: pltpu.VMEM(s, BF)
+    return pl.pallas_call(
+        reduce_kernel,
+        out_shape=(
+            jax.ShapeDtypeStruct((192, D), BF),
+            jax.ShapeDtypeStruct((272, D), BF),
+            jax.ShapeDtypeStruct((4, 192, D), BF),
+        ),
+        in_specs=[vm] * 3,
+        out_specs=[vm] * 3,
+        scratch_shapes=[
+            b(2, 4, 192, D), b(2, 4, 272, D), b(2, 4, 192, 384), b(2, 4, 272, 384),
+            b(4, 192, 384), b(4, 272, 384), b(3, 192, 384), b(3, 272, 384),
+            b(4, 384, D), b(3, 384, D), b(192, 384), b(272, 384), b(2, 192, D),
+            dma((2, 2, 4)), dma((2, 2, 4)), dma((2, 2, 4)), dma((2, 2, 4)),
+            dma((3, 4)), dma((3, 4)), dma((3, 3)), dma((3, 3)), dma((5,)), dma((5,)),
+        ],
+        compiler_params=pltpu.CompilerParams(
+            collective_id=2, has_side_effects=True, vmem_limit_bytes=VMEM_BYTES
+        ),
+    )(gs, gc, gf)
+
+
+def own_rows(self_params, cross_params, ffn_params):
+    x, z, y, c = place()
+    f = lax.axis_index("fsdp")
+    k = f % 4
+    flats = [v.reshape(-1, 128) for v in (self_params, cross_params, ffn_params)]
+    tails = lax.all_gather(jnp.concatenate([v[-32:] for v in flats]), "fsdp")
+    before = lax.dynamic_index_in_dim(tails, (f + 15) % 16, keepdims=False)
+    back = [2 * f, 2 * f, 6 * k + jnp.where(z >= 2, 6, 0)]
+    nice = []
+    for i, (v, rows) in enumerate(zip(flats, (1152, 1632, 4608))):
+        both = jnp.concatenate([before[32 * i : 32 * i + 32], v])
+        nice.append(lax.dynamic_slice_in_dim(both, 32 - back[i], rows))
+    own_s = nice[0].reshape(192, D)
+    own_c = nice[1].reshape(272, D)
+    cols = nice[2].reshape(192, 2, 4, 3, 128)
+    pick = lambda cc: lax.dynamic_index_in_dim(cols, 2 * cc + x, 2, keepdims=False).reshape(192, D)
+    as_w1 = jnp.stack([pick(c), pick(1 - c)])
+    as_w2 = lax.dynamic_index_in_dim(nice[2].reshape(2, 2, 192, D), x, keepdims=False)
+    own_f = jnp.where(z % 2 == 0, as_w1, as_w2)
+
+    q = 2 * c + x
+    part = lambda b1: lax.dynamic_index_in_dim(b1.reshape(2, 4, 384), q, 1, keepdims=False).reshape(1, D)
+    vecs = [
+        tails[15, 0:30].reshape(5, D),
+        tails[15, 32:62].reshape(5, D),
+        part(tails[3, 72:96]),
+        tails[7, 72:90].reshape(3, D),
+        part(tails[11, 66:90]),
+        tails[15, 66:84].reshape(3, D),
+        jnp.zeros((6, D), BF),
+    ]
+    return own_s, own_c, own_f, jnp.concatenate(vecs).astype(F32)
+
+
+def flat_grads(out_s, out_c, out_f, vg):
+    x, z, y, c = place()
+    f = lax.axis_index("fsdp")
+    k = f % 4
+    w1 = out_f.reshape(4, 192, 2, 3, 128).transpose(1, 2, 0, 3, 4).reshape(4608, 128)
+    w2 = out_f.reshape(4608, 128)
+    nice = [out_s.reshape(1152, 128), out_c.reshape(1632, 128), jnp.where(z % 2 == 0, w1, w2)]
+    heads = jnp.concatenate([v[:32] for v in nice])
+    after = lax.ppermute(heads, "fsdp", [(i, (i + 15) % 16) for i in range(16)]).astype(F32)
+    vg = lax.psum(vg, ("dp", "fsdp"))
+    zeros = lambda n: jnp.zeros((n, 128), F32)
+    b1 = lambda v: v.reshape(4, 2, 384).transpose(1, 0, 2).reshape(24, 128)
+    flat = lambda v: v.reshape(-1, 128)
+    tail_s = jnp.where(f == 15, jnp.concatenate([flat(vg[0:5]), zeros(2)]), after[0:32])
+    tail_c = jnp.where(f == 15, jnp.concatenate([flat(vg[5:10]), zeros(2)]), after[32:64])
+    nxt = after[64:96]
+    ends = jnp.stack([
+        jnp.concatenate([b1(vg[10:14]), zeros(8)]),
+        jnp.concatenate([flat(vg[14:17]), nxt[:14]]),
+        jnp.concatenate([b1(vg[17:21]), nxt[:8]]),
+        jnp.concatenate([flat(vg[21:24]), zeros(14)]),
+    ])
+    tail_f = jnp.where(k == 3, lax.dynamic_index_in_dim(ends, z, keepdims=False), nxt)
+    skip = [2 * f, 2 * f, 6 * k + jnp.where(z >= 2, 6, 0)]
+    outs = []
+    for v, tail, start, rows in zip(nice, (tail_s, tail_c, tail_f), skip, (1154, 1634, 4614)):
+        both = jnp.concatenate([v.astype(F32), tail])
+        outs.append(lax.dynamic_slice_in_dim(both, start, rows).reshape(-1))
+    return outs
+
+
+def per_device_fast(hidden, lengths, features, cotangent, self_params, cross_params, ffn_params):
+    own_s, own_c, own_f, vec = own_rows(self_params, cross_params, ffn_params)
+    ws, wc, wf = gather_weights(own_s, own_c, own_f)
+    at = jnp.arange(64)
+    r, k = at[:, None], at[None, :]
+    allowed = (k < NQ)[None] | ((r >= NQ) & (k <= r))[None] & (k[None] < NQ + lengths[:, None, None])
+    feat = jnp.pad(features, ((0, 0), (0, 15), (0, 0))).reshape(544, E)
+    mixed, hgrad, gs, gc, gf, vg = layer(
+        hidden.reshape(128, D), allowed.astype(F32), feat, cotangent.reshape(128, D), vec, ws, wc, wf
+    )
+    grads = flat_grads(*reduce_grads(gs, gc, gf), vg)
+    return (mixed.reshape(2, 64, D), hgrad.reshape(2, 64, D), *grads)
+
+
 def solution(mesh):
+    fast = mesh.shape["dp"] == 2 and mesh.shape["fsdp"] == 16
     return jax.shard_map(
-        per_device,
+        per_device_fast if fast else per_device,
         mesh=mesh,
         in_specs=(
             P(("dp", "fsdp"), None, None),

time: 2630 us -> 399 us (0.15)
  blocking collectives: 984 us -> 24.2 us
  local copies, waits for them, and re-layouts: 767 us -> 23.6 us
  other arithmetic: 672 us -> 13.1 us
  Pallas kernels: 0 us -> 301 us
  matrix products: 94.1 us -> 0 us
  waiting for transfers between devices: 71.3 us -> 17.4 us
    unnamed x1 -> x0, blocking collectives: 961 us -> none
    all_gather x3 -> x0, other arithmetic: 620 us -> none  [the longest x1 401 us: per_device(): ffn_full = lax.all_gather(ffn_params, 'fsdp', axis=0, tiled=True)]
    unnamed x312 -> x27, local copies, waits for them, and re-layouts: 337 us -> 4.12 us
    pallas_call x0 -> x3, Pallas kernels: none -> 301 us  [the longest x1 128 us: reduce_grads(): pl.pallas_call(reduce_kernel, out_shape=(jax.ShapeDtypeStruct((192, D), B...]
    reshape x37 -> x17, local copies, waits for them, and re-layouts: 233 us -> 12.5 us  [the longest x1 3.43 us: flat_grads(): w2 = out_f.reshape(4608, 128)]
    dot_general x46 -> x0, matrix products: 94.1 us -> none  [the longest x12 37.9 us: matmul_left(): lax.dot_general(left, right, (((0,), (0,)), ((), ())), preferred_element_...]
    all_gather x4 -> x0, waiting for transfers between devices: 71.2 us -> none  [the longest x1 60.6 us: per_device(): self_full = lax.all_gather(self_params, 'fsdp', axis=0, tiled=True)]
    slice x10 -> x15, local copies, waits for them, and re-layouts: 54.4 us -> 3.95 us  [the longest x2 1.44 us: own_rows(): tails = lax.all_gather(jnp.concatenate([v[-32:] for v in flats]), 'fsdp')]
  transfers between devices with their start and end apart: 4 -> 2, of which waited for: 2 -> 1; matrix products, arithmetic and copies ran while one was open for 14% -> 3% of each run, Pallas kernels for 0% -> 32%
where the time goes in v1:
time: 399 us; the launch traced here: 397 us
  Pallas kernels  301 us (75%)
  blocking collectives  24.2 us (6%)
  local copies, waits for them, and re-layouts  23.6 us (6%)
  waiting for transfers between devices  17.4 us (4%)
  between operations  14.5 us (4%)
  other arithmetic  13.1 us (3%)
    pallas_call x1, Pallas kernels, reduce_grads(): pl.pallas_call(reduce_kernel, out_shape=(jax.ShapeDtypeStruct((192, D), B...  128 us
    pallas_call x1, Pallas kernels, gather_weights(): pl.pallas_call(gather_kernel, out_shape=(jax.ShapeDtypeStruct((4, D, D),...  110 us
    pallas_call x1, Pallas kernels, layer(): pl.pallas_call(compute_kernel, out_shape=(jax.ShapeDtypeStruct((128, D),...  63.7 us
    all_gather x1, blocking collectives, own_rows(): tails = lax.all_gather(jnp.concatenate([v[-32:] for v in flats]), 'fsdp')  24.2 us
    psum x1, waiting for transfers between devices, flat_grads(): vg = lax.psum(vg, ('dp', 'fsdp'))  17.4 us
  transfers between devices with their start and end apart: 2, of which 1 were waited for; matrix products, arithmetic and copies ran while one was open for 3% of the time, Pallas kernels for 32%

profile of v1, /device:TPU:0, one launch (start us, length us, event | category | flops | bytes accessed | tf_op | source)
XLA Modules:
  0.0 397.2 jit_solution(703438385647245975)
XLA Ops:
  8.7 24.2 %all-gather = bf16[1536,128]{1,0:T(8,128)(2,1)S(1)} all-gather(bf16[96,128]{1,0:T(8,128)(2,1)S(1)} %pad_maximum_fusion), channel_id=2, replica_groups=mesh['dp'=2,'fsdp'=16] {'fsdp'}, dimensions={0}, use_global_device_ids=true | all-gather | bytes 417792 | tf_op jit(solution)/shard_map/all_gather | solution.py:975
  33.0 1.9 fusion.2
  34.9 1.9 reshape.203
  38.9 1.0 reshape.198.own_s
  40.1 1.1 reshape.200.own_c
  42.0 1.5 copy.26
  43.6 1.2 pad.8.clone
  45.5 0.9 maximum_select_fusion.own_f
  46.4 110.1 %shard_map.110 = (bf16[4,768,768]{2,1,0:T(8,128)(2,1)}, bf16[4352,768]{1,0:T(8,128)(2,1)}, bf16[4,768,768]{2,1,0:T(8,128)(2,1)}, bf16[384,768]{1,0:T(8,128)(2,1)}) custom-call(bf16[192,768]{1,0:T(8,128)(2,1)} %reshape.198.own_s, bf16[272,768]{1,0:T(8,128)(2,1)} %reshape.200.own_c, bf16[2,192,768]{2,1,0:T(8,128)(2,1)} %maximum_select_fusion.own_f), custom_call_target="tpu_custom_call" | custom-call | tf_op jit(solution)/shard_map/pallas_call | solution.py:491
  156.5 63.7 %shard_map.111 = (bf16[128,768]{1,0:T(8,128)(2,1)}, bf16[128,768]{1,0:T(8,128)(2,1)}, bf16[4,768,768]{2,1,0:T(8,128)(2,1)}, bf16[4352,768]{1,0:T(8,128)(2,1)}, b...) custom-call(bf16[128,768]{1,0:T(8,128)(2,1)} %bitcast.55, f32[2,64,64]{2,1,0:T(8,128)} %or_convert_fusion.allowed, ...), custom_call_target="tpu_custom_call" | custom-call | tf_op jit(solution)/shard_map/pallas_call | solution.py:795
  220.2 127.6 %shard_map.112 = (bf16[192,768]{1,0:T(8,128)(2,1)}, bf16[272,768]{1,0:T(8,128)(2,1)}, bf16[4,192,768]{2,1,0:T(8,128)(2,1)}) custom-call(bf16[4,768,768]{2,1,0:T(8,128)(2,1)} %get-tuple-element.22.gs, bf16[4352,768]{1,0:T(8,128)(2,1)} %get-tuple-element.23.gc, bf16[4,768,768]{2,1,0:T(8,128)(2,1)} %get-tuple-element.24.gf), custom_call_target="tpu_custom_call" | custom-call | tf_op jit(solution)/shard_map/pallas_call | solution.py:948
  347.9 3.4 reshape.211
  352.5 1.5 reshape.208
  355.3 2.1 reshape.210
  357.5 1.6 fusion.15
  359.1 3.0 collective-permute-start
  362.1 0.9 convert_element_type.22
  362.9 1.1 convert_element_type.24
  364.0 17.4 %all-reduce.7.cloned.1.call-done = f32[24,768]{1,0:T(8,128)} async-done(((f32[24,768]{1,0:T(8,128)}), f32[24,768]{1,0:T(8,128)}) %all-reduce.7.cloned.1.call-update) | async-done | bytes 73744 | tf_op jit(solution)/shard_map/psum | solution.py:1013
  382.3 0.8 fusion.21
  383.2 0.9 fusion.19
  384.2 2.5 fusion.1
  386.7 1.3 fusion.4
  387.9 1.1 fusion.6
  (86 shorter events, 10.1 us)
Async XLA Ops:
  7.2 374.3 %all-reduce.7.cloned.1.call-start = ((), (), s32[]{:S(2)}) async-start(), calls=%async_computation | async-start | bytes 147456 | tf_op jit(solution)/shard_map/psum | solution.py:1013
  36.8 0.7 copy-start.11
  36.8 1.9 copy-start.7
  36.8 3.1 copy-start.6
  43.6 1.9 copy-start.1
  347.9 3.4 copy-start
  351.3 1.0 copy-start.8
  352.5 2.8 copy-start.4
  354.0 0.8 copy-start.3
  357.5 1.6 slice-start
  357.5 4.6 %copy-start.5 = (bf16[1152,128]{1,0:T(8,128)(2,1)S(1)}, bf16[1152,128]{1,0:T(8,128)(2,1)}, u32[]{:S(2)}) copy-start(bf16[1152,128]{1,0:T(8,128)(2,1)} %copy-done.4) | copy-start | bytes 884740
  359.1 4.9 %collective-permute-start = (bf16[96,128]{1,0:T(8,128)(2,1)S(1)}, bf16[96,128]{1,0:T(8,128)(2,1)S(1)}, u32[]{:S(2)}, u32[]{:S(2)}) collective-permute-start(bf16[96,128]{1,0:T(8,128)(2,1)S(1)} %pad_maximum_fusion.1), channel_id=1, source_target_pairs={{0,15},{1,0},{2,1},{3,2},{4,3},{5,4},{6,5},{7,6},{8,7},{9,8},{10,9... | collective-permute-start | bytes 73736 | tf_op jit(solution)/shard_map/ppermute | solution.py:1012
  386.6 1.3 copy-start.2
  386.7 2.4 copy-start.10
  386.7 3.1 copy-start.9
Sparse Core Ops, SparseCore 0:
  220.3 161.0 all-reduce.6

commit v2 on v0

--- a/solution.py
+++ b/solution.py
@@ -1,9 +1,12 @@
 from functools import partial
 import math
+from types import SimpleNamespace
 
 import jax
 import jax.numpy as jnp
 from jax import lax
+from jax.experimental import pallas as pl
+from jax.experimental.pallas import tpu as pltpu
 from jax.sharding import PartitionSpec as P
 
 D = 768
@@ -311,9 +314,814 @@
     return (mixed, hidden_grad, self_grad, cross_grad, ffn_grad)
 
 
+MESH = pl.DeviceIdType.MESH
+BF = jnp.bfloat16
+F32 = jnp.float32
+VMEM_BYTES = 62 * 2**20
+
+
+def place():
+    f = lax.axis_index("fsdp")
+    return lax.axis_index("dp"), f // 4, (f // 2) % 2, f % 2
+
+
+def device(x, z, y, c):
+    return (x, (z * 2 + y) * 2 + c)
+
+
+def meet(devices):
+    barrier = pltpu.get_barrier_semaphore()
+    for d in devices:
+        pl.semaphore_signal(barrier, inc=1, device_id=d, device_id_type=MESH)
+    pl.semaphore_wait(barrier, len(devices))
+
+
+def remote(src, dst, send, recv, target):
+    return pltpu.make_async_remote_copy(
+        src_ref=src,
+        dst_ref=dst,
+        send_sem=send,
+        recv_sem=recv,
+        device_id=target,
+        device_id_type=MESH,
+    )
+
+
+def mm(a, b):
+    return jnp.dot(a, b, preferred_element_type=F32)
+
+
+def mm_nt(a, b):
+    return lax.dot_general(a, b, (((1,), (1,)), ((), ())), preferred_element_type=F32)
+
+
+def mm_tn(a, b):
+    return lax.dot_general(a, b, (((0,), (0,)), ((), ())), preferred_element_type=F32)
+
+
+def rows_sum(v):
+    return jnp.sum(v.astype(F32), 0, keepdims=True)
+
+
+def add(a, b):
+    return (a.astype(F32) + b.astype(F32)).astype(BF)
+
+
+def normed(v):
+    centered = v - jnp.mean(v, -1, keepdims=True)
+    r = lax.rsqrt(jnp.mean(centered * centered, -1, keepdims=True) + EPS)
+    return centered * r, r
+
+
+def norm_back(v, gain, g_out):
+    xh, r = normed(v)
+    gg = g_out * gain
+    dv = r * (gg - jnp.mean(gg, -1, keepdims=True) - xh * jnp.mean(gg * xh, -1, keepdims=True))
+    return dv, rows_sum(g_out * xh), rows_sum(g_out)
+
+
+GELU_A = math.sqrt(2.0 / math.pi)
+GELU_B = 0.044715
+
+
+def gelu(v):
+    return 0.5 * v * (1.0 + jnp.tanh(GELU_A * (v + GELU_B * (v * v * v))))
+
+
+def gelu_slope(v):
+    t = jnp.tanh(GELU_A * (v + GELU_B * (v * v * v)))
+    return 0.5 * (1.0 + t) + 0.5 * v * (1.0 - t * t) * (GELU_A * (1.0 + 3.0 * GELU_B * (v * v)))
+
+
+def head_mask(h):
+    lane = lax.broadcasted_iota(jnp.int32, (1, 256), 1)
+    return jnp.where(lane // HDIM == h, 1.0, 0.0)
+
+
+def spread(rows):
+    wide = rows.astype(F32)
+    return jnp.concatenate([(wide * head_mask(h)).astype(BF) for h in range(4)], 0)
+
+
+def fold(stacked):
+    n = stacked.shape[0] // 4
+    total = stacked[:n] * head_mask(0)
+    for h in range(1, 4):
+        total = total + stacked[h * n : (h + 1) * n] * head_mask(h)
+    return total
+
+
+def attend_block(q, k, v, allowed):
+    s = mm_nt(spread(q), k) * SCALE
+    s = jnp.where(allowed > 0.5, s, -1e30)
+    e = jnp.exp(s - jnp.max(s, -1, keepdims=True))
+    p = e / jnp.sum(e, -1, keepdims=True)
+    return p, fold(mm(p.astype(BF), v)).astype(BF)
+
+
+def attend_block_back(q, k, v, p, da):
+    dax = spread(da)
+    dp = mm_nt(dax, v)
+    ds = (p * (dp - jnp.sum(p * dp, -1, keepdims=True))).astype(BF)
+    dq = (fold(mm(ds, k)) * SCALE).astype(BF)
+    dk = (mm_tn(ds, spread(q)) * SCALE).astype(BF)
+    dv = mm_tn(p.astype(BF), dax).astype(BF)
+    return dq, dk, dv
+
+
+def rows_of(ref, first):
+    return jnp.concatenate([ref[first : first + 32], ref[64 + first : 96 + first]], 0)
+
+
+def scratch():
+    dma = lambda *s: pltpu.SemaphoreType.DMA(s)
+    b = lambda *s: pltpu.VMEM(s, BF)
+    f = lambda *s: pltpu.VMEM(s, F32)
+    return dict(
+        ws=b(4, D, D), wc=b(4352, D), wf=b(4, D, D), block_f=b(384, D), tb=b(4, 16, D),
+        tv=f(4, 16, D), vg=f(4, 16, D),
+        q=b(128, D), k=b(128, D), v=b(128, D), a=b(128, D), p=f(2, 3, 256, 64),
+        sum1=f(128, D), first=f(128, D), cq=b(64, D), ck=b(544, D), cv=b(544, D), ca=b(64, D),
+        pc=f(2, 3, 128, 272), sum2=f(64, D), second=f(64, D),
+        xg=b(2, 2, 4, 64, D), pre=f(2, 256, D), act=b(2, 256, D), part=f(2, 4, 64, D),
+        send_p=b(2, 2, 2, 64, D), recv_p=b(2, 2, 2, 64, D), send_x=b(2, 2, 64, D), recv_x=b(2, 2, 64, D),
+        sum3=f(2, 64, D), dpre=b(2, 256, D), dsum3=f(2, 64, D), dfirst=f(128, D),
+        dq=b(128, D), dk=b(128, D), dv=b(128, D), dck=b(544, D), dcv=b(544, D),
+        core_s=b(2, 4, 192, D), core_c=b(2, 4, 272, D), xs=b(2, 4, 192, 384), xc=b(2, 4, 272, 384),
+        ys=b(4, 192, 384), yc=b(4, 272, 384), zs=b(3, 192, 384), zc=b(3, 272, 384),
+        yf=b(4, 384, D), zf=b(4, 384, D), fin_s=b(192, 384), fin_c=b(272, 384), fin_f=b(2, 192, D),
+        v_send=b(4, 16, D), v_in=b(3, 4, 16, D), v_z=b(4, 16, D), v_zin=b(3, 16, D), v_x=b(16, D), v_xin=b(16, D),
+        loc=dma(4), gz_s=dma(3, 4), gz_r=dma(3, 4), gy_s=dma(3, 4), gy_r=dma(3, 4), gx_s=dma(2, 7), gx_r=dma(2, 7),
+        gc_s=dma(3, 15), gc_r=dma(3, 15), t_s=dma(6), t_r=dma(4),
+        ex_s=dma(2, 2, 3), ex_r=dma(2, 2, 3), rs_s=dma(2, 2, 3), rs_r=dma(2, 2, 3),
+        co_s=dma(2, 2, 4), co_r=dma(2, 2, 4), xx_s=dma(2, 2, 4), xx_r=dma(2, 2, 4), yy_s=dma(3, 4), yy_r=dma(3, 4),
+        zz_s=dma(3, 4), zz_r=dma(3, 4), fi_s=dma(5), fi_r=dma(5), vv_s=dma(5), vv_r=dma(7),
+    )
+
+
+def layer_kernel(*refs):
+    names = [
+        "own_s", "own_c", "own_f", "own_t", "hid", "allowed", "feat", "cot",
+        "mixed", "hgrad", "out_s", "out_c", "out_f", "out_v",
+    ] + list(scratch())
+    r = SimpleNamespace(**dict(zip(names, refs)))
+    x, z, y, c = place()
+    core, xn, yn = device(x, z, y, 1 - c), device(1 - x, z, y, c), device(x, z, 1 - y, c)
+    diag = device(1 - x, z, y, 1 - c)
+    zdev = lambda d: device(x, (z + d) % 4, y, c)
+    meet([core, xn, yn, diag, device(x, z, 1 - y, 1 - c), zdev(1), zdev(2), zdev(3)])
+    me = 2 * c + x
+    cols = lambda h: pl.ds(pl.multiple_of(384 * h, 384), 384)
+    root = jnp.logical_and(y == 1, c == 1)
+    w1 = z % 2 == 0
+
+    def go(sent, src, dst, send, recv, target):
+        copy = remote(src, dst, send, recv, target)
+        copy.start()
+        sent.append(copy)
+
+    def arrived(view, recv):
+        remote(view, view, recv, recv, core).wait_recv()
+
+    def drain(sent):
+        for copy in sent:
+            copy.wait_send()
+
+    def shard_s(zz, yy, cc):
+        return r.ws.at[zz, pl.ds(pl.multiple_of(192 * (2 * yy + cc), 192), 192)]
+
+    def shard_c(zz, yy, cc):
+        return r.wc.at[pl.ds(pl.multiple_of(272 * ((zz * 2 + yy) * 2 + cc), 16), 272)]
+
+    def part_f(zz, yy):
+        return r.wf.at[zz, pl.ds(pl.multiple_of(384 * yy, 384), 384)]
+
+    shards = (shard_s, shard_c)
+    sent_w = ([], [], [])
+
+    def part(g, zz, yy, cc, h):
+        view = shards[g](zz, yy, cc)
+        return view if h is None else view.at[:, cols(h)]
+
+    def gather_own(g, own):
+        s = sent_w[g]
+        for k in (1, 2, 3):
+            go(s, own.at[:, cols(x)], part(g, z, y, c, x), r.gz_s.at[g, k], r.gz_r.at[g, k], zdev(k))
+        go(s, own.at[:, cols(x)], part(g, z, y, c, x), r.gy_s.at[g, 0], r.gy_r.at[g, 0], yn)
+        go(s, own, part(g, z, y, c, None), r.gc_s.at[g, 0], r.gc_r.at[g, 0], core)
+        copy = pltpu.make_async_copy(own, part(g, z, y, c, None), r.loc.at[g])
+        copy.start()
+        return copy
+
+    def gather_z(g):
+        for k in (1, 2, 3):
+            view = part(g, (z - k) % 4, y, c, x)
+            arrived(view, r.gz_r.at[g, k])
+            go(sent_w[g], view, view, r.gy_s.at[g, k], r.gy_r.at[g, k], yn)
+            go(sent_w[g], view, view, r.gx_s.at[g, k - 1], r.gx_r.at[g, k - 1], xn)
+            go(sent_w[g], view, view, r.gc_s.at[g, k], r.gc_r.at[g, k], core)
+
+    def gather_y(g):
+        for j in range(4):
+            view = part(g, (z - j) % 4, 1 - y, c, x)
+            arrived(view, r.gy_r.at[g, j])
+            go(sent_w[g], view, view, r.gx_s.at[g, 3 + j], r.gx_r.at[g, 3 + j], xn)
+            go(sent_w[g], view, view, r.gc_s.at[g, 4 + j], r.gc_r.at[g, 4 + j], core)
+
+    def gather_x(g):
+        for j in range(7):
+            view = part(g, (z - j - 1) % 4, y, c, 1 - x) if j < 3 else part(g, (z - j + 3) % 4, 1 - y, c, 1 - x)
+            arrived(view, r.gx_r.at[g, j])
+            go(sent_w[g], view, view, r.gc_s.at[g, 8 + j], r.gc_r.at[g, 8 + j], core)
+
+    def gather_core(g, which):
+        for j in which:
+            if j == 0:
+                view = part(g, z, y, 1 - c, None)
+            elif j < 4:
+                view = part(g, (z - j) % 4, y, 1 - c, x)
+            elif j < 8:
+                view = part(g, (z - j + 4) % 4, 1 - y, 1 - c, x)
+            elif j < 11:
+                view = part(g, (z - j + 7) % 4, y, 1 - c, 1 - x)
+            else:
+                view = part(g, (z - j + 11) % 4, 1 - y, 1 - c, 1 - x)
+            arrived(view, r.gc_r.at[g, j])
+
+    loc_s = gather_own(0, r.own_s)
+
+    @pl.when(root)
+    def _():
+        mine = pltpu.make_async_copy(r.own_t, r.tb.at[z], r.loc.at[3])
+        mine.start()
+        out = []
+        for k in (1, 2, 3):
+            go(out, r.own_t, r.tb.at[z], r.t_s.at[k - 1], r.t_r.at[k], zdev(k))
+        mine.wait()
+        for k in (1, 2, 3):
+            arrived(r.tb.at[(z - k) % 4], r.t_r.at[k])
+        for i, (yy, cc) in enumerate(((0, 0), (0, 1), (1, 0))):
+            go(out, r.tb, r.tb, r.t_s.at[3 + i], r.t_r.at[0], device(x, z, yy, cc))
+        drain(out)
+
+    loc_c = gather_own(1, r.own_c)
+    fb = pl.ds(pl.multiple_of(192 * c, 192), 192)
+
+    @pl.when(w1)
+    def _():
+        copy = remote(r.own_f.at[1], r.block_f.at[fb], r.gc_s.at[2, 0], r.gc_r.at[2, 0], core)
+        copy.start()
+        mine = pltpu.make_async_copy(r.own_f.at[0], r.block_f.at[fb], r.loc.at[2])
+        mine.start()
+        mine.wait()
+        copy.wait()
+
+    @pl.when(jnp.logical_not(w1))
+    def _():
+        for j in range(2):
+            mine = pltpu.make_async_copy(r.own_f.at[j], r.block_f.at[pl.ds(192 * j, 192)], r.loc.at[2])
+            mine.start()
+            mine.wait()
+
+    for k in (1, 2, 3):
+        go(sent_w[2], r.block_f, part_f(z, y), r.gz_s.at[2, k], r.gz_r.at[2, k], zdev(k))
+    go(sent_w[2], r.block_f, part_f(z, y), r.gy_s.at[2, 0], r.gy_r.at[2, 0], yn)
+    loc_f = pltpu.make_async_copy(r.block_f, part_f(z, y), r.loc.at[2])
+    loc_f.start()
+    r.vg[...] = jnp.zeros_like(r.vg)
+
+    gather_z(0)
+    gather_y(0)
+    gather_z(1)
+    gather_x(0)
+    gather_y(1)
+    loc_s.wait()
+
+    @pl.when(jnp.logical_not(root))
+    def _():
+        arrived(r.tb, r.t_r.at[0])
+
+    r.tv[...] = r.tb[...].astype(F32)
+    gather_core(0, range(15))
+
+    self_v = lambda j: r.tv[3, j : j + 1]
+    cross_v = lambda j: r.tv[3, 5 + j : 6 + j]
+    ffn_b1 = lambda b: r.tv[2 * b, pl.ds(10 + me, 1)]
+    ffn_v = lambda b, j: r.tv[2 * b + 1, 10 + j : 11 + j]
+
+    def slot(xx, cc):
+        return 2 * cc + xx
+
+    def ag_copies(ph, b):
+        buf = r.xg.at[ph, b]
+        pair = [(me, xn), (me, core), (slot(1 - x, c), core)]
+        return [
+            remote(buf.at[s], buf.at[s], r.ex_s.at[ph, b, i], r.ex_r.at[ph, b, i], t)
+            for i, (s, t) in enumerate(pair)
+        ]
+
+    def ag_start(ph, b):
+        to_x, to_p, fwd = ag_copies(ph, b)
+        to_x.start()
+        to_p.start()
+
+    def ag_mid(ph, b):
+        to_x, to_p, fwd = ag_copies(ph, b)
+        to_x.wait_recv()
+        fwd.start()
+
+    def ag_end(ph, b):
+        to_x, to_p, fwd = ag_copies(ph, b)
+        to_p.wait_recv()
+        fwd.wait_recv()
+        to_x.wait_send()
+        to_p.wait_send()
+        fwd.wait_send()
+
+    def rs_copies(ph, b):
+        far = remote(r.send_p.at[ph, b, 0], r.recv_p.at[ph, b, 0], r.rs_s.at[ph, b, 0], r.rs_r.at[ph, b, 0], core)
+        near = remote(r.send_p.at[ph, b, 1], r.recv_p.at[ph, b, 1], r.rs_s.at[ph, b, 1], r.rs_r.at[ph, b, 1], core)
+        over = remote(r.send_x.at[ph, b], r.recv_x.at[ph, b], r.rs_s.at[ph, b, 2], r.rs_r.at[ph, b, 2], xn)
+        return far, near, over
+
+    def rs_start(ph, b):
+        far, near, over = rs_copies(ph, b)
+        r.send_p[ph, b, 0] = r.part[b, slot(1 - x, 1 - c)].astype(BF)
+        far.start()
+        r.send_p[ph, b, 1] = r.part[b, slot(x, 1 - c)].astype(BF)
+        near.start()
+
+    def rs_mid(ph, b):
+        far, near, over = rs_copies(ph, b)
+        far.wait_recv()
+        r.send_x[ph, b] = (r.part[b, slot(1 - x, c)] + r.recv_p[ph, b, 0].astype(F32)).astype(BF)
+        over.start()
+
+    def rs_end(ph, b):
+        far, near, over = rs_copies(ph, b)
+        near.wait_recv()
+        over.wait_recv()
+        far.wait_send()
+        near.wait_send()
+        over.wait_send()
+        return r.part[b, me] + r.recv_p[ph, b, 1].astype(F32) + r.recv_x[ph, b].astype(F32)
+
+    h = r.hid[...]
+    r.q[...] = (mm(h, r.ws[0]) + self_v(0)).astype(BF)
+    r.k[...] = mm(h, r.ws[1]).astype(BF)
+    r.v[...] = (mm(h, r.ws[2]) + self_v(1)).astype(BF)
+    for i in range(2):
+        rows = slice(64 * i, 64 * i + 64)
+        ok = jnp.concatenate([r.allowed[i]] * 4, 0)
+        for g in range(3):
+            lanes = slice(256 * g, 256 * g + 256)
+            p, a = attend_block(r.q[rows, lanes], r.k[rows, lanes], r.v[rows, lanes], ok)
+            r.p[i, g] = p
+            r.a[rows, lanes] = a
+    r.sum1[...] = h.astype(F32) + (mm(r.a[...], r.ws[3]) + self_v(2))
+    xh, _ = normed(r.sum1[...])
+    r.first[...] = xh * self_v(3) + self_v(4)
+    r.xg[0, 1, me] = rows_of(r.first, 32).astype(BF)
+    ag_start(0, 1)
+
+    loc_c.wait()
+    gather_core(1, range(8))
+    for i in range(2):
+        rows = slice(272 * i, 272 * i + 272)
+        r.ck[rows, cols(x)] = mm(r.feat[rows], r.wc[768:2176, cols(x)]).astype(BF)
+        bias = r.tv[3, 6:7, cols(x)]
+        r.cv[rows, cols(x)] = (mm(r.feat[rows], r.wc[2176:3584, cols(x)]) + bias).astype(BF)
+    ag_mid(0, 1)
+    for k in (1, 2, 3):
+        view = part_f((z - k) % 4, y)
+        arrived(view, r.gz_r.at[2, k])
+        go(sent_w[2], view, view, r.gy_s.at[2, k], r.gy_r.at[2, k], yn)
+    gather_x(1)
+    gather_core(1, range(8, 15))
+    far_cols = cols(1 - x)
+    for i in range(2):
+        rows = slice(272 * i, 272 * i + 272)
+        r.ck[rows, far_cols] = mm(r.feat[rows], r.wc[768:2176, far_cols]).astype(BF)
+        bias = r.tv[3, 6:7, far_cols]
+        r.cv[rows, far_cols] = (mm(r.feat[rows], r.wc[2176:3584, far_cols]) + bias).astype(BF)
+    u = rows_of(r.first, 0)
+    r.cq[...] = (mm(u.astype(BF), r.wc[0:768]) + cross_v(0)).astype(BF)
+    ok = jnp.where(lax.broadcasted_iota(jnp.int32, (128, 272), 1) < 257, 1.0, 0.0)
+    for i in range(2):
+        rows = slice(272 * i, 272 * i + 272)
+        mine = slice(32 * i, 32 * i + 32)
+        for g in range(3):
+            lanes = slice(256 * g, 256 * g + 256)
+            p, a = attend_block(r.cq[mine, lanes], r.ck[rows, lanes], r.cv[rows, lanes], ok)
+            r.pc[i, g] = p
+            r.ca[mine, lanes] = a
+    r.sum2[...] = u + (mm(r.ca[...], r.wc[3584:4352]) + cross_v(2))
+    xh, _ = normed(r.sum2[...])
+    r.second[...] = xh * cross_v(3) + cross_v(4)
+    r.xg[0, 0, me] = r.second[...].astype(BF)
+    ag_start(0, 0)
+
+    loc_f.wait()
+    for j in range(4):
+        arrived(part_f((z - j) % 4, 1 - y), r.gy_r.at[2, j])
+
+    def ffn_forward_part(b):
+        rows = r.xg[0, b].reshape(256, D)
+        r.pre[b] = mm(rows, r.wf[2 * b]) + ffn_b1(b)
+        r.act[b] = gelu(r.pre[b]).astype(BF)
+        r.part[b] = mm(r.act[b], r.wf[2 * b + 1]).reshape(4, 64, D)
+
+    def ffn_turn(b):
+        rows = r.second[...] if b == 0 else rows_of(r.first, 32)
+        s3 = rows + (rs_end(0, b) + ffn_v(b, 0))
+        xh, _ = normed(s3)
+        done = (xh * ffn_v(b, 1) + ffn_v(b, 2)).astype(BF)
+        for i in range(2):
+            r.mixed[64 * i + 32 * b : 64 * i + 32 * b + 32] = done[32 * i : 32 * i + 32]
+        g_out = rows_of(r.cot, 32 * b).astype(F32)
+        dsum, dgain, dshift = norm_back(s3, ffn_v(b, 1), g_out)
+        r.dsum3[b] = dsum
+        low = dsum.astype(BF)
+        r.xg[1, b, me] = low
+        r.vg[2 * b + 1, 10:11] = rows_sum(low)
+        r.vg[2 * b + 1, 11:12] = dgain
+        r.vg[2 * b + 1, 12:13] = dshift
+
+    def ffn_backward_part(b):
+        up = r.xg[1, b].reshape(256, D)
+        r.dpre[b] = (mm_nt(up, r.wf[2 * b + 1]) * gelu_slope(r.pre[b])).astype(BF)
+        r.part[b] = mm_nt(r.dpre[b], r.wf[2 * b]).reshape(4, 64, D)
+        db1 = rows_sum(r.dpre[b])
+        for j in range(4):
+            r.vg[2 * b, 10 + j : 11 + j] = jnp.where(j == me, db1, 0.0)
+
+    sent = []
+
+    def ffn_weight_grads(b):
+        rows = r.xg[0, b].reshape(256, D)
+        up = r.xg[1, b].reshape(256, D)
+        r.wf[2 * b] = mm_tn(rows, r.dpre[b]).astype(BF)
+        r.wf[2 * b + 1] = mm_tn(r.act[b], up).astype(BF)
+        for p in (2 * b, 2 * b + 1):
+            go(sent, part_f(p, 1 - y), r.yf.at[p], r.yy_s.at[2, p], r.yy_r.at[2, p], yn)
+
+    def ffn_sum_y(p):
+        arrived(r.yf.at[p], r.yy_r.at[2, p])
+        r.yf[p] = add(r.yf[p], part_f(p, y)[...])
+
+        @pl.when(z != p)
+        def _():
+            remote(r.yf.at[p], r.zf.at[z], r.zz_s.at[2, p], r.zz_r.at[2, z], device(x, p, y, c)).start()
+
+    ag_end(0, 1)
+    ffn_forward_part(1)
+    rs_start(0, 1)
+    ag_mid(0, 0)
+    ag_end(0, 0)
+    rs_mid(0, 1)
+    ffn_forward_part(0)
+    rs_start(0, 0)
+    ffn_turn(1)
+    ag_start(1, 1)
+    rs_mid(0, 0)
+    ag_mid(1, 1)
+    ag_end(1, 1)
+    ffn_backward_part(1)
+    rs_start(1, 1)
+    ffn_turn(0)
+    ag_start(1, 0)
+    rs_mid(1, 1)
+    drain(sent_w[2])
+    ffn_weight_grads(1)
+    ag_mid(1, 0)
+    ag_end(1, 0)
+    ffn_backward_part(0)
+    rs_start(1, 0)
+    d_text = r.dsum3[1] + rs_end(1, 1)
+    for i in range(2):
+        r.dfirst[64 * i + 32 : 64 * i + 64] = d_text[32 * i : 32 * i + 32]
+    rs_mid(1, 0)
+    ffn_weight_grads(0)
+    d_second = r.dsum3[0] + rs_end(1, 0)
+
+    groups = (
+        (shard_s, r.core_s, r.xs, r.ys, r.zs, r.fin_s, r.out_s),
+        (shard_c, r.core_c, r.xc, r.yc, r.zc, r.fin_c, r.out_c),
+    )
+    order = (1, 2, 3, 0)
+
+    def sum_start(g):
+        view, cb = groups[g][:2]
+        for far in range(2):
+            for d in order:
+                zz = (z + d) % 4
+                go(sent, view(zz, y if far else 1 - y, 1 - c), cb.at[far, zz], r.co_s.at[g, far, d], r.co_r.at[g, far, d], core)
+
+    def sum_core(g):
+        view, cb, xb = groups[g][:3]
+        for far in range(2):
+            for d in order:
+                zz = (z + d) % 4
+                arrived(cb.at[far, zz], r.co_r.at[g, far, d])
+                cb[far, zz] = add(cb[far, zz], view(zz, y if far else 1 - y, c)[...])
+                go(sent, cb.at[far, zz, :, cols(1 - x)], xb.at[far, zz], r.xx_s.at[g, far, d], r.xx_r.at[g, far, d], xn)
+
+    def sum_x(g, far):
+        view, cb, xb, yb = groups[g][:4]
+        for d in order:
+            zz = (z + d) % 4
+            arrived(xb.at[far, zz], r.xx_r.at[g, far, d])
+            xb[far, zz] = add(xb[far, zz], cb[far, zz, :, cols(x)])
+            if far == 0:
+                go(sent, xb.at[0, zz], yb.at[zz], r.yy_s.at[g, d], r.yy_r.at[g, d], yn)
+
+    def sum_y(g):
+        view, cb, xb, yb, zb = groups[g][:5]
+        for d in order:
+            zz = (z + d) % 4
+            arrived(yb.at[zz], r.yy_r.at[g, d])
+            yb[zz] = add(yb[zz], xb[1, zz])
+            if d:
+                go(sent, yb.at[zz], zb.at[d - 1], r.zz_s.at[g, d - 1], r.zz_r.at[g, d - 1], device(x, zz, y, c))
+
+    def sum_z(g):
+        view, cb, xb, yb, zb, fin, out = groups[g]
+        for k in range(3):
+            arrived(zb.at[k], r.zz_r.at[g, k])
+        total = yb[z].astype(F32)
+        for k in range(3):
+            total = total + zb[k].astype(F32)
+        fin[...] = total.astype(BF)
+        out[:, cols(x)] = fin[...]
+        go(sent, fin, out.at[:, cols(x)], r.fi_s.at[g], r.fi_r.at[g], xn)
+
+    def ffn_sum_z():
+        total = r.yf[z].astype(F32)
+        for k in (1, 2, 3):
+            zz = (z + k) % 4
+            arrived(r.zf.at[zz], r.zz_r.at[2, zz])
+            total = total + r.zf[zz].astype(F32)
+        r.fin_f[...] = total.astype(BF).reshape(2, 192, D)
+
+        def both(copies):
+            for copy in copies:
+                copy.start()
+            for copy in copies:
+                copy.wait()
+
+        @pl.when(w1)
+        def _():
+            r.out_f[me] = r.fin_f[c]
+            both([
+                remote(r.fin_f.at[c], r.out_f.at[me], r.fi_s.at[2], r.fi_r.at[2], xn),
+                remote(r.fin_f.at[1 - c], r.out_f.at[me], r.fi_s.at[3], r.fi_r.at[3], core),
+                remote(r.fin_f.at[1 - c], r.out_f.at[me], r.fi_s.at[4], r.fi_r.at[4], diag),
+            ])
+
+        @pl.when(jnp.logical_not(w1))
+        def _():
+            copies = []
+            for j in range(2):
+                r.out_f[2 * x + j] = r.fin_f[j]
+                copies.append(remote(r.fin_f.at[j], r.out_f.at[2 * x + j], r.fi_s.at[2 + j], r.fi_r.at[2 + j], xn))
+            both(copies)
+
+    du2, dgain, dshift = norm_back(r.sum2[...], cross_v(3), d_second)
+    r.vg[3, 8:9] = dgain
+    r.vg[3, 9:10] = dshift
+    low = du2.astype(BF)
+    r.vg[3, 7:8] = rows_sum(low)
+    dca = mm_nt(low, r.wc[3584:4352]).astype(BF)
+    drain(sent_w[1])
+    r.wc[3584:4352] = mm_tn(r.ca[...], low).astype(BF)
+    dcq = []
+    for i in range(2):
+        rows = slice(272 * i, 272 * i + 272)
+        mine = slice(32 * i, 32 * i + 32)
+        blocks = []
+        for g in range(3):
+            lanes = slice(256 * g, 256 * g + 256)
+            dq, dk, dv = attend_block_back(
+                r.cq[mine, lanes], r.ck[rows, lanes], r.cv[rows, lanes], r.pc[i, g], dca[mine, lanes]
+            )
+            blocks.append(dq)
+            r.dck[rows, lanes] = dk
+            r.dcv[rows, lanes] = dv
+        dcq.append(jnp.concatenate(blocks, 1))
+    dcq = jnp.concatenate(dcq, 0)
+    r.vg[3, 5:6] = rows_sum(dcq)
+    r.vg[3, 6:7] = rows_sum(r.dcv[...])
+    du = du2 + mm_nt(dcq, r.wc[0:768])
+    for i in range(2):
+        r.dfirst[64 * i : 64 * i + 32] = du[32 * i : 32 * i + 32]
+    r.wc[0:768] = mm_tn(rows_of(r.first, 0).astype(BF), dcq).astype(BF)
+    for j in range(11):
+        block = r.feat[:, 128 * j : 128 * j + 128]
+        r.wc[768 + 128 * j : 896 + 128 * j] = mm_tn(block, r.dck[...]).astype(BF)
+        r.wc[2176 + 128 * j : 2304 + 128 * j] = mm_tn(block, r.dcv[...]).astype(BF)
+    sum_start(1)
+    ffn_sum_y(2)
+    ffn_sum_y(3)
+
+    dsum1, dgain, dshift = norm_back(r.sum1[...], self_v(3), r.dfirst[...])
+    r.vg[3, 3:4] = dgain
+    r.vg[3, 4:5] = dshift
+    low = dsum1.astype(BF)
+    r.vg[3, 2:3] = rows_sum(low)
+    da = mm_nt(low, r.ws[3]).astype(BF)
+    drain(sent_w[0])
+    r.ws[3] = mm_tn(r.a[...], low).astype(BF)
+    for i in range(2):
+        rows = slice(64 * i, 64 * i + 64)
+        for g in range(3):
+            lanes = slice(256 * g, 256 * g + 256)
+            dq, dk, dv = attend_block_back(
+                r.q[rows, lanes], r.k[rows, lanes], r.v[rows, lanes], r.p[i, g], da[rows, lanes]
+            )
+            r.dq[rows, lanes] = dq
+            r.dk[rows, lanes] = dk
+            r.dv[rows, lanes] = dv
+    sum_core(1)
+    r.vg[3, 0:1] = rows_sum(r.dq[...])
+    r.vg[3, 1:2] = rows_sum(r.dv[...])
+    total = dsum1 + mm_nt(r.dq[...], r.ws[0]) + mm_nt(r.dk[...], r.ws[1]) + mm_nt(r.dv[...], r.ws[2])
+    r.hgrad[...] = total.astype(BF)
+    r.ws[0] = mm_tn(r.hid[...], r.dq[...]).astype(BF)
+    r.ws[1] = mm_tn(r.hid[...], r.dk[...]).astype(BF)
+    r.ws[2] = mm_tn(r.hid[...], r.dv[...]).astype(BF)
+    sum_start(0)
+
+    r.v_send[...] = r.vg[...].astype(BF)
+    index = 2 * y + c
+    home = device(x, z, 1, 1)
+
+    @pl.when(jnp.logical_not(root))
+    def _():
+        remote(r.v_send, r.v_in.at[index], r.vv_s.at[0], r.vv_r.at[index], home).start()
+
+    ffn_sum_y(0)
+    ffn_sum_y(1)
+    sum_x(1, 0)
+    sum_core(0)
+
+    @pl.when(root)
+    def _():
+        total = r.vg[...]
+        for i in range(3):
+            arrived(r.v_in.at[i], r.vv_r.at[i])
+            total = total + r.v_in[i].astype(F32)
+        r.v_z[...] = total.astype(BF)
+        for k in (1, 2, 3):
+            zz = (z + k) % 4
+            remote(r.v_z.at[zz], r.v_zin.at[k - 1], r.vv_s.at[k], r.vv_r.at[2 + k], device(x, zz, y, c)).start()
+
+    sum_x(1, 1)
+    sum_y(1)
+    ffn_sum_z()
+    sum_x(0, 0)
+    sum_x(0, 1)
+
+    @pl.when(root)
+    def _():
+        total = r.v_z[z].astype(F32)
+        for k in (1, 2, 3):
+            arrived(r.v_zin.at[k - 1], r.vv_r.at[2 + k])
+            total = total + r.v_zin[k - 1].astype(F32)
+        r.v_x[...] = total.astype(BF)
+        remote(r.v_x, r.v_xin, r.vv_s.at[4], r.vv_r.at[6], xn).start()
+
+    sum_y(0)
+    sum_z(1)
+    sum_z(0)
+
+    @pl.when(root)
+    def _():
+        arrived(r.v_xin, r.vv_r.at[6])
+        r.out_v[...] = r.v_x[...].astype(F32) + r.v_xin[...].astype(F32)
+        for k in (1, 2, 3):
+            zz = (z + k) % 4
+            remote(r.v_z.at[zz], r.v_zin.at[k - 1], r.vv_s.at[k], r.vv_r.at[2 + k], device(x, zz, y, c)).wait_send()
+        remote(r.v_x, r.v_xin, r.vv_s.at[4], r.vv_r.at[6], xn).wait_send()
+
+    @pl.when(jnp.logical_not(root))
+    def _():
+        r.out_v[...] = jnp.zeros_like(r.out_v)
+        remote(r.v_send, r.v_in.at[index], r.vv_s.at[0], r.vv_r.at[index], home).wait_send()
+
+    for g in range(2):
+        arrived(groups[g][6].at[:, cols(1 - x)], r.fi_r.at[g])
+    for p in range(4):
+
+        @pl.when(z != p)
+        def _():
+            remote(r.yf.at[p], r.zf.at[z], r.zz_s.at[2, p], r.zz_r.at[2, z], device(x, p, y, c)).wait_send()
+
+    drain(sent)
+
+
+def layer(own_s, own_c, own_f, own_t, hid, allowed, feat, cot):
+    vm = pl.BlockSpec(memory_space=pltpu.VMEM)
+    anywhere = pl.BlockSpec(memory_space=pl.ANY)
+    return pl.pallas_call(
+        layer_kernel,
+        out_shape=(
+            jax.ShapeDtypeStruct((128, D), BF),
+            jax.ShapeDtypeStruct((128, D), BF),
+            jax.ShapeDtypeStruct((192, D), BF),
+            jax.ShapeDtypeStruct((272, D), BF),
+            jax.ShapeDtypeStruct((4, 192, D), BF),
+            jax.ShapeDtypeStruct((16, D), F32),
+        ),
+        in_specs=[anywhere] * 4 + [vm] * 4,
+        out_specs=[vm] * 6,
+        scratch_shapes=list(scratch().values()),
+        compiler_params=pltpu.CompilerParams(
+            collective_id=0, has_side_effects=True, vmem_limit_bytes=VMEM_BYTES
+        ),
+    )(own_s, own_c, own_f, own_t, hid, allowed, feat, cot)
+
+
+def shift_back():
+    x, z, y, c = place()
+    f = lax.axis_index("fsdp")
+    return 2 * f, 2 * f, 6 * (f % 4) + jnp.where(z >= 2, 6, 0)
+
+
+def own_rows(self_params, cross_params, ffn_params):
+    x, z, y, c = place()
+    flats = [v.reshape(-1, 128) for v in (self_params, cross_params, ffn_params)]
+    tails = jnp.concatenate([v[-32:] for v in flats])
+    before = lax.ppermute(tails, "fsdp", [(i, (i + 1) % 16) for i in range(16)])
+    nice = []
+    for i, (v, rows, back) in enumerate(zip(flats, (1152, 1632, 4608), shift_back())):
+        both = jnp.concatenate([before[32 * i : 32 * i + 32], v])
+        nice.append(lax.dynamic_slice_in_dim(both, 32 - back, rows))
+    own_s = nice[0].reshape(192, D)
+    own_c = nice[1].reshape(272, D)
+    cols = nice[2].reshape(192, 2, 4, 3, 128)
+    pick = lambda cc: lax.dynamic_index_in_dim(cols, 2 * cc + x, 2, keepdims=False).reshape(192, D)
+    as_w1 = jnp.stack([pick(c), pick(1 - c)])
+    as_w2 = lax.dynamic_index_in_dim(nice[2].reshape(2, 2, 192, D), x, keepdims=False)
+    own_f = jnp.where(z % 2 == 0, as_w1, as_w2)
+
+    b1 = lambda v: v.reshape(2, 4, 384).transpose(1, 0, 2).reshape(4, D)
+    rest = lambda v: jnp.concatenate([v.reshape(3, D), jnp.zeros((1, D), BF)])
+    ffn = jnp.stack([b1(tails[72:96]), rest(tails[72:90]), b1(tails[66:90]), rest(tails[66:84])])
+    own_t = jnp.concatenate([
+        tails[0:30].reshape(5, D),
+        tails[32:62].reshape(5, D),
+        lax.dynamic_index_in_dim(ffn, z, keepdims=False),
+        jnp.zeros((2, D), BF),
+    ])
+    return own_s, own_c, own_f, own_t
+
+
+def flat_grads(out_s, out_c, out_f, out_v):
+    x, z, y, c = place()
+    f = lax.axis_index("fsdp")
+    k = f % 4
+    w1 = out_f.reshape(4, 192, 2, 3, 128).transpose(1, 2, 0, 3, 4).reshape(4608, 128)
+    w2 = out_f.reshape(4608, 128)
+    nice = [out_s.reshape(1152, 128), out_c.reshape(1632, 128), jnp.where(z % 2 == 0, w1, w2)]
+    heads = jnp.concatenate([v[:32] for v in nice])
+    after = lax.ppermute(heads, "fsdp", [(i, (i + 15) % 16) for i in range(16)]).astype(F32)
+    zeros = lambda n: jnp.zeros((n, 128), F32)
+    flat = lambda v: v.reshape(-1, 128)
+    tail_s = jnp.where(f == 15, jnp.concatenate([flat(out_v[0:5]), zeros(2)]), after[0:32])
+    tail_c = jnp.where(f == 15, jnp.concatenate([flat(out_v[5:10]), zeros(2)]), after[32:64])
+    nxt = after[64:96]
+    b1 = out_v[10:14].reshape(4, 2, 384).transpose(1, 0, 2).reshape(24, 128)
+    rest = flat(out_v[10:13])
+    ends = jnp.stack([
+        jnp.concatenate([b1, zeros(8)]),
+        jnp.concatenate([rest, nxt[:14]]),
+        jnp.concatenate([b1, nxt[:8]]),
+        jnp.concatenate([rest, zeros(14)]),
+    ])
+    tail_f = jnp.where(k == 3, lax.dynamic_index_in_dim(ends, z, keepdims=False), nxt)
+    outs = []
+    for v, tail, start, rows in zip(nice, (tail_s, tail_c, tail_f), shift_back(), (1154, 1634, 4614)):
+        both = jnp.concatenate([v.astype(F32), tail])
+        outs.append(lax.dynamic_slice_in_dim(both, start, rows).reshape(-1))
+    return outs
+
+
+def per_device_fast(hidden, lengths, features, cotangent, self_params, cross_params, ffn_params):
+    own = own_rows(self_params, cross_params, ffn_params)
+    at = jnp.arange(64)
+    r, k = at[:, None], at[None, :]
+    allowed = (k < NQ)[None] | ((r >= NQ) & (k <= r))[None] & (k[None] < NQ + lengths[:, None, None])
+    feat = jnp.pad(features, ((0, 0), (0, 15), (0, 0))).reshape(544, E)
+    mixed, hgrad, *sums = layer(
+        *own, hidden.reshape(128, D), allowed.astype(F32), feat, cotangent.reshape(128, D)
+    )
+    return (mixed.reshape(2, 64, D), hgrad.reshape(2, 64, D), *flat_grads(*sums))
+
+
 def solution(mesh):
+    fast = mesh.shape["dp"] == 2 and mesh.shape["fsdp"] == 16
     return jax.shard_map(
-        per_device,
+        per_device_fast if fast else per_device,
         mesh=mesh,
         in_specs=(
             P(("dp", "fsdp"), None, None),

time: 2630 us -> 347 us (0.13)
  blocking collectives: 984 us -> 0 us
  local copies, waits for them, and re-layouts: 767 us -> 27 us
  other arithmetic: 672 us -> 13.9 us
  Pallas kernels: 0 us -> 295 us
  matrix products: 94.1 us -> 0 us
  waiting for transfers between devices: 71.3 us -> 0.01 us
    unnamed x1 -> x0, blocking collectives: 961 us -> none
    all_gather x3 -> x0, other arithmetic: 620 us -> none  [the longest x1 401 us: per_device(): ffn_full = lax.all_gather(ffn_params, 'fsdp', axis=0, tiled=True)]
    unnamed x312 -> x29, local copies, waits for them, and re-layouts: 337 us -> 3.66 us
    pallas_call x0 -> x1, Pallas kernels: none -> 295 us  [layer(): pl.pallas_call(layer_kernel, out_shape=(jax.ShapeDtypeStruct((128, D), BF...]
    reshape x37 -> x18, local copies, waits for them, and re-layouts: 233 us -> 13.6 us  [the longest x2 4.57 us: flat_grads(): out_f.reshape(4, 192, 2, 3, 128).transpose(1, 2, 0, 3, 4).reshape(4608, 128)]
    dot_general x46 -> x0, matrix products: 94.1 us -> none  [the longest x12 37.9 us: matmul_left(): lax.dot_general(left, right, (((0,), (0,)), ((), ())), preferred_element_...]
    all_gather x4 -> x0, waiting for transfers between devices: 71.2 us -> none  [the longest x1 60.6 us: per_device(): self_full = lax.all_gather(self_params, 'fsdp', axis=0, tiled=True)]
    transpose x3 -> x2, local copies, waits for them, and re-layouts: 48.2 us -> 0.55 us  [the longest x1 0.54 us: flat_grads(): out_f.reshape(4, 192, 2, 3, 128).transpose(1, 2, 0, 3, 4).reshape(4608, 128)]
  transfers between devices with their start and end apart: 4 -> 2, of which waited for: 2 -> 0; matrix products, arithmetic and copies ran while one was open for 14% -> 4% of each run, Pallas kernels for 0% -> 0%
where the time goes in v2:
time: 347 us; the launch traced here: 342 us
  Pallas kernels  295 us (85%)
  local copies, waits for them, and re-layouts  27 us (8%)
  other arithmetic  13.9 us (4%)
  starting transfers between devices  4.65 us (1%)
    pallas_call x1, Pallas kernels, layer(): pl.pallas_call(layer_kernel, out_shape=(jax.ShapeDtypeStruct((128, D), BF...  295 us
  transfers between devices with their start and end apart: 2, of which 0 were waited for; matrix products, arithmetic and copies ran while one was open for 4% of the time, Pallas kernels for 0%

profile of v2, /device:TPU:0, one launch (start us, length us, event | category | flops | bytes accessed | tf_op | source)
XLA Modules:
  0.0 342.1 jit_solution(13138698303369855840)
XLA Ops:
  0.6 0.7 slice_bitcast_fusion.2
  1.3 0.7 slice_bitcast_fusion
  2.6 0.8 fusion.21
  3.4 0.8 fusion.20
  8.0 1.5 copy.18
  9.5 1.2 pad.10.clone
  12.5 1.9 reshape.216
  15.7 1.1 reshape.213.refs_1_
  17.0 1.0 reshape.211.refs_0_
  18.0 0.9 maximum_select_fusion.refs_2_
  18.9 295.2 %shard_map.110 = (bf16[128,768]{1,0:T(8,128)(2,1)}, bf16[128,768]{1,0:T(8,128)(2,1)}, bf16[192,768]{1,0:T(8,128)(2,1)}, bf16[272,768]{1,0:T(8,128)(2,1)}, bf16[4...) custom-call(bf16[192,768]{1,0:T(8,128)(2,1)} %reshape.211.refs_0_, bf16[272,768]{1,0:T(8,128)(2,1)} %reshape.213.refs_1_, ...), custom_call_target="tpu_custom_call" | custom-call | tf_op jit(solution)/shard_map/pallas_call | solution.py:1025
  314.1 2.4 reshape.229
  316.5 1.9 reshape.231
  319.0 2.1 reshape.230
  321.1 1.6 fusion.19
  323.1 1.4 reshape.226
  325.1 4.1 %collective-permute-start.1 = (bf16[96,128]{1,0:T(8,128)(2,1)}, bf16[96,128]{1,0:T(8,128)(2,1)}, u32[]{:S(2)}, u32[]{:S(2)}) collective-permute-start(bf16[96,128]{1,0:T(8,128)(2,1)} %pad_maximum_fusion.1), channel_id=1, source_target_pairs={{0,15},{1,0},{2,1},{3,2},{4,3},{5,4},{6,5},{7,6},{8,7},{9,8},{10,9... | collective-permute-start | bytes 73736 | tf_op jit(solution)/shard_map/ppermute | solution.py:1087
  330.5 1.1 convert_element_type.20
  331.6 0.9 convert_element_type.18
  332.4 0.7 reshape.237
  334.6 0.7 convert_element_type.19
  335.4 2.5 fusion.1
  337.9 1.3 fusion.4
  339.2 1.1 fusion.6
  (78 shorter events, 13.1 us)
Async XLA Ops:
  2.1 8.7 %collective-permute-start = (bf16[96,128]{1,0:T(8,128)(2,1)S(1)}, bf16[96,128]{1,0:T(8,128)(2,1)S(1)}, u32[]{:S(2)}, u32[]{:S(2)}) collective-permute-start(bf16[96,128]{1,0:T(8,128)(2,1)S(1)} %pad_maximum_fusion), channel_id=1, source_target_pairs={{0,1},{1,2},{2,3},{3,4},{4,5},{5,6},{6,7},{7,8},{8,9},{9,10},{10,1... | collective-permute-start | bytes 73736 | tf_op jit(solution)/shard_map/ppermute | solution.py:1054
  9.5 1.8 copy-start.4
  14.4 1.0 copy-start.5
  15.0 1.9 copy-start.7
  15.7 2.3 copy-start.1
  314.1 2.5 copy-start
  321.1 1.6 copy-start.6
  322.7 6.6 %copy-start.10 = (f32[16,768]{1,0:T(8,128)S(1)}, f32[16,768]{1,0:T(8,128)}, u32[]{:S(2)}) copy-start(f32[16,768]{1,0:T(8,128)} %get-tuple-element.14) | copy-start | bytes 147460
  323.1 7.4 %copy-start.3 = (bf16[1632,128]{1,0:T(8,128)(2,1)}, bf16[1632,128]{1,0:T(8,128)(2,1)S(1)}, u32[]{:S(2)}) copy-start(bf16[1632,128]{1,0:T(8,128)(2,1)S(1)} %reshape.228) | copy-start | bytes 1253380
  325.1 8.1 %collective-permute-start.1 = (bf16[96,128]{1,0:T(8,128)(2,1)}, bf16[96,128]{1,0:T(8,128)(2,1)}, u32[]{:S(2)}, u32[]{:S(2)}) collective-permute-start(bf16[96,128]{1,0:T(8,128)(2,1)} %pad_maximum_fusion.1), channel_id=1, source_target_pairs={{0,15},{1,0},{2,1},{3,2},{4,3},{5,4},{6,5},{7,6},{8,7},{9,8},{10,9... | collective-permute-start | bytes 73736 | tf_op jit(solution)/shard_map/ppermute | solution.py:1087
  330.5 2.7 copy-start.12
  330.5 2.7 copy-start.11
  337.9 1.3 copy-start.2
  337.9 2.4 copy-start.9
  339.2 1.8 copy-start.8

commit v3 on v2

--- a/solution.py
+++ b/solution.py
@@ -433,6 +433,11 @@
     return jnp.concatenate([ref[first : first + 32], ref[64 + first : 96 + first]], 0)
 
 
+SPLIT = 288
+REST = 384 - SPLIT
+STREAMS = ((192, 384), (272, 384), (SPLIT, D), (REST, D), (REST, D))
+
+
 def scratch():
     dma = lambda *s: pltpu.SemaphoreType.DMA(s)
     b = lambda *s: pltpu.VMEM(s, BF)
@@ -448,14 +453,15 @@
         sum3=f(2, 64, D), dpre=b(2, 256, D), dsum3=f(2, 64, D), dfirst=f(128, D),
         dq=b(128, D), dk=b(128, D), dv=b(128, D), dck=b(544, D), dcv=b(544, D),
         core_s=b(2, 4, 192, D), core_c=b(2, 4, 272, D), xs=b(2, 4, 192, 384), xc=b(2, 4, 272, 384),
-        ys=b(4, 192, 384), yc=b(4, 272, 384), zs=b(3, 192, 384), zc=b(3, 272, 384),
-        yf=b(4, 384, D), zf=b(4, 384, D), fin_s=b(192, 384), fin_c=b(272, 384), fin_f=b(2, 192, D),
+        ys=b(4, 192, 384), yc=b(4, 272, 384), yf=b(4, SPLIT, D), yf2=b(REST, D), of=b(REST, D),
+        fin_s=b(192, 384), fin_c=b(272, 384), fin_f=b(384, D),
+        **{f"{n}{i}": b(*lead, *shape) for i, shape in enumerate(STREAMS) for n, lead in (("zb", (3,)), ("zr", ()), ("zq", ()))},
         v_send=b(4, 16, D), v_in=b(3, 4, 16, D), v_z=b(4, 16, D), v_zin=b(3, 16, D), v_x=b(16, D), v_xin=b(16, D),
-        loc=dma(4), gz_s=dma(3, 4), gz_r=dma(3, 4), gy_s=dma(3, 4), gy_r=dma(3, 4), gx_s=dma(2, 7), gx_r=dma(2, 7),
+        loc=dma(4), gz_s=dma(7, 4), gz_r=dma(7, 4), gy_s=dma(7, 4), gy_r=dma(7, 4), gx_s=dma(2, 7), gx_r=dma(2, 7),
         gc_s=dma(3, 15), gc_r=dma(3, 15), t_s=dma(6), t_r=dma(4),
         ex_s=dma(2, 2, 3), ex_r=dma(2, 2, 3), rs_s=dma(2, 2, 3), rs_r=dma(2, 2, 3),
-        co_s=dma(2, 2, 4), co_r=dma(2, 2, 4), xx_s=dma(2, 2, 4), xx_r=dma(2, 2, 4), yy_s=dma(3, 4), yy_r=dma(3, 4),
-        zz_s=dma(3, 4), zz_r=dma(3, 4), fi_s=dma(5), fi_r=dma(5), vv_s=dma(5), vv_r=dma(7),
+        co_s=dma(2, 2, 4), co_r=dma(2, 2, 4), xx_s=dma(2, 2, 4), xx_r=dma(2, 2, 4), yy_s=dma(4, 4), yy_r=dma(4, 4),
+        zz_s=dma(5, 4), zz_r=dma(5, 4), zq_s=dma(5), zq_r=dma(5), fi_s=dma(5), fi_r=dma(5), vv_s=dma(5), vv_r=dma(7),
     )
 
 
@@ -475,17 +481,26 @@
     root = jnp.logical_and(y == 1, c == 1)
     w1 = z % 2 == 0
 
-    def go(sent, src, dst, send, recv, target):
-        copy = remote(src, dst, send, recv, target)
-        copy.start()
-        sent.append(copy)
+    inner = jnp.logical_and(z > 0, z < 3)
+    outer = jnp.logical_not(inner)
+
+    def when(cond, what):
+        if cond is None:
+            what()
+        else:
+            pl.when(cond)(what)
+
+    def go(sent, src, dst, send, recv, target, cond=None):
+        make = lambda: remote(src, dst, send, recv, target)
+        when(cond, lambda: make().start())
+        sent.append((make, cond))
 
     def arrived(view, recv):
         remote(view, view, recv, recv, core).wait_recv()
 
     def drain(sent):
-        for copy in sent:
-            copy.wait_send()
+        for make, cond in sent:
+            when(cond, lambda: make().wait_send())
 
     def shard_s(zz, yy, cc):
         return r.ws.at[zz, pl.ds(pl.multiple_of(192 * (2 * yy + cc), 192), 192)]
@@ -493,40 +508,75 @@
     def shard_c(zz, yy, cc):
         return r.wc.at[pl.ds(pl.multiple_of(272 * ((zz * 2 + yy) * 2 + cc), 16), 272)]
 
-    def part_f(zz, yy):
-        return r.wf.at[zz, pl.ds(pl.multiple_of(384 * yy, 384), 384)]
+    def part_f(zz, yy, lo=0, n=384):
+        return r.wf.at[zz, pl.ds(pl.multiple_of(384 * yy + lo, 16), n)]
 
     shards = (shard_s, shard_c)
     sent_w = ([], [], [])
+    steps = [jnp.where(z == 0, 3 - i, jnp.where(z == 3, 1 + i, (2, 1, 3)[i])) for i in range(3)]
 
     def part(g, zz, yy, cc, h):
+        if g >= 2:
+            return part_f(zz, yy, 96 * (g - 2), 96)
         view = shards[g](zz, yy, cc)
         return view if h is None else view.at[:, cols(h)]
 
-    def gather_own(g, own):
-        s = sent_w[g]
-        for k in (1, 2, 3):
-            go(s, own.at[:, cols(x)], part(g, z, y, c, x), r.gz_s.at[g, k], r.gz_r.at[g, k], zdev(k))
-        go(s, own.at[:, cols(x)], part(g, z, y, c, x), r.gy_s.at[g, 0], r.gy_r.at[g, 0], yn)
-        go(s, own, part(g, z, y, c, None), r.gc_s.at[g, 0], r.gc_r.at[g, 0], core)
+    def own_part(g):
+        if g >= 2:
+            return r.block_f.at[pl.ds(96 * (g - 2), 96)]
+        return (r.own_s, r.own_c)[g].at[:, cols(x)]
+
+    def z_out(src, dst, g, i):
+        for k in (2, 1, 3):
+            cond = {1: z != 3, 2: None, 3: z != 0}[k]
+            go(sent_w[min(g, 2)], src, dst, r.gz_s.at[i, k], r.gz_r.at[i, k], zdev(k), cond)
+
+    def z_on(view, g, i, k):
+        cond = jnp.logical_and(inner, k == 2)
+        go(sent_w[min(g, 2)], view, view, r.gz_s.at[i, 0], r.gz_r.at[i, 2 * z - 1], device(x, 3 * (z - 1), y, c), cond)
+
+    def own_z(g):
+        z_out(own_part(g), part(g, z, y, c, x), g, g)
+
+    def own_y(g):
+        go(sent_w[min(g, 2)], own_part(g), part(g, z, y, c, x), r.gy_s.at[g, 0], r.gy_r.at[g, 0], yn)
+
+    def own_core(g):
+        own = (r.own_s, r.own_c)[g]
+        go(sent_w[g], own, part(g, z, y, c, None), r.gc_s.at[g, 0], r.gc_r.at[g, 0], core)
         copy = pltpu.make_async_copy(own, part(g, z, y, c, None), r.loc.at[g])
         copy.start()
         return copy
 
-    def gather_z(g):
-        for k in (1, 2, 3):
+    def gather_z(g, last=False):
+        for k in steps:
             view = part(g, (z - k) % 4, y, c, x)
             arrived(view, r.gz_r.at[g, k])
-            go(sent_w[g], view, view, r.gy_s.at[g, k], r.gy_r.at[g, k], yn)
-            go(sent_w[g], view, view, r.gx_s.at[g, k - 1], r.gx_r.at[g, k - 1], xn)
-            go(sent_w[g], view, view, r.gc_s.at[g, k], r.gc_r.at[g, k], core)
-
-    def gather_y(g):
-        for j in range(4):
+            z_on(view, g, g, k)
+            if not last:
+                go(sent_w[min(g, 2)], view, view, r.gy_s.at[g, k], r.gy_r.at[g, k], yn)
+            if g < 2:
+                go(sent_w[g], view, view, r.gx_s.at[g, k - 1], r.gx_r.at[g, k - 1], xn)
+                go(sent_w[g], view, view, r.gc_s.at[g, k], r.gc_r.at[g, k], core)
+
+    def gather_y(g, which=(0, 1, 2, 3)):
+        for j in which:
             view = part(g, (z - j) % 4, 1 - y, c, x)
             arrived(view, r.gy_r.at[g, j])
-            go(sent_w[g], view, view, r.gx_s.at[g, 3 + j], r.gx_r.at[g, 3 + j], xn)
-            go(sent_w[g], view, view, r.gc_s.at[g, 4 + j], r.gc_r.at[g, 4 + j], core)
+            if g < 2:
+                go(sent_w[g], view, view, r.gx_s.at[g, 3 + j], r.gx_r.at[g, 3 + j], xn)
+                go(sent_w[g], view, view, r.gc_s.at[g, 4 + j], r.gc_r.at[g, 4 + j], core)
+
+    def other_z():
+        view = part(5, z, 1 - y, c, x)
+        arrived(view, r.gy_r.at[5, 0])
+        z_out(view, view, 5, 6)
+
+    def other_arrivals():
+        for k in steps:
+            view = part(5, (z - k) % 4, 1 - y, c, x)
+            arrived(view, r.gz_r.at[6, k])
+            z_on(view, 5, 6, k)
 
     def gather_x(g):
         for j in range(7):
@@ -548,7 +598,9 @@
                 view = part(g, (z - j + 11) % 4, 1 - y, 1 - c, 1 - x)
             arrived(view, r.gc_r.at[g, j])
 
-    loc_s = gather_own(0, r.own_s)
+    own_z(0)
+    own_y(0)
+    loc_s = own_core(0)
 
     @pl.when(root)
     def _():
@@ -564,7 +616,9 @@
             go(out, r.tb, r.tb, r.t_s.at[3 + i], r.t_r.at[0], device(x, z, yy, cc))
         drain(out)
 
-    loc_c = gather_own(1, r.own_c)
+    own_z(1)
+    own_y(1)
+    loc_c = own_core(1)
     fb = pl.ds(pl.multiple_of(192 * c, 192), 192)
 
     @pl.when(w1)
@@ -583,18 +637,25 @@
             mine.start()
             mine.wait()
 
-    for k in (1, 2, 3):
-        go(sent_w[2], r.block_f, part_f(z, y), r.gz_s.at[2, k], r.gz_r.at[2, k], zdev(k))
-    go(sent_w[2], r.block_f, part_f(z, y), r.gy_s.at[2, 0], r.gy_r.at[2, 0], yn)
     loc_f = pltpu.make_async_copy(r.block_f, part_f(z, y), r.loc.at[2])
     loc_f.start()
     r.vg[...] = jnp.zeros_like(r.vg)
 
+    own_y(5)
     gather_z(0)
+    own_z(2)
+    for g in (2, 3, 4):
+        own_y(g)
     gather_y(0)
+    own_z(3)
     gather_z(1)
+    own_z(4)
+    own_z(5)
+    other_z()
+    gather_y(1, (0,))
+    gather_z(2)
     gather_x(0)
-    gather_y(1)
+    gather_y(1, (1, 2, 3))
     loc_s.wait()
 
     @pl.when(jnp.logical_not(root))
@@ -612,58 +673,47 @@
     def slot(xx, cc):
         return 2 * cc + xx
 
-    def ag_copies(ph, b):
+    def ag_copy(ph, b, i):
         buf = r.xg.at[ph, b]
         pair = [(me, xn), (me, core), (slot(1 - x, c), core)]
-        return [
-            remote(buf.at[s], buf.at[s], r.ex_s.at[ph, b, i], r.ex_r.at[ph, b, i], t)
-            for i, (s, t) in enumerate(pair)
-        ]
+        s, t = pair[i]
+        return remote(buf.at[s], buf.at[s], r.ex_s.at[ph, b, i], r.ex_r.at[ph, b, i], t)
 
     def ag_start(ph, b):
-        to_x, to_p, fwd = ag_copies(ph, b)
-        to_x.start()
-        to_p.start()
+        ag_copy(ph, b, 0).start()
+        ag_copy(ph, b, 1).start()
 
     def ag_mid(ph, b):
-        to_x, to_p, fwd = ag_copies(ph, b)
-        to_x.wait_recv()
-        fwd.start()
+        ag_copy(ph, b, 0).wait_recv()
+        ag_copy(ph, b, 2).start()
 
     def ag_end(ph, b):
-        to_x, to_p, fwd = ag_copies(ph, b)
-        to_p.wait_recv()
-        fwd.wait_recv()
-        to_x.wait_send()
-        to_p.wait_send()
-        fwd.wait_send()
-
-    def rs_copies(ph, b):
-        far = remote(r.send_p.at[ph, b, 0], r.recv_p.at[ph, b, 0], r.rs_s.at[ph, b, 0], r.rs_r.at[ph, b, 0], core)
-        near = remote(r.send_p.at[ph, b, 1], r.recv_p.at[ph, b, 1], r.rs_s.at[ph, b, 1], r.rs_r.at[ph, b, 1], core)
-        over = remote(r.send_x.at[ph, b], r.recv_x.at[ph, b], r.rs_s.at[ph, b, 2], r.rs_r.at[ph, b, 2], xn)
-        return far, near, over
+        ag_copy(ph, b, 1).wait_recv()
+        ag_copy(ph, b, 2).wait_recv()
+        for i in range(3):
+            ag_copy(ph, b, i).wait_send()
+
+    def rs_copy(ph, b, i):
+        src = r.send_x.at[ph, b] if i == 2 else r.send_p.at[ph, b, i]
+        dst = r.recv_x.at[ph, b] if i == 2 else r.recv_p.at[ph, b, i]
+        return remote(src, dst, r.rs_s.at[ph, b, i], r.rs_r.at[ph, b, i], xn if i == 2 else core)
 
     def rs_start(ph, b):
-        far, near, over = rs_copies(ph, b)
         r.send_p[ph, b, 0] = r.part[b, slot(1 - x, 1 - c)].astype(BF)
-        far.start()
+        rs_copy(ph, b, 0).start()
         r.send_p[ph, b, 1] = r.part[b, slot(x, 1 - c)].astype(BF)
-        near.start()
+        rs_copy(ph, b, 1).start()
 
     def rs_mid(ph, b):
-        far, near, over = rs_copies(ph, b)
-        far.wait_recv()
+        rs_copy(ph, b, 0).wait_recv()
         r.send_x[ph, b] = (r.part[b, slot(1 - x, c)] + r.recv_p[ph, b, 0].astype(F32)).astype(BF)
-        over.start()
+        rs_copy(ph, b, 2).start()
 
     def rs_end(ph, b):
-        far, near, over = rs_copies(ph, b)
-        near.wait_recv()
-        over.wait_recv()
-        far.wait_send()
-        near.wait_send()
-        over.wait_send()
+        rs_copy(ph, b, 1).wait_recv()
+        rs_copy(ph, b, 2).wait_recv()
+        for i in range(3):
+            rs_copy(ph, b, i).wait_send()
         return r.part[b, me] + r.recv_p[ph, b, 1].astype(F32) + r.recv_x[ph, b].astype(F32)
 
     h = r.hid[...]
@@ -692,10 +742,8 @@
         bias = r.tv[3, 6:7, cols(x)]
         r.cv[rows, cols(x)] = (mm(r.feat[rows], r.wc[2176:3584, cols(x)]) + bias).astype(BF)
     ag_mid(0, 1)
-    for k in (1, 2, 3):
-        view = part_f((z - k) % 4, y)
-        arrived(view, r.gz_r.at[2, k])
-        go(sent_w[2], view, view, r.gy_s.at[2, k], r.gy_r.at[2, k], yn)
+    gather_z(3)
+    gather_z(4)
     gather_x(1)
     gather_core(1, range(8, 15))
     far_cols = cols(1 - x)
@@ -722,8 +770,10 @@
     ag_start(0, 0)
 
     loc_f.wait()
-    for j in range(4):
-        arrived(part_f((z - j) % 4, 1 - y), r.gy_r.at[2, j])
+    gather_z(5, last=True)
+    other_arrivals()
+    for g in (2, 3, 4):
+        gather_y(g)
 
     def ffn_forward_part(b):
         rows = r.xg[0, b].reshape(256, D)
@@ -763,15 +813,60 @@
         r.wf[2 * b] = mm_tn(rows, r.dpre[b]).astype(BF)
         r.wf[2 * b + 1] = mm_tn(r.act[b], up).astype(BF)
         for p in (2 * b, 2 * b + 1):
-            go(sent, part_f(p, 1 - y), r.yf.at[p], r.yy_s.at[2, p], r.yy_r.at[2, p], yn)
+            go(sent, part_f(p, 1 - y, 0, SPLIT), r.yf.at[p], r.yy_s.at[2, p], r.yy_r.at[2, p], yn)
+        for p in (2 * b, 2 * b + 1):
+            for i, yy in ((4, 1 - y), (3, y)):
+                z_out_sum(i, part_f(p, yy, SPLIT, REST), p)
+
+    hop = jnp.where(z < 2, 1, 2)
+
+    def z_out_sum(i, src, p):
+        zb, zr = getattr(r, f"zb{i}"), getattr(r, f"zr{i}")
+        d = (p - z) % 4
+        far = {0: z == 3, 3: z == 0}.get(p)
+        later = {0: z == 2, 3: z == 1}.get(p)
+        direct = z != p
+        if far is not None:
+            go(sent, src, zr, r.zq_s.at[i], r.zq_r.at[i], device(x, hop, y, c), far)
+            direct = jnp.logical_and(direct, jnp.logical_not(jnp.logical_or(far, later)))
+        go(sent, src, zb.at[d - 1], r.zz_s.at[i, p], r.zz_r.at[i, d], device(x, p, y, c), direct)
+
+    def z_add_sum(i, src, p):
+        later = {0: z == 2, 3: z == 1}.get(p)
+        if later is None:
+            return
+        zb, zr, zq = (getattr(r, f"{n}{i}") for n in ("zb", "zr", "zq"))
+
+        @pl.when(later)
+        def _():
+            arrived(zr, r.zq_r.at[i])
+            zq[...] = add(zr[...], src[...])
+
+        go(sent, zq, zb.at[1], r.zz_s.at[i, p], r.zz_r.at[i, 2], device(x, p, y, c), later)
+
+    def z_total(i, own, out):
+        zb = getattr(r, f"zb{i}")
+        arrived(zb.at[1], r.zz_r.at[i, 2])
+        out[...] = add(own, zb[1])
+        for d, without in ((1, 0), (3, 3)):
+
+            @pl.when(z != without)
+            def _():
+                arrived(zb.at[d - 1], r.zz_r.at[i, d])
+                out[...] = add(out[...], zb[d - 1])
 
     def ffn_sum_y(p):
         arrived(r.yf.at[p], r.yy_r.at[2, p])
-        r.yf[p] = add(r.yf[p], part_f(p, y)[...])
-
-        @pl.when(z != p)
-        def _():
-            remote(r.yf.at[p], r.zf.at[z], r.zz_s.at[2, p], r.zz_r.at[2, z], device(x, p, y, c)).start()
+        r.yf[p] = add(r.yf[p], part_f(p, y, 0, SPLIT)[...])
+        z_out_sum(2, r.yf.at[p], p)
+
+    def ffn_add(p):
+        for i, yy in ((4, 1 - y), (3, y)):
+            z_add_sum(i, part_f(p, yy, SPLIT, REST), p)
+
+    def ffn_sum_other():
+        z_total(4, part_f(z, 1 - y, SPLIT, REST)[...], r.of)
+        go(sent, r.of, r.yf2, r.yy_s.at[3, 0], r.yy_r.at[3, 0], yn)
 
     ag_end(0, 1)
     ffn_forward_part(1)
@@ -805,10 +900,10 @@
     d_second = r.dsum3[0] + rs_end(1, 0)
 
     groups = (
-        (shard_s, r.core_s, r.xs, r.ys, r.zs, r.fin_s, r.out_s),
-        (shard_c, r.core_c, r.xc, r.yc, r.zc, r.fin_c, r.out_c),
-    )
-    order = (1, 2, 3, 0)
+        (shard_s, r.core_s, r.xs, r.ys, r.fin_s, r.out_s),
+        (shard_c, r.core_c, r.xc, r.yc, r.fin_c, r.out_c),
+    )
+    order = (3, 1, 2, 0)
 
     def sum_start(g):
         view, cb = groups[g][:2]
@@ -836,55 +931,60 @@
                 go(sent, xb.at[0, zz], yb.at[zz], r.yy_s.at[g, d], r.yy_r.at[g, d], yn)
 
     def sum_y(g):
-        view, cb, xb, yb, zb = groups[g][:5]
+        view, cb, xb, yb = groups[g][:4]
+        zb, zr, zq = (getattr(r, f"{n}{g}") for n in ("zb", "zr", "zq"))
         for d in order:
             zz = (z + d) % 4
             arrived(yb.at[zz], r.yy_r.at[g, d])
             yb[zz] = add(yb[zz], xb[1, zz])
-            if d:
-                go(sent, yb.at[zz], zb.at[d - 1], r.zz_s.at[g, d - 1], r.zz_r.at[g, d - 1], device(x, zz, y, c))
+            if d == 2:
+
+                @pl.when(inner)
+                def _():
+                    arrived(zr, r.zq_r.at[g])
+                    zq[...] = add(zr[...], yb[zz])
+
+                go(sent, zq, zb.at[1], r.zz_s.at[g, 2], r.zz_r.at[g, 2], zdev(2), inner)
+                go(sent, yb.at[zz], zb.at[1], r.zz_s.at[g, 2], r.zz_r.at[g, 2], zdev(2), outer)
+            elif d:
+                far = z == (0 if d == 3 else 3)
+                go(sent, yb.at[zz], zr, r.zq_s.at[g], r.zq_r.at[g], device(x, hop, y, c), far)
+                go(sent, yb.at[zz], zb.at[d - 1], r.zz_s.at[g, d], r.zz_r.at[g, d], zdev(d), jnp.logical_not(far))
 
     def sum_z(g):
-        view, cb, xb, yb, zb, fin, out = groups[g]
-        for k in range(3):
-            arrived(zb.at[k], r.zz_r.at[g, k])
-        total = yb[z].astype(F32)
-        for k in range(3):
-            total = total + zb[k].astype(F32)
-        fin[...] = total.astype(BF)
+        view, cb, xb, yb, fin, out = groups[g]
+        z_total(g, yb[z], fin)
         out[:, cols(x)] = fin[...]
         go(sent, fin, out.at[:, cols(x)], r.fi_s.at[g], r.fi_r.at[g], xn)
 
     def ffn_sum_z():
-        total = r.yf[z].astype(F32)
-        for k in (1, 2, 3):
-            zz = (z + k) % 4
-            arrived(r.zf.at[zz], r.zz_r.at[2, zz])
-            total = total + r.zf[zz].astype(F32)
-        r.fin_f[...] = total.astype(BF).reshape(2, 192, D)
-
-        def both(copies):
-            for copy in copies:
-                copy.start()
-            for copy in copies:
-                copy.wait()
+        z_total(2, r.yf[z], r.fin_f.at[0:SPLIT])
+        last = r.fin_f.at[SPLIT:384]
+        z_total(3, part_f(z, y, SPLIT, REST)[...], last)
+        arrived(r.yf2, r.yy_r.at[3, 0])
+        last[...] = add(last[...], r.yf2[...])
+        half = lambda j: r.fin_f.at[pl.ds(pl.multiple_of(192 * j, 192), 192)]
 
         @pl.when(w1)
         def _():
-            r.out_f[me] = r.fin_f[c]
-            both([
-                remote(r.fin_f.at[c], r.out_f.at[me], r.fi_s.at[2], r.fi_r.at[2], xn),
-                remote(r.fin_f.at[1 - c], r.out_f.at[me], r.fi_s.at[3], r.fi_r.at[3], core),
-                remote(r.fin_f.at[1 - c], r.out_f.at[me], r.fi_s.at[4], r.fi_r.at[4], diag),
-            ])
+            r.out_f[me] = half(c)[...]
+            remote(half(c), r.out_f.at[me], r.fi_s.at[2], r.fi_r.at[2], xn).start()
+            remote(half(1 - c), r.out_f.at[me], r.fi_s.at[3], r.fi_r.at[3], core).start()
+            remote(half(1 - c), r.out_f.at[me], r.fi_s.at[4], r.fi_r.at[4], diag).start()
 
         @pl.when(jnp.logical_not(w1))
         def _():
-            copies = []
             for j in range(2):
-                r.out_f[2 * x + j] = r.fin_f[j]
-                copies.append(remote(r.fin_f.at[j], r.out_f.at[2 * x + j], r.fi_s.at[2 + j], r.fi_r.at[2 + j], xn))
-            both(copies)
+                r.out_f[2 * x + j] = half(j)[...]
+                remote(half(j), r.out_f.at[2 * x + j], r.fi_s.at[2 + j], r.fi_r.at[2 + j], xn).start()
+
+    def ffn_end():
+        def ends(n):
+            for j in range(n):
+                remote(r.fin_f.at[0:192], r.out_f.at[0], r.fi_s.at[2 + j], r.fi_r.at[2 + j], xn).wait()
+
+        pl.when(w1)(lambda: ends(3))
+        pl.when(jnp.logical_not(w1))(lambda: ends(2))
 
     du2, dgain, dshift = norm_back(r.sum2[...], cross_v(3), d_second)
     r.vg[3, 8:9] = dgain
@@ -920,6 +1020,7 @@
         r.wc[768 + 128 * j : 896 + 128 * j] = mm_tn(block, r.dck[...]).astype(BF)
         r.wc[2176 + 128 * j : 2304 + 128 * j] = mm_tn(block, r.dcv[...]).astype(BF)
     sum_start(1)
+    ffn_add(3)
     ffn_sum_y(2)
     ffn_sum_y(3)
 
@@ -959,8 +1060,11 @@
     def _():
         remote(r.v_send, r.v_in.at[index], r.vv_s.at[0], r.vv_r.at[index], home).start()
 
+    ffn_add(0)
     ffn_sum_y(0)
     ffn_sum_y(1)
+    z_add_sum(2, r.yf.at[0], 0)
+    z_add_sum(2, r.yf.at[3], 3)
     sum_x(1, 0)
     sum_core(0)
 
@@ -976,6 +1080,7 @@
             remote(r.v_z.at[zz], r.v_zin.at[k - 1], r.vv_s.at[k], r.vv_r.at[2 + k], device(x, zz, y, c)).start()
 
     sum_x(1, 1)
+    ffn_sum_other()
     sum_y(1)
     ffn_sum_z()
     sum_x(0, 0)
@@ -1009,13 +1114,8 @@
         remote(r.v_send, r.v_in.at[index], r.vv_s.at[0], r.vv_r.at[index], home).wait_send()
 
     for g in range(2):
-        arrived(groups[g][6].at[:, cols(1 - x)], r.fi_r.at[g])
-    for p in range(4):
-
-        @pl.when(z != p)
-        def _():
-            remote(r.yf.at[p], r.zf.at[z], r.zz_s.at[2, p], r.zz_r.at[2, z], device(x, p, y, c)).wait_send()
-
+        arrived(groups[g][5].at[:, cols(1 - x)], r.fi_r.at[g])
+    ffn_end()
     drain(sent)
 
 

time: 347 us -> 282 us (0.81)
  Pallas kernels: 295 us -> 234 us
  starting transfers between devices: 4.65 us -> 0.88 us
    pallas_call x1, Pallas kernels: 295 us -> 234 us  [layer(): pl.pallas_call(layer_kernel, out_shape=(jax.ShapeDtypeStruct((128, D), BF...]
    ppermute x1, starting transfers between devices: 4.14 us -> 0.37 us  [flat_grads(): lax.ppermute(heads, 'fsdp', [(i, (i + 15) % 16) for i in range(16)])]
where the time goes in v3:
time: 282 us; the launch traced here: 277 us
  Pallas kernels  234 us (83%)
  local copies, waits for them, and re-layouts  27 us (10%)
  other arithmetic  13.9 us (5%)
    pallas_call x1, Pallas kernels, layer(): pl.pallas_call(layer_kernel, out_shape=(jax.ShapeDtypeStruct((128, D), BF...  234 us
  transfers between devices with their start and end apart: 2, of which 0 were waited for; matrix products, arithmetic and copies ran while one was open for 4% of the time, Pallas kernels for 0%

profile of v3, /device:TPU:0, one launch (start us, length us, event | category | flops | bytes accessed | tf_op | source)
XLA Modules:
  0.0 277.3 jit_solution(14660648160292712180)
XLA Ops:
  0.6 0.7 slice_bitcast_fusion.2
  1.3 0.7 slice_bitcast_fusion
  2.6 0.8 fusion.21
  3.4 0.8 fusion.20
  4.1 0.7 slice.144
  8.0 1.5 copy.18
  9.5 1.2 pad.10.clone
  12.5 1.9 reshape.216
  15.7 1.1 reshape.213.refs_1_
  17.0 1.0 reshape.211.refs_0_
  18.0 0.9 maximum_select_fusion.refs_2_
  18.9 234.2 %shard_map.110 = (bf16[128,768]{1,0:T(8,128)(2,1)}, bf16[128,768]{1,0:T(8,128)(2,1)}, bf16[192,768]{1,0:T(8,128)(2,1)}, bf16[272,768]{1,0:T(8,128)(2,1)}, bf16[4...) custom-call(bf16[192,768]{1,0:T(8,128)(2,1)} %reshape.211.refs_0_, bf16[272,768]{1,0:T(8,128)(2,1)} %reshape.213.refs_1_, ...), custom_call_target="tpu_custom_call" | custom-call | tf_op jit(solution)/shard_map/pallas_call | solution.py:1125
  253.1 2.4 reshape.229
  255.6 1.9 reshape.231
  258.0 2.1 reshape.230
  260.1 1.6 fusion.19
  262.1 1.4 reshape.226
  265.7 1.1 convert_element_type.20
  266.8 0.9 convert_element_type.18
  267.7 0.7 reshape.237
  269.8 0.7 convert_element_type.19
  270.6 2.5 fusion.1
  273.1 1.3 fusion.4
  274.4 1.1 fusion.6
  (78 shorter events, 12.8 us)
Async XLA Ops:
  2.1 8.7 %collective-permute-start = (bf16[96,128]{1,0:T(8,128)(2,1)S(1)}, bf16[96,128]{1,0:T(8,128)(2,1)S(1)}, u32[]{:S(2)}, u32[]{:S(2)}) collective-permute-start(bf16[96,128]{1,0:T(8,128)(2,1)S(1)} %pad_maximum_fusion), channel_id=1, source_target_pairs={{0,1},{1,2},{2,3},{3,4},{4,5},{5,6},{6,7},{7,8},{8,9},{9,10},{10,1... | collective-permute-start | bytes 73736 | tf_op jit(solution)/shard_map/ppermute | solution.py:1154
  9.5 1.8 copy-start.4
  14.4 1.0 copy-start.5
  15.0 1.9 copy-start.7
  15.7 2.3 copy-start.1
  253.1 2.5 copy-start
  260.1 1.6 copy-start.6
  261.7 2.8 %copy-start.10 = (f32[16,768]{1,0:T(8,128)S(1)}, f32[16,768]{1,0:T(8,128)}, u32[]{:S(2)}) copy-start(f32[16,768]{1,0:T(8,128)} %get-tuple-element.14) | copy-start | bytes 147460
  262.1 3.6 %copy-start.3 = (bf16[1632,128]{1,0:T(8,128)(2,1)}, bf16[1632,128]{1,0:T(8,128)(2,1)S(1)}, u32[]{:S(2)}) copy-start(bf16[1632,128]{1,0:T(8,128)(2,1)S(1)} %reshape.228) | copy-start | bytes 1253380
  264.1 4.4 %collective-permute-start.1 = (bf16[96,128]{1,0:T(8,128)(2,1)}, bf16[96,128]{1,0:T(8,128)(2,1)}, u32[]{:S(2)}, u32[]{:S(2)}) collective-permute-start(bf16[96,128]{1,0:T(8,128)(2,1)} %pad_maximum_fusion.1), channel_id=1, source_target_pairs={{0,15},{1,0},{2,1},{3,2},{4,3},{5,4},{6,5},{7,6},{8,7},{9,8},{10,9... | collective-permute-start | bytes 73736 | tf_op jit(solution)/shard_map/ppermute | solution.py:1187
  265.7 2.7 copy-start.12
  265.7 2.7 copy-start.11
  273.1 1.3 copy-start.2
  273.1 2.4 copy-start.9
  274.4 1.8 copy-start.8

commit v4 on v3

--- a/solution.py
+++ b/solution.py
@@ -443,7 +443,7 @@
     b = lambda *s: pltpu.VMEM(s, BF)
     f = lambda *s: pltpu.VMEM(s, F32)
     return dict(
-        ws=b(4, D, D), wc=b(4352, D), wf=b(4, D, D), block_f=b(384, D), tb=b(4, 16, D),
+        ws=b(4, D, D), wc=b(4352, D), wf=b(4, D, D), theirs=b(192, D), own_t=b(16, D), tb=b(4, 16, D), before=b(96, 128),
         tv=f(4, 16, D), vg=f(4, 16, D),
         q=b(128, D), k=b(128, D), v=b(128, D), a=b(128, D), p=f(2, 3, 256, 64),
         sum1=f(128, D), first=f(128, D), cq=b(64, D), ck=b(544, D), cv=b(544, D), ca=b(64, D),
@@ -451,13 +451,14 @@
         xg=b(2, 2, 4, 64, D), pre=f(2, 256, D), act=b(2, 256, D), part=f(2, 4, 64, D),
         send_p=b(2, 2, 2, 64, D), recv_p=b(2, 2, 2, 64, D), send_x=b(2, 2, 64, D), recv_x=b(2, 2, 64, D),
         sum3=f(2, 64, D), dpre=b(2, 256, D), dsum3=f(2, 64, D), dfirst=f(128, D),
-        dq=b(128, D), dk=b(128, D), dv=b(128, D), dck=b(544, D), dcv=b(544, D),
         core_s=b(2, 4, 192, D), core_c=b(2, 4, 272, D), xs=b(2, 4, 192, 384), xc=b(2, 4, 272, 384),
         ys=b(4, 192, 384), yc=b(4, 272, 384), yf=b(4, SPLIT, D), yf2=b(REST, D), of=b(REST, D),
         fin_s=b(192, 384), fin_c=b(272, 384), fin_f=b(384, D),
-        **{f"{n}{i}": b(*lead, *shape) for i, shape in enumerate(STREAMS) for n, lead in (("zb", (3,)), ("zr", ()), ("zq", ()))},
+        **{f"{n}{i}": b(*lead, *shape) for i, shape in enumerate(STREAMS) for n, lead in (("zb", (3,)), ("zr", ()))},
         v_send=b(4, 16, D), v_in=b(3, 4, 16, D), v_z=b(4, 16, D), v_zin=b(3, 16, D), v_x=b(16, D), v_xin=b(16, D),
-        loc=dma(4), gz_s=dma(7, 4), gz_r=dma(7, 4), gy_s=dma(7, 4), gy_r=dma(7, 4), gx_s=dma(2, 7), gx_r=dma(2, 7),
+        nice_s=b(192, D), nice_c=b(272, D), nice_f=b(4, 192, D), total_v=b(16, D), heads=b(3, 32, 128), after=b(3, 32, 128),
+        fl_s=f(1184, 128), fl_c=f(1664, 128), fl_f=f(4640, 128),
+        loc=dma(1), out_sem=dma(3), tail_s=dma(1), tail_r=dma(1), head_s=dma(3), head_r=dma(3), gz_s=dma(7, 4), gz_r=dma(7, 4), gy_s=dma(7, 4), gy_r=dma(7, 4), gx_s=dma(2, 7), gx_r=dma(2, 7),
         gc_s=dma(3, 15), gc_r=dma(3, 15), t_s=dma(6), t_r=dma(4),
         ex_s=dma(2, 2, 3), ex_r=dma(2, 2, 3), rs_s=dma(2, 2, 3), rs_r=dma(2, 2, 3),
         co_s=dma(2, 2, 4), co_r=dma(2, 2, 4), xx_s=dma(2, 2, 4), xx_r=dma(2, 2, 4), yy_s=dma(4, 4), yy_r=dma(4, 4),
@@ -467,15 +468,17 @@
 
 def layer_kernel(*refs):
     names = [
-        "own_s", "own_c", "own_f", "own_t", "hid", "allowed", "feat", "cot",
-        "mixed", "hgrad", "out_s", "out_c", "out_f", "out_v",
+        "flat_s", "flat_c", "flat_f", "tails", "lens", "hid", "feat", "cot",
+        "mixed", "hgrad", "out_s", "out_c", "out_f",
     ] + list(scratch())
     r = SimpleNamespace(**dict(zip(names, refs)))
     x, z, y, c = place()
     core, xn, yn = device(x, z, y, 1 - c), device(1 - x, z, y, c), device(x, z, 1 - y, c)
     diag = device(1 - x, z, y, 1 - c)
     zdev = lambda d: device(x, (z + d) % 4, y, c)
-    meet([core, xn, yn, diag, device(x, z, 1 - y, 1 - c), zdev(1), zdev(2), zdev(3)])
+    f = lax.axis_index("fsdp")
+    following, preceding = (x, (f + 1) % 16), (x, (f + 15) % 16)
+    meet([core, xn, yn, diag, device(x, z, 1 - y, 1 - c), zdev(1), zdev(2), zdev(3), following, preceding])
     me = 2 * c + x
     cols = lambda h: pl.ds(pl.multiple_of(384 * h, 384), 384)
     root = jnp.logical_and(y == 1, c == 1)
@@ -522,9 +525,7 @@
         return view if h is None else view.at[:, cols(h)]
 
     def own_part(g):
-        if g >= 2:
-            return r.block_f.at[pl.ds(96 * (g - 2), 96)]
-        return (r.own_s, r.own_c)[g].at[:, cols(x)]
+        return part(g, z, y, c, x)
 
     def z_out(src, dst, g, i):
         for k in (2, 1, 3):
@@ -542,11 +543,8 @@
         go(sent_w[min(g, 2)], own_part(g), part(g, z, y, c, x), r.gy_s.at[g, 0], r.gy_r.at[g, 0], yn)
 
     def own_core(g):
-        own = (r.own_s, r.own_c)[g]
-        go(sent_w[g], own, part(g, z, y, c, None), r.gc_s.at[g, 0], r.gc_r.at[g, 0], core)
-        copy = pltpu.make_async_copy(own, part(g, z, y, c, None), r.loc.at[g])
-        copy.start()
-        return copy
+        own = part(g, z, y, c, None)
+        go(sent_w[g], own, own, r.gc_s.at[g, 0], r.gc_r.at[g, 0], core)
 
     def gather_z(g, last=False):
         for k in steps:
@@ -598,13 +596,65 @@
                 view = part(g, (z - j + 11) % 4, 1 - y, 1 - c, 1 - x)
             arrived(view, r.gc_r.at[g, j])
 
+    tail = remote(r.tails, r.before, r.tail_s.at[0], r.tail_r.at[0], following)
+    tail.start()
+    back = (2 * f, 2 * f, 6 * (f % 4) + jnp.where(z >= 2, 6, 0))
+
+    def one_hot(shape, pick):
+        row = lax.broadcasted_iota(jnp.int32, shape, 0)
+        col = lax.broadcasted_iota(jnp.int32, shape, 1)
+        return jnp.where(col == pick(row), 1.0, 0.0).astype(BF)
+
+    def to_rows(g):
+        return one_hot((96, 128), lambda i: 32 - back[g] + 6 * (i % 16) + i // 16)
+
+    def store_rows(dst, row, tiles, n=6):
+        for j in range(n):
+            dst[pl.ds(pl.multiple_of(row, 16), 16), 128 * j : 128 * j + 128] = tiles[16 * j : 16 * j + 16]
+
+    def first_window(g, flat, n):
+        return jnp.concatenate([r.before[32 * g : 32 * g + 32], flat[0:n]], 0)
+
+    def lay_rows(g, flat, dst, n):
+        perm = to_rows(g)
+
+        def body(i, carry):
+            window = flat[pl.ds(pl.multiple_of(96 * i - 32, 32), 128)]
+            store_rows(dst, 16 * i, mm(perm, window).astype(BF))
+            return carry
+
+        lax.fori_loop(1, n, body, 0)
+        return perm
+
+    tail_v = one_hot(
+        (96, 96),
+        lambda i: jnp.where(
+            i % 16 < 5,
+            6 * (i % 16) + i // 16,
+            jnp.where(
+                i % 16 < 10,
+                32 + 6 * (i % 16 - 5) + i // 16,
+                jnp.where(z < 2, 72, 66)
+                + jnp.where(
+                    z % 2 == 0,
+                    12 * (i // 48) + 3 * (i % 16 - 10) + (i // 16) % 3,
+                    6 * (i % 16 - 10) + i // 16,
+                ),
+            ),
+        ),
+    )
+    store_rows(r.own_t, 0, mm(tail_v, r.tails[...]).astype(BF))
+    mine_s, mine_c = part(0, z, y, c, None), part(1, z, y, c, None)
+    perm = lay_rows(0, r.flat_s, mine_s, 12)
+    tail.wait_recv()
+    store_rows(mine_s, 0, mm(perm, first_window(0, r.flat_s, 96)).astype(BF))
     own_z(0)
     own_y(0)
-    loc_s = own_core(0)
+    own_core(0)
 
     @pl.when(root)
     def _():
-        mine = pltpu.make_async_copy(r.own_t, r.tb.at[z], r.loc.at[3])
+        mine = pltpu.make_async_copy(r.own_t, r.tb.at[z], r.loc.at[0])
         mine.start()
         out = []
         for k in (1, 2, 3):
@@ -616,29 +666,54 @@
             go(out, r.tb, r.tb, r.t_s.at[3 + i], r.t_r.at[0], device(x, z, yy, cc))
         drain(out)
 
+    perm = lay_rows(1, r.flat_c, mine_c, 17)
+    store_rows(mine_c, 0, mm(perm, first_window(1, r.flat_c, 96)).astype(BF))
     own_z(1)
     own_y(1)
-    loc_c = own_core(1)
-    fb = pl.ds(pl.multiple_of(192 * c, 192), 192)
+    own_core(1)
 
     @pl.when(w1)
     def _():
-        copy = remote(r.own_f.at[1], r.block_f.at[fb], r.gc_s.at[2, 0], r.gc_r.at[2, 0], core)
-        copy.start()
-        mine = pltpu.make_async_copy(r.own_f.at[0], r.block_f.at[fb], r.loc.at[2])
-        mine.start()
-        mine.wait()
-        copy.wait()
+        def pick(i):
+            m, j = i % 16, i // 16
+            q = 2 * jnp.where(j < 6, c, 1 - c) + x
+            j = j % 6
+            return 32 - back[2] + 24 * m + 12 * (j // 3) + 3 * q + j % 3
+
+        perm = one_hot((192, 416), pick)
+        mine = part_f(z, y, 192 * c, 192)
+
+        def put(i, window):
+            tiles = mm(perm, window).astype(BF)
+            store_rows(r.theirs, 16 * i, tiles[96:192])
+            store_rows(mine, 16 * i, tiles[0:96])
+
+        def body(i, carry):
+            put(i, r.flat_f[pl.ds(pl.multiple_of(384 * i - 32, 32), 416)])
+            return carry
+
+        put(0, first_window(2, r.flat_f, 384))
+        lax.fori_loop(1, 12, body, 0)
+        swap = remote(r.theirs, mine, r.gc_s.at[2, 0], r.gc_r.at[2, 0], core)
+        swap.start()
+        swap.wait()
 
     @pl.when(jnp.logical_not(w1))
     def _():
-        for j in range(2):
-            mine = pltpu.make_async_copy(r.own_f.at[j], r.block_f.at[pl.ds(192 * j, 192)], r.loc.at[2])
-            mine.start()
-            mine.wait()
-
-    loc_f = pltpu.make_async_copy(r.block_f, part_f(z, y), r.loc.at[2])
-    loc_f.start()
+        perm = to_rows(2)
+        mine = part_f(z, y)
+
+        def body(i, carry):
+            window = r.flat_f[pl.ds(pl.multiple_of(2304 * x + 96 * i - 32, 32), 128)]
+            store_rows(mine, 16 * i, mm(perm, window).astype(BF))
+            return carry
+
+        lax.fori_loop(1, 24, body, 0)
+        lead = jnp.where(x == 0, r.before[64:96], r.flat_f[2304 - 32 : 2304])
+        rest = r.flat_f[pl.ds(pl.multiple_of(2304 * x, 32), 96)]
+        store_rows(mine, 0, mm(perm, jnp.concatenate([lead, rest], 0)).astype(BF))
+
+    tail.wait_send()
     r.vg[...] = jnp.zeros_like(r.vg)
 
     own_y(5)
@@ -656,7 +731,6 @@
     gather_z(2)
     gather_x(0)
     gather_y(1, (1, 2, 3))
-    loc_s.wait()
 
     @pl.when(jnp.logical_not(root))
     def _():
@@ -722,7 +796,10 @@
     r.v[...] = (mm(h, r.ws[2]) + self_v(1)).astype(BF)
     for i in range(2):
         rows = slice(64 * i, 64 * i + 64)
-        ok = jnp.concatenate([r.allowed[i]] * 4, 0)
+        at = lax.broadcasted_iota(jnp.int32, (256, 64), 0) % 64
+        key = lax.broadcasted_iota(jnp.int32, (256, 64), 1)
+        caption = jnp.where(at >= NQ, 1.0, 0.0) * jnp.where(key <= at, 1.0, 0.0)
+        ok = jnp.where(key < NQ, 1.0, caption * jnp.where(key < NQ + r.lens[i], 1.0, 0.0))
         for g in range(3):
             lanes = slice(256 * g, 256 * g + 256)
             p, a = attend_block(r.q[rows, lanes], r.k[rows, lanes], r.v[rows, lanes], ok)
@@ -734,13 +811,15 @@
     r.xg[0, 1, me] = rows_of(r.first, 32).astype(BF)
     ag_start(0, 1)
 
-    loc_c.wait()
+    for i in range(2):
+        r.ck[272 * i + 256 : 272 * i + 272] = jnp.zeros((16, D), BF)
+        r.cv[272 * i + 256 : 272 * i + 272] = jnp.zeros((16, D), BF)
     gather_core(1, range(8))
     for i in range(2):
-        rows = slice(272 * i, 272 * i + 272)
-        r.ck[rows, cols(x)] = mm(r.feat[rows], r.wc[768:2176, cols(x)]).astype(BF)
+        rows = slice(272 * i, 272 * i + 257)
+        r.ck[rows, cols(x)] = mm(r.feat[i], r.wc[768:2176, cols(x)]).astype(BF)
         bias = r.tv[3, 6:7, cols(x)]
-        r.cv[rows, cols(x)] = (mm(r.feat[rows], r.wc[2176:3584, cols(x)]) + bias).astype(BF)
+        r.cv[rows, cols(x)] = (mm(r.feat[i], r.wc[2176:3584, cols(x)]) + bias).astype(BF)
     ag_mid(0, 1)
     gather_z(3)
     gather_z(4)
@@ -748,10 +827,10 @@
     gather_core(1, range(8, 15))
     far_cols = cols(1 - x)
     for i in range(2):
-        rows = slice(272 * i, 272 * i + 272)
-        r.ck[rows, far_cols] = mm(r.feat[rows], r.wc[768:2176, far_cols]).astype(BF)
+        rows = slice(272 * i, 272 * i + 257)
+        r.ck[rows, far_cols] = mm(r.feat[i], r.wc[768:2176, far_cols]).astype(BF)
         bias = r.tv[3, 6:7, far_cols]
-        r.cv[rows, far_cols] = (mm(r.feat[rows], r.wc[2176:3584, far_cols]) + bias).astype(BF)
+        r.cv[rows, far_cols] = (mm(r.feat[i], r.wc[2176:3584, far_cols]) + bias).astype(BF)
     u = rows_of(r.first, 0)
     r.cq[...] = (mm(u.astype(BF), r.wc[0:768]) + cross_v(0)).astype(BF)
     ok = jnp.where(lax.broadcasted_iota(jnp.int32, (128, 272), 1) < 257, 1.0, 0.0)
@@ -769,7 +848,6 @@
     r.xg[0, 0, me] = r.second[...].astype(BF)
     ag_start(0, 0)
 
-    loc_f.wait()
     gather_z(5, last=True)
     other_arrivals()
     for g in (2, 3, 4):
@@ -835,14 +913,14 @@
         later = {0: z == 2, 3: z == 1}.get(p)
         if later is None:
             return
-        zb, zr, zq = (getattr(r, f"{n}{i}") for n in ("zb", "zr", "zq"))
+        zb, zr = getattr(r, f"zb{i}"), getattr(r, f"zr{i}")
 
         @pl.when(later)
         def _():
             arrived(zr, r.zq_r.at[i])
-            zq[...] = add(zr[...], src[...])
-
-        go(sent, zq, zb.at[1], r.zz_s.at[i, p], r.zz_r.at[i, 2], device(x, p, y, c), later)
+            zr[...] = add(zr[...], src[...])
+
+        go(sent, zr, zb.at[1], r.zz_s.at[i, p], r.zz_r.at[i, 2], device(x, p, y, c), later)
 
     def z_total(i, own, out):
         zb = getattr(r, f"zb{i}")
@@ -900,8 +978,8 @@
     d_second = r.dsum3[0] + rs_end(1, 0)
 
     groups = (
-        (shard_s, r.core_s, r.xs, r.ys, r.fin_s, r.out_s),
-        (shard_c, r.core_c, r.xc, r.yc, r.fin_c, r.out_c),
+        (shard_s, r.core_s, r.xs, r.ys, r.fin_s, r.nice_s),
+        (shard_c, r.core_c, r.xc, r.yc, r.fin_c, r.nice_c),
     )
     order = (3, 1, 2, 0)
 
@@ -932,7 +1010,7 @@
 
     def sum_y(g):
         view, cb, xb, yb = groups[g][:4]
-        zb, zr, zq = (getattr(r, f"{n}{g}") for n in ("zb", "zr", "zq"))
+        zb, zr = getattr(r, f"zb{g}"), getattr(r, f"zr{g}")
         for d in order:
             zz = (z + d) % 4
             arrived(yb.at[zz], r.yy_r.at[g, d])
@@ -942,9 +1020,9 @@
                 @pl.when(inner)
                 def _():
                     arrived(zr, r.zq_r.at[g])
-                    zq[...] = add(zr[...], yb[zz])
-
-                go(sent, zq, zb.at[1], r.zz_s.at[g, 2], r.zz_r.at[g, 2], zdev(2), inner)
+                    zr[...] = add(zr[...], yb[zz])
+
+                go(sent, zr, zb.at[1], r.zz_s.at[g, 2], r.zz_r.at[g, 2], zdev(2), inner)
                 go(sent, yb.at[zz], zb.at[1], r.zz_s.at[g, 2], r.zz_r.at[g, 2], zdev(2), outer)
             elif d:
                 far = z == (0 if d == 3 else 3)
@@ -967,21 +1045,21 @@
 
         @pl.when(w1)
         def _():
-            r.out_f[me] = half(c)[...]
-            remote(half(c), r.out_f.at[me], r.fi_s.at[2], r.fi_r.at[2], xn).start()
-            remote(half(1 - c), r.out_f.at[me], r.fi_s.at[3], r.fi_r.at[3], core).start()
-            remote(half(1 - c), r.out_f.at[me], r.fi_s.at[4], r.fi_r.at[4], diag).start()
+            r.nice_f[me] = half(c)[...]
+            remote(half(c), r.nice_f.at[me], r.fi_s.at[2], r.fi_r.at[2], xn).start()
+            remote(half(1 - c), r.nice_f.at[me], r.fi_s.at[3], r.fi_r.at[3], core).start()
+            remote(half(1 - c), r.nice_f.at[me], r.fi_s.at[4], r.fi_r.at[4], diag).start()
 
         @pl.when(jnp.logical_not(w1))
         def _():
             for j in range(2):
-                r.out_f[2 * x + j] = half(j)[...]
-                remote(half(j), r.out_f.at[2 * x + j], r.fi_s.at[2 + j], r.fi_r.at[2 + j], xn).start()
+                r.nice_f[2 * x + j] = half(j)[...]
+                remote(half(j), r.nice_f.at[2 * x + j], r.fi_s.at[2 + j], r.fi_r.at[2 + j], xn).start()
 
     def ffn_end():
         def ends(n):
             for j in range(n):
-                remote(r.fin_f.at[0:192], r.out_f.at[0], r.fi_s.at[2 + j], r.fi_r.at[2 + j], xn).wait()
+                remote(r.fin_f.at[0:192], r.nice_f.at[0], r.fi_s.at[2 + j], r.fi_r.at[2 + j], xn).wait()
 
         pl.when(w1)(lambda: ends(3))
         pl.when(jnp.logical_not(w1))(lambda: ends(2))
@@ -1005,20 +1083,21 @@
                 r.cq[mine, lanes], r.ck[rows, lanes], r.cv[rows, lanes], r.pc[i, g], dca[mine, lanes]
             )
             blocks.append(dq)
-            r.dck[rows, lanes] = dk
-            r.dcv[rows, lanes] = dv
+            r.ck[rows, lanes] = dk
+            r.cv[rows, lanes] = dv
         dcq.append(jnp.concatenate(blocks, 1))
     dcq = jnp.concatenate(dcq, 0)
     r.vg[3, 5:6] = rows_sum(dcq)
-    r.vg[3, 6:7] = rows_sum(r.dcv[...])
+    r.vg[3, 6:7] = rows_sum(r.cv[...])
     du = du2 + mm_nt(dcq, r.wc[0:768])
     for i in range(2):
         r.dfirst[64 * i : 64 * i + 32] = du[32 * i : 32 * i + 32]
     r.wc[0:768] = mm_tn(rows_of(r.first, 0).astype(BF), dcq).astype(BF)
     for j in range(11):
-        block = r.feat[:, 128 * j : 128 * j + 128]
-        r.wc[768 + 128 * j : 896 + 128 * j] = mm_tn(block, r.dck[...]).astype(BF)
-        r.wc[2176 + 128 * j : 2304 + 128 * j] = mm_tn(block, r.dcv[...]).astype(BF)
+        block = [r.feat[i, :, 128 * j : 128 * j + 128] for i in range(2)]
+        both = lambda d: mm_tn(block[0], d[0:257]) + mm_tn(block[1], d[272:529])
+        r.wc[768 + 128 * j : 896 + 128 * j] = both(r.ck).astype(BF)
+        r.wc[2176 + 128 * j : 2304 + 128 * j] = both(r.cv).astype(BF)
     sum_start(1)
     ffn_add(3)
     ffn_sum_y(2)
@@ -1039,17 +1118,17 @@
             dq, dk, dv = attend_block_back(
                 r.q[rows, lanes], r.k[rows, lanes], r.v[rows, lanes], r.p[i, g], da[rows, lanes]
             )
-            r.dq[rows, lanes] = dq
-            r.dk[rows, lanes] = dk
-            r.dv[rows, lanes] = dv
+            r.q[rows, lanes] = dq
+            r.k[rows, lanes] = dk
+            r.v[rows, lanes] = dv
     sum_core(1)
-    r.vg[3, 0:1] = rows_sum(r.dq[...])
-    r.vg[3, 1:2] = rows_sum(r.dv[...])
-    total = dsum1 + mm_nt(r.dq[...], r.ws[0]) + mm_nt(r.dk[...], r.ws[1]) + mm_nt(r.dv[...], r.ws[2])
+    r.vg[3, 0:1] = rows_sum(r.q[...])
+    r.vg[3, 1:2] = rows_sum(r.v[...])
+    total = dsum1 + mm_nt(r.q[...], r.ws[0]) + mm_nt(r.k[...], r.ws[1]) + mm_nt(r.v[...], r.ws[2])
     r.hgrad[...] = total.astype(BF)
-    r.ws[0] = mm_tn(r.hid[...], r.dq[...]).astype(BF)
-    r.ws[1] = mm_tn(r.hid[...], r.dk[...]).astype(BF)
-    r.ws[2] = mm_tn(r.hid[...], r.dv[...]).astype(BF)
+    r.ws[0] = mm_tn(r.hid[...], r.q[...]).astype(BF)
+    r.ws[1] = mm_tn(r.hid[...], r.k[...]).astype(BF)
+    r.ws[2] = mm_tn(r.hid[...], r.v[...]).astype(BF)
     sum_start(0)
 
     r.v_send[...] = r.vg[...].astype(BF)
@@ -1102,7 +1181,7 @@
     @pl.when(root)
     def _():
         arrived(r.v_xin, r.vv_r.at[6])
-        r.out_v[...] = r.v_x[...].astype(F32) + r.v_xin[...].astype(F32)
+        r.total_v[...] = add(r.v_x[...], r.v_xin[...])
         for k in (1, 2, 3):
             zz = (z + k) % 4
             remote(r.v_z.at[zz], r.v_zin.at[k - 1], r.vv_s.at[k], r.vv_r.at[2 + k], device(x, zz, y, c)).wait_send()
@@ -1110,112 +1189,128 @@
 
     @pl.when(jnp.logical_not(root))
     def _():
-        r.out_v[...] = jnp.zeros_like(r.out_v)
+        r.total_v[...] = jnp.zeros_like(r.total_v)
         remote(r.v_send, r.v_in.at[index], r.vv_s.at[0], r.vv_r.at[index], home).wait_send()
 
-    for g in range(2):
-        arrived(groups[g][5].at[:, cols(1 - x)], r.fi_r.at[g])
     ffn_end()
+
+    def stack(src, row, n=6):
+        return jnp.concatenate(
+            [src[pl.ds(pl.multiple_of(row, 16), 16), 128 * j : 128 * j + 128] for j in range(n)], 0
+        )
+
+    to_flat = one_hot((96, 96), lambda i: 16 * (i % 6) + i // 6)
+
+    def lay_flat(src, dst, n, base=0):
+        def body(i, carry):
+            dst[pl.ds(pl.multiple_of(base + 96 * i, 32), 96)] = mm(to_flat, stack(src, 16 * i))
+            return carry
+
+        lax.fori_loop(0, n, body, 0)
+
+    def head_out(g, fl):
+        r.heads[g] = fl[0:32].astype(BF)
+        go(sent, r.heads.at[g], r.after.at[g], r.head_s.at[g], r.head_r.at[g], preceding)
+
+    @pl.when(w1)
+    def _():
+        def pick(i):
+            m, t = i // 24, i % 24
+            return 96 * ((t % 12) // 3) + 16 * (3 * (t // 12) + t % 3) + m
+
+        perm = one_hot((384, 384), pick)
+
+        def body(i, carry):
+            tiles = jnp.concatenate([stack(r.nice_f.at[q], 16 * i) for q in range(4)], 0)
+            r.fl_f[pl.ds(pl.multiple_of(384 * i, 128), 384)] = mm(perm, tiles)
+            return carry
+
+        lax.fori_loop(0, 12, body, 0)
+
+    @pl.when(jnp.logical_not(w1))
+    def _():
+        for q in range(4):
+            lay_flat(r.nice_f.at[q], r.fl_f, 12, 1152 * q)
+
+    head_out(2, r.fl_f)
+    arrived(groups[1][5].at[:, cols(1 - x)], r.fi_r.at[1])
+    lay_flat(r.nice_c, r.fl_c, 17)
+    head_out(1, r.fl_c)
+    arrived(groups[0][5].at[:, cols(1 - x)], r.fi_r.at[0])
+    lay_flat(r.nice_s, r.fl_s, 12)
+    head_out(0, r.fl_s)
+
+    vectors = stack(r.total_v, 0)
+    end = (f == 15, f == 15, f % 4 == 3)
+    plain = lambda first: lambda i: 16 * (i % 6) + first + i // 6
+    hidden = lambda i: 16 * (3 * (i // 12) + i % 3) + 10 + (i % 12) // 3
+    none = -1
+    count = jnp.where(w1, 24, 18)
+
+    def from_vectors(g):
+        if g < 2:
+            return lambda i: jnp.where(jnp.logical_and(end[g], i < 30), plain(5 * g)(i), none)
+        pick = lambda i: jnp.where(w1, hidden(i), plain(10)(i))
+        return lambda i: jnp.where(jnp.logical_and(end[2], i < count), pick(i), none)
+
+    def from_next(g):
+        if g < 2:
+            return lambda i: jnp.where(end[g], none, i)
+        inside = jnp.logical_or(z == 1, z == 2)
+        return lambda i: jnp.where(
+            end[2], jnp.where(jnp.logical_and(inside, i >= count), i - count, none), i
+        )
+
+    ends = ((r.fl_s, r.out_s, 1152, 1154), (r.fl_c, r.out_c, 1632, 1634), (r.fl_f, r.out_f, 4608, 4614))
+    copies = []
+    for g in (2, 1, 0):
+        fl, out, rows, size = ends[g]
+        arrived(r.after.at[g], r.head_r.at[g])
+        fl[rows : rows + 32] = mm(one_hot((32, 96), from_vectors(g)), vectors) + mm(
+            one_hot((32, 32), from_next(g)), r.after[g]
+        )
+
+        def body(i, carry):
+            fl[pl.ds(pl.multiple_of(128 * i, 128), 128)] = fl[pl.ds(back[g] + 128 * i, 128)]
+            return carry
+
+        lax.fori_loop(0, size // 128, body, 0)
+        done = size // 128 * 128
+        fl[done:size] = fl[pl.ds(back[g] + done, size - done)]
+        copy = pltpu.make_async_copy(fl.at[0:size], out, r.out_sem.at[g])
+        copy.start()
+        copies.append(copy)
+    for copy in copies:
+        copy.wait()
+
     drain(sent)
 
 
-def layer(own_s, own_c, own_f, own_t, hid, allowed, feat, cot):
+def layer(flat_s, flat_c, flat_f, tails, lens, hid, feat, cot):
     vm = pl.BlockSpec(memory_space=pltpu.VMEM)
-    anywhere = pl.BlockSpec(memory_space=pl.ANY)
     return pl.pallas_call(
         layer_kernel,
         out_shape=(
             jax.ShapeDtypeStruct((128, D), BF),
             jax.ShapeDtypeStruct((128, D), BF),
-            jax.ShapeDtypeStruct((192, D), BF),
-            jax.ShapeDtypeStruct((272, D), BF),
-            jax.ShapeDtypeStruct((4, 192, D), BF),
-            jax.ShapeDtypeStruct((16, D), F32),
+            *[jax.ShapeDtypeStruct((v.shape[0], 128), F32) for v in (flat_s, flat_c, flat_f)],
         ),
-        in_specs=[anywhere] * 4 + [vm] * 4,
-        out_specs=[vm] * 6,
+        in_specs=[vm] * 4 + [pl.BlockSpec(memory_space=pltpu.SMEM)] + [vm] * 3,
+        out_specs=[vm] * 2 + [pl.BlockSpec(memory_space=pl.ANY)] * 3,
         scratch_shapes=list(scratch().values()),
         compiler_params=pltpu.CompilerParams(
             collective_id=0, has_side_effects=True, vmem_limit_bytes=VMEM_BYTES
         ),
-    )(own_s, own_c, own_f, own_t, hid, allowed, feat, cot)
-
-
-def shift_back():
-    x, z, y, c = place()
-    f = lax.axis_index("fsdp")
-    return 2 * f, 2 * f, 6 * (f % 4) + jnp.where(z >= 2, 6, 0)
-
-
-def own_rows(self_params, cross_params, ffn_params):
-    x, z, y, c = place()
+    )(flat_s, flat_c, flat_f, tails, lens, hid, feat, cot)
+
+
+def per_device_fast(hidden, lengths, features, cotangent, self_params, cross_params, ffn_params):
     flats = [v.reshape(-1, 128) for v in (self_params, cross_params, ffn_params)]
     tails = jnp.concatenate([v[-32:] for v in flats])
-    before = lax.ppermute(tails, "fsdp", [(i, (i + 1) % 16) for i in range(16)])
-    nice = []
-    for i, (v, rows, back) in enumerate(zip(flats, (1152, 1632, 4608), shift_back())):
-        both = jnp.concatenate([before[32 * i : 32 * i + 32], v])
-        nice.append(lax.dynamic_slice_in_dim(both, 32 - back, rows))
-    own_s = nice[0].reshape(192, D)
-    own_c = nice[1].reshape(272, D)
-    cols = nice[2].reshape(192, 2, 4, 3, 128)
-    pick = lambda cc: lax.dynamic_index_in_dim(cols, 2 * cc + x, 2, keepdims=False).reshape(192, D)
-    as_w1 = jnp.stack([pick(c), pick(1 - c)])
-    as_w2 = lax.dynamic_index_in_dim(nice[2].reshape(2, 2, 192, D), x, keepdims=False)
-    own_f = jnp.where(z % 2 == 0, as_w1, as_w2)
-
-    b1 = lambda v: v.reshape(2, 4, 384).transpose(1, 0, 2).reshape(4, D)
-    rest = lambda v: jnp.concatenate([v.reshape(3, D), jnp.zeros((1, D), BF)])
-    ffn = jnp.stack([b1(tails[72:96]), rest(tails[72:90]), b1(tails[66:90]), rest(tails[66:84])])
-    own_t = jnp.concatenate([
-        tails[0:30].reshape(5, D),
-        tails[32:62].reshape(5, D),
-        lax.dynamic_index_in_dim(ffn, z, keepdims=False),
-        jnp.zeros((2, D), BF),
-    ])
-    return own_s, own_c, own_f, own_t
-
-
-def flat_grads(out_s, out_c, out_f, out_v):
-    x, z, y, c = place()
-    f = lax.axis_index("fsdp")
-    k = f % 4
-    w1 = out_f.reshape(4, 192, 2, 3, 128).transpose(1, 2, 0, 3, 4).reshape(4608, 128)
-    w2 = out_f.reshape(4608, 128)
-    nice = [out_s.reshape(1152, 128), out_c.reshape(1632, 128), jnp.where(z % 2 == 0, w1, w2)]
-    heads = jnp.concatenate([v[:32] for v in nice])
-    after = lax.ppermute(heads, "fsdp", [(i, (i + 15) % 16) for i in range(16)]).astype(F32)
-    zeros = lambda n: jnp.zeros((n, 128), F32)
-    flat = lambda v: v.reshape(-1, 128)
-    tail_s = jnp.where(f == 15, jnp.concatenate([flat(out_v[0:5]), zeros(2)]), after[0:32])
-    tail_c = jnp.where(f == 15, jnp.concatenate([flat(out_v[5:10]), zeros(2)]), after[32:64])
-    nxt = after[64:96]
-    b1 = out_v[10:14].reshape(4, 2, 384).transpose(1, 0, 2).reshape(24, 128)
-    rest = flat(out_v[10:13])
-    ends = jnp.stack([
-        jnp.concatenate([b1, zeros(8)]),
-        jnp.concatenate([rest, nxt[:14]]),
-        jnp.concatenate([b1, nxt[:8]]),
-        jnp.concatenate([rest, zeros(14)]),
-    ])
-    tail_f = jnp.where(k == 3, lax.dynamic_index_in_dim(ends, z, keepdims=False), nxt)
-    outs = []
-    for v, tail, start, rows in zip(nice, (tail_s, tail_c, tail_f), shift_back(), (1154, 1634, 4614)):
-        both = jnp.concatenate([v.astype(F32), tail])
-        outs.append(lax.dynamic_slice_in_dim(both, start, rows).reshape(-1))
-    return outs
-
-
-def per_device_fast(hidden, lengths, features, cotangent, self_params, cross_params, ffn_params):
-    own = own_rows(self_params, cross_params, ffn_params)
-    at = jnp.arange(64)
-    r, k = at[:, None], at[None, :]
-    allowed = (k < NQ)[None] | ((r >= NQ) & (k <= r))[None] & (k[None] < NQ + lengths[:, None, None])
-    feat = jnp.pad(features, ((0, 0), (0, 15), (0, 0))).reshape(544, E)
-    mixed, hgrad, *sums = layer(
-        *own, hidden.reshape(128, D), allowed.astype(F32), feat, cotangent.reshape(128, D)
-    )
-    return (mixed.reshape(2, 64, D), hgrad.reshape(2, 64, D), *flat_grads(*sums))
+    mixed, hgrad, *grads = layer(
+        *flats, tails, lengths, hidden.reshape(128, D), features, cotangent.reshape(128, D)
+    )
+    return (mixed.reshape(2, 64, D), hgrad.reshape(2, 64, D), *[v.reshape(-1) for v in grads])
 
 
 def solution(mesh):

time: 282 us -> 257 us (0.911); the launches traced: 277 us -> 256 us
  local copies, waits for them, and re-layouts: 27 us -> 12 us
  other arithmetic: 13.9 us -> 0.61 us
  Pallas kernels: 234 us -> 243 us
    reshape x18 -> x0, local copies, waits for them, and re-layouts: 13.6 us -> none  [the longest x2 4.57 us: flat_grads(): out_f.reshape(4, 192, 2, 3, 128).transpose(1, 2, 0, 3, 4).reshape(4608, 128)]
    pallas_call x1, Pallas kernels: 234 us -> 243 us  [layer(): pl.pallas_call(layer_kernel, out_shape=(jax.ShapeDtypeStruct((128, D), BF...]
    unnamed x29 -> x10, local copies, waits for them, and re-layouts: 3.66 us -> 10.5 us
    slice x17 -> x2, local copies, waits for them, and re-layouts: 7.02 us -> 1.44 us  [per_device_fast(): tails = jnp.concatenate([v[-32:] for v in flats])]
    reshape x3 -> x0, other arithmetic: 4.87 us -> none  [flat_grads(): outs.append(lax.dynamic_slice_in_dim(both, start, rows).reshape(-1))]
    convert_element_type x5 -> x0, other arithmetic: 4.86 us -> none  [the longest x3 3.48 us: flat_grads(): both = jnp.concatenate([v.astype(F32), tail])]
  transfers between devices with their start and end apart: 2 -> 0, of which waited for: 0 -> 0; matrix products, arithmetic and copies ran while one was open for 4% -> 0% of each run, Pallas kernels for 0% -> 0%
where the time goes in v4:
time: 257 us; the launch traced here: 256 us
  Pallas kernels  243 us (95%)
  local copies, waits for them, and re-layouts  12 us (5%)
    pallas_call x1, Pallas kernels, layer(): pl.pallas_call(layer_kernel, out_shape=(jax.ShapeDtypeStruct((128, D), BF...  243 us
    unnamed x10, local copies, waits for them, and re-layouts  10.5 us

profile of v4, /device:TPU:0, one launch (start us, length us, event | category | flops | bytes accessed | tf_op | source)
XLA Modules:
  0.0 255.9 jit_solution(7517651472297011325)
XLA Ops:
  0.6 0.7 slice_bitcast_fusion.2
  1.3 0.7 slice_bitcast_fusion
  2.1 0.6 pad_maximum_fusion.refs_3_
  2.7 2.6 %copy.12.refs_6_ = bf16[2,257,1408]{2,1,0:T(8,128)(2,1)} copy(bf16[2,257,1408]{2,0,1:T(2,128)(2,1)} %param.9) | data formatting | bytes 2894848 | tf_op args[2]
  5.3 242.7 %shard_map.110 = (bf16[128,768]{1,0:T(8,128)(2,1)}, bf16[128,768]{1,0:T(8,128)(2,1)}, f32[1154,128]{1,0:T(8,128)}, f32[1634,128]{1,0:T(8,128)}, f32[4614,128]{1,0:T(8,128)}) custom-call(bf16[1154,128]{1,0:T(8,128)(2,1)} %bitcast.21, bf16[1634,128]{1,0:T(8,128)(2,1)} %bitcast.20, bf16[4614,128]{1,0:T(8,128)(2,1)} %bitcast.17, ...), custom_call_target="tpu_custom_call" | custom-call | tf_op jit(solution)/shard_map/pallas_call | solution.py:1291
  248.0 0.0 copy-start.1
  248.0 1.7 copy.18
  249.7 1.6 copy.19
  251.3 0.0 copy-start
  251.3 2.1 copy.20
  253.4 0.0 copy-done.1
  253.4 1.0 copy.21
  254.4 0.0 copy-done
  254.4 1.6 copy.22
Async XLA Ops:
  248.0 5.4 %copy-start.1 = (f32[1634,128]{1,0:T(8,128)S(1)}, f32[1634,128]{1,0:T(8,128)}, u32[]{:S(2)}) copy-start(f32[1634,128]{1,0:T(8,128)} %get-tuple-element.13) | copy-start | bytes 2509828
  251.3 3.0 %copy-start = (f32[4614,128]{1,0:T(8,128)S(1)}, f32[4614,128]{1,0:T(8,128)}, u32[]{:S(2)}) copy-start(f32[4614,128]{1,0:T(8,128)} %get-tuple-element.14) | copy-start | bytes 7087108

commit v5 on v4

--- a/solution.py
+++ b/solution.py
@@ -329,6 +329,11 @@
     return (x, (z * 2 + y) * 2 + c)
 
 
+def shift_back():
+    f = lax.axis_index("fsdp")
+    return 2 * f, 2 * f, 6 * (f % 4) + jnp.where(f >= 8, 6, 0)
+
+
 def meet(devices):
     barrier = pltpu.get_barrier_semaphore()
     for d in devices:
@@ -433,8 +438,11 @@
     return jnp.concatenate([ref[first : first + 32], ref[64 + first : 96 + first]], 0)
 
 
-SPLIT = 288
+SPLIT = 240
 REST = 384 - SPLIT
+X_FIRST = (False, True)
+SIDE = tuple((2, 4) if first else (4,) for first in X_FIRST)
+WIDTH = tuple(384 if first else 768 for first in X_FIRST)
 STREAMS = ((192, 384), (272, 384), (SPLIT, D), (REST, D), (REST, D))
 
 
@@ -451,14 +459,13 @@
         xg=b(2, 2, 4, 64, D), pre=f(2, 256, D), act=b(2, 256, D), part=f(2, 4, 64, D),
         send_p=b(2, 2, 2, 64, D), recv_p=b(2, 2, 2, 64, D), send_x=b(2, 2, 64, D), recv_x=b(2, 2, 64, D),
         sum3=f(2, 64, D), dpre=b(2, 256, D), dsum3=f(2, 64, D), dfirst=f(128, D),
-        core_s=b(2, 4, 192, D), core_c=b(2, 4, 272, D), xs=b(2, 4, 192, 384), xc=b(2, 4, 272, 384),
-        ys=b(4, 192, 384), yc=b(4, 272, 384), yf=b(4, SPLIT, D), yf2=b(REST, D), of=b(REST, D),
+        core_s=b(2, 4, 192, D), core_c=b(2, 4, 272, D), xs=b(*SIDE[0], 192, 384), xc=b(*SIDE[1], 272, 384),
+        ys=b(4, 192, WIDTH[0]), yc=b(4, 272, WIDTH[1]), yf=b(4, SPLIT, D), yf2=b(REST, D), of=b(REST, D),
         fin_s=b(192, 384), fin_c=b(272, 384), fin_f=b(384, D),
         **{f"{n}{i}": b(*lead, *shape) for i, shape in enumerate(STREAMS) for n, lead in (("zb", (3,)), ("zr", ()))},
         v_send=b(4, 16, D), v_in=b(3, 4, 16, D), v_z=b(4, 16, D), v_zin=b(3, 16, D), v_x=b(16, D), v_xin=b(16, D),
         nice_s=b(192, D), nice_c=b(272, D), nice_f=b(4, 192, D), total_v=b(16, D), heads=b(3, 32, 128), after=b(3, 32, 128),
-        fl_s=f(1184, 128), fl_c=f(1664, 128), fl_f=f(4640, 128),
-        loc=dma(1), out_sem=dma(3), tail_s=dma(1), tail_r=dma(1), head_s=dma(3), head_r=dma(3), gz_s=dma(7, 4), gz_r=dma(7, 4), gy_s=dma(7, 4), gy_r=dma(7, 4), gx_s=dma(2, 7), gx_r=dma(2, 7),
+        loc=dma(1), tail_s=dma(1), tail_r=dma(1), head_s=dma(3), head_r=dma(3), gz_s=dma(7, 4), gz_r=dma(7, 4), gy_s=dma(7, 4), gy_r=dma(7, 4), gx_s=dma(2, 7), gx_r=dma(2, 7),
         gc_s=dma(3, 15), gc_r=dma(3, 15), t_s=dma(6), t_r=dma(4),
         ex_s=dma(2, 2, 3), ex_r=dma(2, 2, 3), rs_s=dma(2, 2, 3), rs_r=dma(2, 2, 3),
         co_s=dma(2, 2, 4), co_r=dma(2, 2, 4), xx_s=dma(2, 2, 4), xx_r=dma(2, 2, 4), yy_s=dma(4, 4), yy_r=dma(4, 4),
@@ -598,7 +605,7 @@
 
     tail = remote(r.tails, r.before, r.tail_s.at[0], r.tail_r.at[0], following)
     tail.start()
-    back = (2 * f, 2 * f, 6 * (f % 4) + jnp.where(z >= 2, 6, 0))
+    back = shift_back()
 
     def one_hot(shape, pick):
         row = lax.broadcasted_iota(jnp.int32, shape, 0)
@@ -728,10 +735,7 @@
     own_z(5)
     other_z()
     gather_y(1, (0,))
-    gather_z(2)
     gather_x(0)
-    gather_y(1, (1, 2, 3))
-
     @pl.when(jnp.logical_not(root))
     def _():
         arrived(r.tb, r.t_r.at[0])
@@ -810,6 +814,9 @@
     r.first[...] = xh * self_v(3) + self_v(4)
     r.xg[0, 1, me] = rows_of(r.first, 32).astype(BF)
     ag_start(0, 1)
+    gather_z(2)
+    gather_y(1, (1, 2, 3))
+    gather_z(3)
 
     for i in range(2):
         r.ck[272 * i + 256 : 272 * i + 272] = jnp.zeros((16, D), BF)
@@ -821,7 +828,6 @@
         bias = r.tv[3, 6:7, cols(x)]
         r.cv[rows, cols(x)] = (mm(r.feat[i], r.wc[2176:3584, cols(x)]) + bias).astype(BF)
     ag_mid(0, 1)
-    gather_z(3)
     gather_z(4)
     gather_x(1)
     gather_core(1, range(8, 15))
@@ -842,13 +848,14 @@
             p, a = attend_block(r.cq[mine, lanes], r.ck[rows, lanes], r.cv[rows, lanes], ok)
             r.pc[i, g] = p
             r.ca[mine, lanes] = a
+        if i == 0:
+            gather_z(5, last=True)
     r.sum2[...] = u + (mm(r.ca[...], r.wc[3584:4352]) + cross_v(2))
     xh, _ = normed(r.sum2[...])
     r.second[...] = xh * cross_v(3) + cross_v(4)
     r.xg[0, 0, me] = r.second[...].astype(BF)
     ag_start(0, 0)
 
-    gather_z(5, last=True)
     other_arrivals()
     for g in (2, 3, 4):
         gather_y(g)
@@ -990,48 +997,65 @@
                 zz = (z + d) % 4
                 go(sent, view(zz, y if far else 1 - y, 1 - c), cb.at[far, zz], r.co_s.at[g, far, d], r.co_r.at[g, far, d], core)
 
-    def sum_core(g):
-        view, cb, xb = groups[g][:3]
-        for far in range(2):
+    def sum_core(g, fars=(0, 1)):
+        view, cb, xb, yb = groups[g][:4]
+        for far in fars:
             for d in order:
                 zz = (z + d) % 4
                 arrived(cb.at[far, zz], r.co_r.at[g, far, d])
                 cb[far, zz] = add(cb[far, zz], view(zz, y if far else 1 - y, c)[...])
-                go(sent, cb.at[far, zz, :, cols(1 - x)], xb.at[far, zz], r.xx_s.at[g, far, d], r.xx_r.at[g, far, d], xn)
-
-    def sum_x(g, far):
+                if X_FIRST[g]:
+                    go(sent, cb.at[far, zz, :, cols(1 - x)], xb.at[far, zz], r.xx_s.at[g, far, d], r.xx_r.at[g, far, d], xn)
+                elif far == 0:
+                    go(sent, cb.at[0, zz], yb.at[zz], r.yy_s.at[g, d], r.yy_r.at[g, d], yn)
+
+    def sum_mid(g, fars=(0, 1)):
+        view, cb, xb, yb = groups[g][:4]
+        for far in fars if X_FIRST[g] else (0,):
+            for d in order:
+                zz = (z + d) % 4
+                if X_FIRST[g]:
+                    arrived(xb.at[far, zz], r.xx_r.at[g, far, d])
+                    xb[far, zz] = add(xb[far, zz], cb[far, zz, :, cols(x)])
+                    if far == 0:
+                        go(sent, xb.at[0, zz], yb.at[zz], r.yy_s.at[g, d], r.yy_r.at[g, d], yn)
+                else:
+                    arrived(yb.at[zz], r.yy_r.at[g, d])
+                    yb[zz] = add(yb[zz], cb[1, zz])
+                    go(sent, yb.at[zz, :, cols(1 - x)], xb.at[zz], r.xx_s.at[g, 0, d], r.xx_r.at[g, 0, d], xn)
+
+    def to_z(g, mine, d):
+        zb, zr = getattr(r, f"zb{g}"), getattr(r, f"zr{g}")
+        if d == 2:
+
+            @pl.when(inner)
+            def _():
+                arrived(zr, r.zq_r.at[g])
+                zr[...] = add(zr[...], mine[...])
+
+            go(sent, zr, zb.at[1], r.zz_s.at[g, 2], r.zz_r.at[g, 2], zdev(2), inner)
+            go(sent, mine, zb.at[1], r.zz_s.at[g, 2], r.zz_r.at[g, 2], zdev(2), outer)
+        elif d:
+            far = z == (0 if d == 3 else 3)
+            go(sent, mine, zr, r.zq_s.at[g], r.zq_r.at[g], device(x, hop, y, c), far)
+            go(sent, mine, zb.at[d - 1], r.zz_s.at[g, d], r.zz_r.at[g, d], zdev(d), jnp.logical_not(far))
+
+    def sum_last(g):
         view, cb, xb, yb = groups[g][:4]
         for d in order:
             zz = (z + d) % 4
-            arrived(xb.at[far, zz], r.xx_r.at[g, far, d])
-            xb[far, zz] = add(xb[far, zz], cb[far, zz, :, cols(x)])
-            if far == 0:
-                go(sent, xb.at[0, zz], yb.at[zz], r.yy_s.at[g, d], r.yy_r.at[g, d], yn)
-
-    def sum_y(g):
-        view, cb, xb, yb = groups[g][:4]
-        zb, zr = getattr(r, f"zb{g}"), getattr(r, f"zr{g}")
-        for d in order:
-            zz = (z + d) % 4
-            arrived(yb.at[zz], r.yy_r.at[g, d])
-            yb[zz] = add(yb[zz], xb[1, zz])
-            if d == 2:
-
-                @pl.when(inner)
-                def _():
-                    arrived(zr, r.zq_r.at[g])
-                    zr[...] = add(zr[...], yb[zz])
-
-                go(sent, zr, zb.at[1], r.zz_s.at[g, 2], r.zz_r.at[g, 2], zdev(2), inner)
-                go(sent, yb.at[zz], zb.at[1], r.zz_s.at[g, 2], r.zz_r.at[g, 2], zdev(2), outer)
-            elif d:
-                far = z == (0 if d == 3 else 3)
-                go(sent, yb.at[zz], zr, r.zq_s.at[g], r.zq_r.at[g], device(x, hop, y, c), far)
-                go(sent, yb.at[zz], zb.at[d - 1], r.zz_s.at[g, d], r.zz_r.at[g, d], zdev(d), jnp.logical_not(far))
+            if X_FIRST[g]:
+                arrived(yb.at[zz], r.yy_r.at[g, d])
+                yb[zz] = add(yb[zz], xb[1, zz])
+                to_z(g, yb.at[zz], d)
+            else:
+                arrived(xb.at[zz], r.xx_r.at[g, 0, d])
+                xb[zz] = add(xb[zz], yb[zz, :, cols(x)])
+                to_z(g, xb.at[zz], d)
 
     def sum_z(g):
         view, cb, xb, yb, fin, out = groups[g]
-        z_total(g, yb[z], fin)
+        z_total(g, yb[z] if X_FIRST[g] else xb[z], fin)
         out[:, cols(x)] = fin[...]
         go(sent, fin, out.at[:, cols(x)], r.fi_s.at[g], r.fi_r.at[g], xn)
 
@@ -1121,7 +1145,7 @@
             r.q[rows, lanes] = dq
             r.k[rows, lanes] = dk
             r.v[rows, lanes] = dv
-    sum_core(1)
+    sum_core(1, (0,))
     r.vg[3, 0:1] = rows_sum(r.q[...])
     r.vg[3, 1:2] = rows_sum(r.v[...])
     total = dsum1 + mm_nt(r.q[...], r.ws[0]) + mm_nt(r.k[...], r.ws[1]) + mm_nt(r.v[...], r.ws[2])
@@ -1130,6 +1154,8 @@
     r.ws[1] = mm_tn(r.hid[...], r.k[...]).astype(BF)
     r.ws[2] = mm_tn(r.hid[...], r.v[...]).astype(BF)
     sum_start(0)
+    sum_core(1, (1,))
+    sum_core(0)
 
     r.v_send[...] = r.vg[...].astype(BF)
     index = 2 * y + c
@@ -1144,8 +1170,7 @@
     ffn_sum_y(1)
     z_add_sum(2, r.yf.at[0], 0)
     z_add_sum(2, r.yf.at[3], 3)
-    sum_x(1, 0)
-    sum_core(0)
+    sum_mid(1, (0,))
 
     @pl.when(root)
     def _():
@@ -1158,12 +1183,10 @@
             zz = (z + k) % 4
             remote(r.v_z.at[zz], r.v_zin.at[k - 1], r.vv_s.at[k], r.vv_r.at[2 + k], device(x, zz, y, c)).start()
 
-    sum_x(1, 1)
+    sum_mid(0)
+    sum_mid(1, (1,))
     ffn_sum_other()
-    sum_y(1)
-    ffn_sum_z()
-    sum_x(0, 0)
-    sum_x(0, 1)
+    sum_last(1)
 
     @pl.when(root)
     def _():
@@ -1174,7 +1197,8 @@
         r.v_x[...] = total.astype(BF)
         remote(r.v_x, r.v_xin, r.vv_s.at[4], r.vv_r.at[6], xn).start()
 
-    sum_y(0)
+    ffn_sum_z()
+    sum_last(0)
     sum_z(1)
     sum_z(0)
 
@@ -1203,13 +1227,13 @@
 
     def lay_flat(src, dst, n, base=0):
         def body(i, carry):
-            dst[pl.ds(pl.multiple_of(base + 96 * i, 32), 96)] = mm(to_flat, stack(src, 16 * i))
+            dst[pl.ds(pl.multiple_of(base + 96 * i, 32), 96)] = mm(to_flat, stack(src, 16 * i)).astype(BF)
             return carry
 
         lax.fori_loop(0, n, body, 0)
 
     def head_out(g, fl):
-        r.heads[g] = fl[0:32].astype(BF)
+        r.heads[g] = fl[0:32]
         go(sent, r.heads.at[g], r.after.at[g], r.head_s.at[g], r.head_r.at[g], preceding)
 
     @pl.when(w1)
@@ -1222,7 +1246,7 @@
 
         def body(i, carry):
             tiles = jnp.concatenate([stack(r.nice_f.at[q], 16 * i) for q in range(4)], 0)
-            r.fl_f[pl.ds(pl.multiple_of(384 * i, 128), 384)] = mm(perm, tiles)
+            r.out_f[pl.ds(pl.multiple_of(384 * i, 128), 384)] = mm(perm, tiles).astype(BF)
             return carry
 
         lax.fori_loop(0, 12, body, 0)
@@ -1230,15 +1254,15 @@
     @pl.when(jnp.logical_not(w1))
     def _():
         for q in range(4):
-            lay_flat(r.nice_f.at[q], r.fl_f, 12, 1152 * q)
-
-    head_out(2, r.fl_f)
+            lay_flat(r.nice_f.at[q], r.out_f, 12, 1152 * q)
+
+    head_out(2, r.out_f)
     arrived(groups[1][5].at[:, cols(1 - x)], r.fi_r.at[1])
-    lay_flat(r.nice_c, r.fl_c, 17)
-    head_out(1, r.fl_c)
+    lay_flat(r.nice_c, r.out_c, 17)
+    head_out(1, r.out_c)
     arrived(groups[0][5].at[:, cols(1 - x)], r.fi_r.at[0])
-    lay_flat(r.nice_s, r.fl_s, 12)
-    head_out(0, r.fl_s)
+    lay_flat(r.nice_s, r.out_s, 12)
+    head_out(0, r.out_s)
 
     vectors = stack(r.total_v, 0)
     end = (f == 15, f == 15, f % 4 == 3)
@@ -1261,27 +1285,10 @@
             end[2], jnp.where(jnp.logical_and(inside, i >= count), i - count, none), i
         )
 
-    ends = ((r.fl_s, r.out_s, 1152, 1154), (r.fl_c, r.out_c, 1632, 1634), (r.fl_f, r.out_f, 4608, 4614))
-    copies = []
-    for g in (2, 1, 0):
-        fl, out, rows, size = ends[g]
+    for g, (fl, rows) in enumerate(((r.out_s, 1152), (r.out_c, 1632), (r.out_f, 4608))):
         arrived(r.after.at[g], r.head_r.at[g])
-        fl[rows : rows + 32] = mm(one_hot((32, 96), from_vectors(g)), vectors) + mm(
-            one_hot((32, 32), from_next(g)), r.after[g]
-        )
-
-        def body(i, carry):
-            fl[pl.ds(pl.multiple_of(128 * i, 128), 128)] = fl[pl.ds(back[g] + 128 * i, 128)]
-            return carry
-
-        lax.fori_loop(0, size // 128, body, 0)
-        done = size // 128 * 128
-        fl[done:size] = fl[pl.ds(back[g] + done, size - done)]
-        copy = pltpu.make_async_copy(fl.at[0:size], out, r.out_sem.at[g])
-        copy.start()
-        copies.append(copy)
-    for copy in copies:
-        copy.wait()
+        tail = mm(one_hot((32, 96), from_vectors(g)), vectors) + mm(one_hot((32, 32), from_next(g)), r.after[g])
+        fl[rows : rows + 32] = tail.astype(BF)
 
     drain(sent)
 
@@ -1293,10 +1300,10 @@
         out_shape=(
             jax.ShapeDtypeStruct((128, D), BF),
             jax.ShapeDtypeStruct((128, D), BF),
-            *[jax.ShapeDtypeStruct((v.shape[0], 128), F32) for v in (flat_s, flat_c, flat_f)],
+            *[jax.ShapeDtypeStruct((n, 128), BF) for n in (1184, 1664, 4640)],
         ),
         in_specs=[vm] * 4 + [pl.BlockSpec(memory_space=pltpu.SMEM)] + [vm] * 3,
-        out_specs=[vm] * 2 + [pl.BlockSpec(memory_space=pl.ANY)] * 3,
+        out_specs=[vm] * 5,
         scratch_shapes=list(scratch().values()),
         compiler_params=pltpu.CompilerParams(
             collective_id=0, has_side_effects=True, vmem_limit_bytes=VMEM_BYTES
@@ -1310,7 +1317,11 @@
     mixed, hgrad, *grads = layer(
         *flats, tails, lengths, hidden.reshape(128, D), features, cotangent.reshape(128, D)
     )
-    return (mixed.reshape(2, 64, D), hgrad.reshape(2, 64, D), *[v.reshape(-1) for v in grads])
+    outs = [
+        lax.dynamic_slice_in_dim(rows, back, flat.shape[0]).astype(F32).reshape(-1)
+        for rows, back, flat in zip(grads, shift_back(), flats)
+    ]
+    return (mixed.reshape(2, 64, D), hgrad.reshape(2, 64, D), *outs)
 
 
 def solution(mesh):

time: 257 us -> 244 us (0.949)
  Pallas kernels: 243 us -> 229 us
  local copies, waits for them, and re-layouts: 12 us -> 5.44 us
  other arithmetic: 0.61 us -> 5.45 us
    pallas_call x1, Pallas kernels: 243 us -> 229 us  [layer(): pl.pallas_call(layer_kernel, out_shape=(jax.ShapeDtypeStruct((128, D), BF...]
    unnamed x10 -> x11, local copies, waits for them, and re-layouts: 10.5 us -> 4 us
    reshape x0 -> x3, other arithmetic: none -> 4.84 us  [per_device_fast(): lax.dynamic_slice_in_dim(rows, back, flat.shape[0]).astype(F32).reshape(-1)]
where the time goes in v5:
time: 244 us; the launch traced here: 241 us
  Pallas kernels  229 us (94%)
  other arithmetic  5.45 us (2%)
  local copies, waits for them, and re-layouts  5.44 us (2%)
    pallas_call x1, Pallas kernels, layer(): pl.pallas_call(layer_kernel, out_shape=(jax.ShapeDtypeStruct((128, D), BF...  229 us

profile of v5, /device:TPU:0, one launch (start us, length us, event | category | flops | bytes accessed | tf_op | source)
XLA Modules:
  0.0 241.0 jit_solution(7470852512113522281)
XLA Ops:
  0.7 0.7 slice_bitcast_fusion
  1.4 0.7 slice_bitcast_fusion.2
  2.1 0.6 pad_maximum_fusion.refs_3_
  2.7 2.6 %copy.12.refs_6_ = bf16[2,257,1408]{2,1,0:T(8,128)(2,1)} copy(bf16[2,257,1408]{2,0,1:T(2,128)(2,1)} %param.9) | data formatting | bytes 2894848 | tf_op args[2]
  5.3 229.5 %shard_map.110 = (bf16[128,768]{1,0:T(8,128)(2,1)}, bf16[128,768]{1,0:T(8,128)(2,1)}, bf16[1184,128]{1,0:T(8,128)(2,1)}, bf16[1664,128]{1,0:T(8,128)(2,1)}, bf16[4640,128]{1,0:T(8,128)(2,1)}) custom-call(bf16[1154,128]{1,0:T(8,128)(2,1)} %bitcast.24, bf16[1634,128]{1,0:T(8,128)(2,1)} %bitcast.23, bf16[4614,128]{1,0:T(8,128)(2,1)} %bitcast.22, ...), custom_call_target="tpu_custom_call" | custom-call | tf_op jit(solution)/shard_map/pallas_call | solution.py:1298
  234.8 0.0 copy-start
  234.8 3.0 %bitcast_convert_fusion = f32[590592]{0:T(1024)} fusion(bf16[4640,128]{1,0:T(8,128)(2,1)} %get-tuple-element.14, s32[]{:T(128)S(6)} %select_n.24), kind=kLoop, calls=%fused_computation | loop fusion | flops 590592 | bytes 3543556 | tf_op jit(solution)/shard_map/reshape | solution.py:1321
  237.8 0.0 copy-start.1
  237.8 0.0 copy-start.3
  237.8 0.0 copy-done
  237.8 0.0 copy-start.2
  237.8 1.0 bitcast_convert_fusion.1
  238.8 0.0 copy-done.1
  238.8 0.9 bitcast_convert_fusion.2
  239.7 0.0 copy-done.3
  239.7 0.7 copy.15
  240.4 0.0 copy-done.2
  240.4 0.7 copy.16
Async XLA Ops:
  234.8 3.0 %copy-start = (bf16[1664,128]{1,0:T(8,128)(2,1)S(1)}, bf16[1664,128]{1,0:T(8,128)(2,1)}, u32[]{:S(2)}) copy-start(bf16[1664,128]{1,0:T(8,128)(2,1)} %get-tuple-element.13) | copy-start | bytes 1277956
  237.8 1.0 copy-start.1
  237.8 1.9 copy-start.3
  237.8 2.6 %copy-start.2 = (bf16[128,768]{1,0:T(8,128)(2,1)S(1)}, bf16[128,768]{1,0:T(8,128)(2,1)}, u32[]{:S(2)}) copy-start(bf16[128,768]{1,0:T(8,128)(2,1)} %get-tuple-element.11) | copy-start | bytes 589828

commit v6 on v5

--- a/solution.py
+++ b/solution.py
@@ -522,7 +522,7 @@
         return r.wf.at[zz, pl.ds(pl.multiple_of(384 * yy + lo, 16), n)]
 
     shards = (shard_s, shard_c)
-    sent_w = ([], [], [])
+    sent_w, sent_f = ([], []), ([], [])
     steps = [jnp.where(z == 0, 3 - i, jnp.where(z == 3, 1 + i, (2, 1, 3)[i])) for i in range(3)]
 
     def part(g, zz, yy, cc, h):
@@ -534,54 +534,76 @@
     def own_part(g):
         return part(g, z, y, c, x)
 
-    def z_out(src, dst, g, i):
+    def both(a, b):
+        return a if b is None else b if a is None else jnp.logical_and(a, b)
+
+    branch = (z < 2, z >= 2)
+
+    def sent_of(g, b):
+        return sent_w[g] if g < 2 else sent_f[b]
+
+    def z_out(src, dst, g, i, b=None):
         for k in (2, 1, 3):
-            cond = {1: z != 3, 2: None, 3: z != 0}[k]
-            go(sent_w[min(g, 2)], src, dst, r.gz_s.at[i, k], r.gz_r.at[i, k], zdev(k), cond)
-
-    def z_on(view, g, i, k):
+            cond = both({1: z != 3, 2: None, 3: z != 0}[k], None if b is None else branch[b])
+            go(sent_of(g, b), src, dst, r.gz_s.at[i, k], r.gz_r.at[i, k], zdev(k), cond)
+
+    def z_on(view, g, k):
         cond = jnp.logical_and(inner, k == 2)
-        go(sent_w[min(g, 2)], view, view, r.gz_s.at[i, 0], r.gz_r.at[i, 2 * z - 1], device(x, 3 * (z - 1), y, c), cond)
-
-    def own_z(g):
-        z_out(own_part(g), part(g, z, y, c, x), g, g)
-
-    def own_y(g):
-        go(sent_w[min(g, 2)], own_part(g), part(g, z, y, c, x), r.gy_s.at[g, 0], r.gy_r.at[g, 0], yn)
+        go(sent_w[g], view, view, r.gz_s.at[g, 0], r.gz_r.at[g, 2 * z - 1], device(x, 3 * (z - 1), y, c), cond)
+
+    def own_z(g, b=None):
+        z_out(own_part(g), part(g, z, y, c, x), g, g, b)
+
+    def own_y(g, b=None):
+        cond = None if b is None else branch[b]
+        go(sent_of(g, b), own_part(g), part(g, z, y, c, x), r.gy_s.at[g, 0], r.gy_r.at[g, 0], yn, cond)
 
     def own_core(g):
         own = part(g, z, y, c, None)
         go(sent_w[g], own, own, r.gc_s.at[g, 0], r.gc_r.at[g, 0], core)
 
-    def gather_z(g, last=False):
-        for k in steps:
-            view = part(g, (z - k) % 4, y, c, x)
-            arrived(view, r.gz_r.at[g, k])
-            z_on(view, g, g, k)
-            if not last:
-                go(sent_w[min(g, 2)], view, view, r.gy_s.at[g, k], r.gy_r.at[g, k], yn)
-            if g < 2:
-                go(sent_w[g], view, view, r.gx_s.at[g, k - 1], r.gx_r.at[g, k - 1], xn)
-                go(sent_w[g], view, view, r.gc_s.at[g, k], r.gc_r.at[g, k], core)
-
-    def gather_y(g, which=(0, 1, 2, 3)):
-        for j in which:
-            view = part(g, (z - j) % 4, 1 - y, c, x)
-            arrived(view, r.gy_r.at[g, j])
-            if g < 2:
-                go(sent_w[g], view, view, r.gx_s.at[g, 3 + j], r.gx_r.at[g, 3 + j], xn)
-                go(sent_w[g], view, view, r.gc_s.at[g, 4 + j], r.gc_r.at[g, 4 + j], core)
-
-    def other_z():
+    def gather_z(g, i):
+        k = steps[i]
+        view = part(g, (z - k) % 4, y, c, x)
+        arrived(view, r.gz_r.at[g, k])
+        z_on(view, g, k)
+        go(sent_w[g], view, view, r.gy_s.at[g, k], r.gy_r.at[g, k], yn)
+        go(sent_w[g], view, view, r.gx_s.at[g, k - 1], r.gx_r.at[g, k - 1], xn)
+        go(sent_w[g], view, view, r.gc_s.at[g, k], r.gc_r.at[g, k], core)
+
+    def gather_y(g, j):
+        view = part(g, (z - j) % 4, 1 - y, c, x)
+        arrived(view, r.gy_r.at[g, j])
+        go(sent_w[g], view, view, r.gx_s.at[g, 3 + j], r.gx_r.at[g, 3 + j], xn)
+        go(sent_w[g], view, view, r.gc_s.at[g, 4 + j], r.gc_r.at[g, 4 + j], core)
+
+    def ffn_z(g, p, other=False):
+        i = 6 if other else g
+        view = part(g, p, 1 - y if other else y, c, x)
+        b = p // 2
+        k = (z - p) % 4
+
+        @pl.when(z != p)
+        def _():
+            arrived(view, r.gz_r.at[i, k])
+
+        if p in (0, 3):
+            at, to, slot_at = (2, 3, 3) if p == 0 else (1, 0, 1)
+            go(sent_f[b], view, view, r.gz_s.at[i, 0], r.gz_r.at[i, slot_at], device(x, to, y, c), z == at)
+        if g < 5:
+            go(sent_f[b], view, view, r.gy_s.at[g, k], r.gy_r.at[g, k], yn, z != p)
+
+    def ffn_y(g, p):
+        arrived(part(g, p, 1 - y, c, x), r.gy_r.at[g, (z - p) % 4])
+
+    def other_z(b):
         view = part(5, z, 1 - y, c, x)
-        arrived(view, r.gy_r.at[5, 0])
-        z_out(view, view, 5, 6)
-
-    def other_arrivals():
-        for k in steps:
-            view = part(5, (z - k) % 4, 1 - y, c, x)
-            arrived(view, r.gz_r.at[6, k])
-            z_on(view, 5, 6, k)
+
+        @pl.when(branch[b])
+        def _():
+            arrived(view, r.gy_r.at[5, 0])
+
+        z_out(view, view, 5, 6, b)
 
     def gather_x(g):
         for j in range(7):
@@ -604,7 +626,6 @@
             arrived(view, r.gc_r.at[g, j])
 
     tail = remote(r.tails, r.before, r.tail_s.at[0], r.tail_r.at[0], following)
-    tail.start()
     back = shift_back()
 
     def one_hot(shape, pick):
@@ -650,98 +671,88 @@
             ),
         ),
     )
-    store_rows(r.own_t, 0, mm(tail_v, r.tails[...]).astype(BF))
     mine_s, mine_c = part(0, z, y, c, None), part(1, z, y, c, None)
-    perm = lay_rows(0, r.flat_s, mine_s, 12)
-    tail.wait_recv()
-    store_rows(mine_s, 0, mm(perm, first_window(0, r.flat_s, 96)).astype(BF))
-    own_z(0)
-    own_y(0)
-    own_core(0)
-
-    @pl.when(root)
-    def _():
-        mine = pltpu.make_async_copy(r.own_t, r.tb.at[z], r.loc.at[0])
-        mine.start()
-        out = []
-        for k in (1, 2, 3):
-            go(out, r.own_t, r.tb.at[z], r.t_s.at[k - 1], r.t_r.at[k], zdev(k))
-        mine.wait()
-        for k in (1, 2, 3):
-            arrived(r.tb.at[(z - k) % 4], r.t_r.at[k])
-        for i, (yy, cc) in enumerate(((0, 0), (0, 1), (1, 0))):
-            go(out, r.tb, r.tb, r.t_s.at[3 + i], r.t_r.at[0], device(x, z, yy, cc))
-        drain(out)
-
-    perm = lay_rows(1, r.flat_c, mine_c, 17)
-    store_rows(mine_c, 0, mm(perm, first_window(1, r.flat_c, 96)).astype(BF))
-    own_z(1)
-    own_y(1)
-    own_core(1)
-
-    @pl.when(w1)
-    def _():
-        def pick(i):
-            m, j = i % 16, i // 16
-            q = 2 * jnp.where(j < 6, c, 1 - c) + x
-            j = j % 6
-            return 32 - back[2] + 24 * m + 12 * (j // 3) + 3 * q + j % 3
-
-        perm = one_hot((192, 416), pick)
-        mine = part_f(z, y, 192 * c, 192)
-
-        def put(i, window):
-            tiles = mm(perm, window).astype(BF)
-            store_rows(r.theirs, 16 * i, tiles[96:192])
-            store_rows(mine, 16 * i, tiles[0:96])
-
-        def body(i, carry):
-            put(i, r.flat_f[pl.ds(pl.multiple_of(384 * i - 32, 32), 416)])
-            return carry
-
-        put(0, first_window(2, r.flat_f, 384))
-        lax.fori_loop(1, 12, body, 0)
-        swap = remote(r.theirs, mine, r.gc_s.at[2, 0], r.gc_r.at[2, 0], core)
-        swap.start()
-        swap.wait()
-
-    @pl.when(jnp.logical_not(w1))
-    def _():
-        perm = to_rows(2)
-        mine = part_f(z, y)
-
-        def body(i, carry):
-            window = r.flat_f[pl.ds(pl.multiple_of(2304 * x + 96 * i - 32, 32), 128)]
-            store_rows(mine, 16 * i, mm(perm, window).astype(BF))
-            return carry
-
-        lax.fori_loop(1, 24, body, 0)
-        lead = jnp.where(x == 0, r.before[64:96], r.flat_f[2304 - 32 : 2304])
-        rest = r.flat_f[pl.ds(pl.multiple_of(2304 * x, 32), 96)]
-        store_rows(mine, 0, mm(perm, jnp.concatenate([lead, rest], 0)).astype(BF))
-
-    tail.wait_send()
-    r.vg[...] = jnp.zeros_like(r.vg)
-
-    own_y(5)
-    gather_z(0)
-    own_z(2)
-    for g in (2, 3, 4):
-        own_y(g)
-    gather_y(0)
-    own_z(3)
-    gather_z(1)
-    own_z(4)
-    own_z(5)
-    other_z()
-    gather_y(1, (0,))
-    gather_x(0)
-    @pl.when(jnp.logical_not(root))
-    def _():
-        arrived(r.tb, r.t_r.at[0])
-
-    r.tv[...] = r.tb[...].astype(F32)
-    gather_core(0, range(15))
+
+    def rows_s():
+        store_rows(r.own_t, 0, mm(tail_v, r.tails[...]).astype(BF))
+        perm = lay_rows(0, r.flat_s, mine_s, 12)
+        tail.wait_recv()
+        store_rows(mine_s, 0, mm(perm, first_window(0, r.flat_s, 96)).astype(BF))
+
+    def rows_c():
+        perm = lay_rows(1, r.flat_c, mine_c, 17)
+        store_rows(mine_c, 0, mm(perm, first_window(1, r.flat_c, 96)).astype(BF))
+
+    def rows_f():
+        @pl.when(w1)
+        def _():
+            def pick(i):
+                m, j = i % 16, i // 16
+                q = 2 * jnp.where(j < 6, c, 1 - c) + x
+                j = j % 6
+                return 32 - back[2] + 24 * m + 12 * (j // 3) + 3 * q + j % 3
+
+            perm = one_hot((192, 416), pick)
+            mine = part_f(z, y, 192 * c, 192)
+
+            def put(i, window):
+                tiles = mm(perm, window).astype(BF)
+                store_rows(r.theirs, 16 * i, tiles[96:192])
+                store_rows(mine, 16 * i, tiles[0:96])
+
+            def body(i, carry):
+                put(i, r.flat_f[pl.ds(pl.multiple_of(384 * i - 32, 32), 416)])
+                return carry
+
+            put(0, first_window(2, r.flat_f, 384))
+            lax.fori_loop(1, 12, body, 0)
+            swap = remote(r.theirs, mine, r.gc_s.at[2, 0], r.gc_r.at[2, 0], core)
+            swap.start()
+            swap.wait()
+
+        @pl.when(jnp.logical_not(w1))
+        def _():
+            perm = to_rows(2)
+            mine = part_f(z, y)
+
+            def body(i, carry):
+                window = r.flat_f[pl.ds(pl.multiple_of(2304 * x + 96 * i - 32, 32), 128)]
+                store_rows(mine, 16 * i, mm(perm, window).astype(BF))
+                return carry
+
+            lax.fori_loop(1, 24, body, 0)
+            lead = jnp.where(x == 0, r.before[64:96], r.flat_f[2304 - 32 : 2304])
+            rest = r.flat_f[pl.ds(pl.multiple_of(2304 * x, 32), 96)]
+            store_rows(mine, 0, mm(perm, jnp.concatenate([lead, rest], 0)).astype(BF))
+
+    def vectors_out():
+        @pl.when(root)
+        def _():
+            own = pltpu.make_async_copy(r.own_t, r.tb.at[z], r.loc.at[0])
+            own.start()
+            for k in (1, 2, 3):
+                remote(r.own_t, r.tb.at[z], r.t_s.at[k - 1], r.t_r.at[k], zdev(k)).start()
+            own.wait()
+
+    def vectors_on():
+        @pl.when(root)
+        def _():
+            for k in (1, 2, 3):
+                arrived(r.tb.at[(z - k) % 4], r.t_r.at[k])
+            out = []
+            for i, (yy, cc) in enumerate(((0, 0), (0, 1), (1, 0))):
+                go(out, r.tb, r.tb, r.t_s.at[3 + i], r.t_r.at[0], device(x, z, yy, cc))
+            drain(out)
+            for k in (1, 2, 3):
+                remote(r.own_t, r.tb.at[z], r.t_s.at[k - 1], r.t_r.at[k], zdev(k)).wait_send()
+
+    def vectors_in():
+        @pl.when(jnp.logical_not(root))
+        def _():
+            arrived(r.tb, r.t_r.at[0])
+
+        r.tv[...] = r.tb[...].astype(F32)
+        r.vg[...] = jnp.zeros_like(r.vg)
 
     self_v = lambda j: r.tv[3, j : j + 1]
     cross_v = lambda j: r.tv[3, 5 + j : 6 + j]
@@ -794,53 +805,47 @@
             rs_copy(ph, b, i).wait_send()
         return r.part[b, me] + r.recv_p[ph, b, 1].astype(F32) + r.recv_x[ph, b].astype(F32)
 
-    h = r.hid[...]
-    r.q[...] = (mm(h, r.ws[0]) + self_v(0)).astype(BF)
-    r.k[...] = mm(h, r.ws[1]).astype(BF)
-    r.v[...] = (mm(h, r.ws[2]) + self_v(1)).astype(BF)
-    for i in range(2):
-        rows = slice(64 * i, 64 * i + 64)
-        at = lax.broadcasted_iota(jnp.int32, (256, 64), 0) % 64
-        key = lax.broadcasted_iota(jnp.int32, (256, 64), 1)
-        caption = jnp.where(at >= NQ, 1.0, 0.0) * jnp.where(key <= at, 1.0, 0.0)
-        ok = jnp.where(key < NQ, 1.0, caption * jnp.where(key < NQ + r.lens[i], 1.0, 0.0))
-        for g in range(3):
-            lanes = slice(256 * g, 256 * g + 256)
-            p, a = attend_block(r.q[rows, lanes], r.k[rows, lanes], r.v[rows, lanes], ok)
-            r.p[i, g] = p
-            r.a[rows, lanes] = a
-    r.sum1[...] = h.astype(F32) + (mm(r.a[...], r.ws[3]) + self_v(2))
-    xh, _ = normed(r.sum1[...])
-    r.first[...] = xh * self_v(3) + self_v(4)
-    r.xg[0, 1, me] = rows_of(r.first, 32).astype(BF)
-    ag_start(0, 1)
-    gather_z(2)
-    gather_y(1, (1, 2, 3))
-    gather_z(3)
-
-    for i in range(2):
-        r.ck[272 * i + 256 : 272 * i + 272] = jnp.zeros((16, D), BF)
-        r.cv[272 * i + 256 : 272 * i + 272] = jnp.zeros((16, D), BF)
-    gather_core(1, range(8))
-    for i in range(2):
-        rows = slice(272 * i, 272 * i + 257)
-        r.ck[rows, cols(x)] = mm(r.feat[i], r.wc[768:2176, cols(x)]).astype(BF)
-        bias = r.tv[3, 6:7, cols(x)]
-        r.cv[rows, cols(x)] = (mm(r.feat[i], r.wc[2176:3584, cols(x)]) + bias).astype(BF)
-    ag_mid(0, 1)
-    gather_z(4)
-    gather_x(1)
-    gather_core(1, range(8, 15))
-    far_cols = cols(1 - x)
-    for i in range(2):
-        rows = slice(272 * i, 272 * i + 257)
-        r.ck[rows, far_cols] = mm(r.feat[i], r.wc[768:2176, far_cols]).astype(BF)
-        bias = r.tv[3, 6:7, far_cols]
-        r.cv[rows, far_cols] = (mm(r.feat[i], r.wc[2176:3584, far_cols]) + bias).astype(BF)
-    u = rows_of(r.first, 0)
-    r.cq[...] = (mm(u.astype(BF), r.wc[0:768]) + cross_v(0)).astype(BF)
-    ok = jnp.where(lax.broadcasted_iota(jnp.int32, (128, 272), 1) < 257, 1.0, 0.0)
-    for i in range(2):
+    keep = SimpleNamespace()
+
+    def self_attention():
+        h = r.hid[...]
+        r.q[...] = (mm(h, r.ws[0]) + self_v(0)).astype(BF)
+        r.k[...] = mm(h, r.ws[1]).astype(BF)
+        r.v[...] = (mm(h, r.ws[2]) + self_v(1)).astype(BF)
+        for i in range(2):
+            rows = slice(64 * i, 64 * i + 64)
+            at = lax.broadcasted_iota(jnp.int32, (256, 64), 0) % 64
+            key = lax.broadcasted_iota(jnp.int32, (256, 64), 1)
+            caption = jnp.where(at >= NQ, 1.0, 0.0) * jnp.where(key <= at, 1.0, 0.0)
+            ok = jnp.where(key < NQ, 1.0, caption * jnp.where(key < NQ + r.lens[i], 1.0, 0.0))
+            for g in range(3):
+                lanes = slice(256 * g, 256 * g + 256)
+                p, a = attend_block(r.q[rows, lanes], r.k[rows, lanes], r.v[rows, lanes], ok)
+                r.p[i, g] = p
+                r.a[rows, lanes] = a
+        r.sum1[...] = h.astype(F32) + (mm(r.a[...], r.ws[3]) + self_v(2))
+        xh, _ = normed(r.sum1[...])
+        r.first[...] = xh * self_v(3) + self_v(4)
+        r.xg[0, 1, me] = rows_of(r.first, 32).astype(BF)
+
+    def image_rows(lanes):
+        for i in range(2):
+            rows = slice(272 * i, 272 * i + 257)
+            r.ck[rows, lanes] = mm(r.feat[i], r.wc[768:2176, lanes]).astype(BF)
+            bias = r.tv[3, 6:7, lanes]
+            r.cv[rows, lanes] = (mm(r.feat[i], r.wc[2176:3584, lanes]) + bias).astype(BF)
+
+    def pad_rows():
+        for i in range(2):
+            r.ck[272 * i + 256 : 272 * i + 272] = jnp.zeros((16, D), BF)
+            r.cv[272 * i + 256 : 272 * i + 272] = jnp.zeros((16, D), BF)
+
+    def cross_start():
+        keep.u = rows_of(r.first, 0)
+        r.cq[...] = (mm(keep.u.astype(BF), r.wc[0:768]) + cross_v(0)).astype(BF)
+
+    def cross_attention(i):
+        ok = jnp.where(lax.broadcasted_iota(jnp.int32, (128, 272), 1) < 257, 1.0, 0.0)
         rows = slice(272 * i, 272 * i + 272)
         mine = slice(32 * i, 32 * i + 32)
         for g in range(3):
@@ -848,17 +853,14 @@
             p, a = attend_block(r.cq[mine, lanes], r.ck[rows, lanes], r.cv[rows, lanes], ok)
             r.pc[i, g] = p
             r.ca[mine, lanes] = a
-        if i == 0:
-            gather_z(5, last=True)
-    r.sum2[...] = u + (mm(r.ca[...], r.wc[3584:4352]) + cross_v(2))
-    xh, _ = normed(r.sum2[...])
-    r.second[...] = xh * cross_v(3) + cross_v(4)
-    r.xg[0, 0, me] = r.second[...].astype(BF)
-    ag_start(0, 0)
-
-    other_arrivals()
-    for g in (2, 3, 4):
-        gather_y(g)
+
+    def cross_end():
+        r.sum2[...] = keep.u + (mm(r.ca[...], r.wc[3584:4352]) + cross_v(2))
+        xh, _ = normed(r.sum2[...])
+        r.second[...] = xh * cross_v(3) + cross_v(4)
+        r.xg[0, 0, me] = r.second[...].astype(BF)
+
+    sent = []
 
     def ffn_forward_part(b):
         rows = r.xg[0, b].reshape(256, D)
@@ -890,13 +892,14 @@
         for j in range(4):
             r.vg[2 * b, 10 + j : 11 + j] = jnp.where(j == me, db1, 0.0)
 
-    sent = []
-
     def ffn_weight_grads(b):
+        drain(sent_f[b])
         rows = r.xg[0, b].reshape(256, D)
         up = r.xg[1, b].reshape(256, D)
         r.wf[2 * b] = mm_tn(rows, r.dpre[b]).astype(BF)
         r.wf[2 * b + 1] = mm_tn(r.act[b], up).astype(BF)
+
+    def ffn_sum_start(b):
         for p in (2 * b, 2 * b + 1):
             go(sent, part_f(p, 1 - y, 0, SPLIT), r.yf.at[p], r.yy_s.at[2, p], r.yy_r.at[2, p], yn)
         for p in (2 * b, 2 * b + 1):
@@ -953,49 +956,17 @@
         z_total(4, part_f(z, 1 - y, SPLIT, REST)[...], r.of)
         go(sent, r.of, r.yf2, r.yy_s.at[3, 0], r.yy_r.at[3, 0], yn)
 
-    ag_end(0, 1)
-    ffn_forward_part(1)
-    rs_start(0, 1)
-    ag_mid(0, 0)
-    ag_end(0, 0)
-    rs_mid(0, 1)
-    ffn_forward_part(0)
-    rs_start(0, 0)
-    ffn_turn(1)
-    ag_start(1, 1)
-    rs_mid(0, 0)
-    ag_mid(1, 1)
-    ag_end(1, 1)
-    ffn_backward_part(1)
-    rs_start(1, 1)
-    ffn_turn(0)
-    ag_start(1, 0)
-    rs_mid(1, 1)
-    drain(sent_w[2])
-    ffn_weight_grads(1)
-    ag_mid(1, 0)
-    ag_end(1, 0)
-    ffn_backward_part(0)
-    rs_start(1, 0)
-    d_text = r.dsum3[1] + rs_end(1, 1)
-    for i in range(2):
-        r.dfirst[64 * i + 32 : 64 * i + 64] = d_text[32 * i : 32 * i + 32]
-    rs_mid(1, 0)
-    ffn_weight_grads(0)
-    d_second = r.dsum3[0] + rs_end(1, 0)
-
     groups = (
         (shard_s, r.core_s, r.xs, r.ys, r.fin_s, r.nice_s),
         (shard_c, r.core_c, r.xc, r.yc, r.fin_c, r.nice_c),
     )
     order = (3, 1, 2, 0)
 
-    def sum_start(g):
+    def sum_start(g, far):
         view, cb = groups[g][:2]
-        for far in range(2):
-            for d in order:
-                zz = (z + d) % 4
-                go(sent, view(zz, y if far else 1 - y, 1 - c), cb.at[far, zz], r.co_s.at[g, far, d], r.co_r.at[g, far, d], core)
+        for d in order:
+            zz = (z + d) % 4
+            go(sent, view(zz, y if far else 1 - y, 1 - c), cb.at[far, zz], r.co_s.at[g, far, d], r.co_r.at[g, far, d], core)
 
     def sum_core(g, fars=(0, 1)):
         view, cb, xb, yb = groups[g][:4]
@@ -1088,136 +1059,6 @@
         pl.when(w1)(lambda: ends(3))
         pl.when(jnp.logical_not(w1))(lambda: ends(2))
 
-    du2, dgain, dshift = norm_back(r.sum2[...], cross_v(3), d_second)
-    r.vg[3, 8:9] = dgain
-    r.vg[3, 9:10] = dshift
-    low = du2.astype(BF)
-    r.vg[3, 7:8] = rows_sum(low)
-    dca = mm_nt(low, r.wc[3584:4352]).astype(BF)
-    drain(sent_w[1])
-    r.wc[3584:4352] = mm_tn(r.ca[...], low).astype(BF)
-    dcq = []
-    for i in range(2):
-        rows = slice(272 * i, 272 * i + 272)
-        mine = slice(32 * i, 32 * i + 32)
-        blocks = []
-        for g in range(3):
-            lanes = slice(256 * g, 256 * g + 256)
-            dq, dk, dv = attend_block_back(
-                r.cq[mine, lanes], r.ck[rows, lanes], r.cv[rows, lanes], r.pc[i, g], dca[mine, lanes]
-            )
-            blocks.append(dq)
-            r.ck[rows, lanes] = dk
-            r.cv[rows, lanes] = dv
-        dcq.append(jnp.concatenate(blocks, 1))
-    dcq = jnp.concatenate(dcq, 0)
-    r.vg[3, 5:6] = rows_sum(dcq)
-    r.vg[3, 6:7] = rows_sum(r.cv[...])
-    du = du2 + mm_nt(dcq, r.wc[0:768])
-    for i in range(2):
-        r.dfirst[64 * i : 64 * i + 32] = du[32 * i : 32 * i + 32]
-    r.wc[0:768] = mm_tn(rows_of(r.first, 0).astype(BF), dcq).astype(BF)
-    for j in range(11):
-        block = [r.feat[i, :, 128 * j : 128 * j + 128] for i in range(2)]
-        both = lambda d: mm_tn(block[0], d[0:257]) + mm_tn(block[1], d[272:529])
-        r.wc[768 + 128 * j : 896 + 128 * j] = both(r.ck).astype(BF)
-        r.wc[2176 + 128 * j : 2304 + 128 * j] = both(r.cv).astype(BF)
-    sum_start(1)
-    ffn_add(3)
-    ffn_sum_y(2)
-    ffn_sum_y(3)
-
-    dsum1, dgain, dshift = norm_back(r.sum1[...], self_v(3), r.dfirst[...])
-    r.vg[3, 3:4] = dgain
-    r.vg[3, 4:5] = dshift
-    low = dsum1.astype(BF)
-    r.vg[3, 2:3] = rows_sum(low)
-    da = mm_nt(low, r.ws[3]).astype(BF)
-    drain(sent_w[0])
-    r.ws[3] = mm_tn(r.a[...], low).astype(BF)
-    for i in range(2):
-        rows = slice(64 * i, 64 * i + 64)
-        for g in range(3):
-            lanes = slice(256 * g, 256 * g + 256)
-            dq, dk, dv = attend_block_back(
-                r.q[rows, lanes], r.k[rows, lanes], r.v[rows, lanes], r.p[i, g], da[rows, lanes]
-            )
-            r.q[rows, lanes] = dq
-            r.k[rows, lanes] = dk
-            r.v[rows, lanes] = dv
-    sum_core(1, (0,))
-    r.vg[3, 0:1] = rows_sum(r.q[...])
-    r.vg[3, 1:2] = rows_sum(r.v[...])
-    total = dsum1 + mm_nt(r.q[...], r.ws[0]) + mm_nt(r.k[...], r.ws[1]) + mm_nt(r.v[...], r.ws[2])
-    r.hgrad[...] = total.astype(BF)
-    r.ws[0] = mm_tn(r.hid[...], r.q[...]).astype(BF)
-    r.ws[1] = mm_tn(r.hid[...], r.k[...]).astype(BF)
-    r.ws[2] = mm_tn(r.hid[...], r.v[...]).astype(BF)
-    sum_start(0)
-    sum_core(1, (1,))
-    sum_core(0)
-
-    r.v_send[...] = r.vg[...].astype(BF)
-    index = 2 * y + c
-    home = device(x, z, 1, 1)
-
-    @pl.when(jnp.logical_not(root))
-    def _():
-        remote(r.v_send, r.v_in.at[index], r.vv_s.at[0], r.vv_r.at[index], home).start()
-
-    ffn_add(0)
-    ffn_sum_y(0)
-    ffn_sum_y(1)
-    z_add_sum(2, r.yf.at[0], 0)
-    z_add_sum(2, r.yf.at[3], 3)
-    sum_mid(1, (0,))
-
-    @pl.when(root)
-    def _():
-        total = r.vg[...]
-        for i in range(3):
-            arrived(r.v_in.at[i], r.vv_r.at[i])
-            total = total + r.v_in[i].astype(F32)
-        r.v_z[...] = total.astype(BF)
-        for k in (1, 2, 3):
-            zz = (z + k) % 4
-            remote(r.v_z.at[zz], r.v_zin.at[k - 1], r.vv_s.at[k], r.vv_r.at[2 + k], device(x, zz, y, c)).start()
-
-    sum_mid(0)
-    sum_mid(1, (1,))
-    ffn_sum_other()
-    sum_last(1)
-
-    @pl.when(root)
-    def _():
-        total = r.v_z[z].astype(F32)
-        for k in (1, 2, 3):
-            arrived(r.v_zin.at[k - 1], r.vv_r.at[2 + k])
-            total = total + r.v_zin[k - 1].astype(F32)
-        r.v_x[...] = total.astype(BF)
-        remote(r.v_x, r.v_xin, r.vv_s.at[4], r.vv_r.at[6], xn).start()
-
-    ffn_sum_z()
-    sum_last(0)
-    sum_z(1)
-    sum_z(0)
-
-    @pl.when(root)
-    def _():
-        arrived(r.v_xin, r.vv_r.at[6])
-        r.total_v[...] = add(r.v_x[...], r.v_xin[...])
-        for k in (1, 2, 3):
-            zz = (z + k) % 4
-            remote(r.v_z.at[zz], r.v_zin.at[k - 1], r.vv_s.at[k], r.vv_r.at[2 + k], device(x, zz, y, c)).wait_send()
-        remote(r.v_x, r.v_xin, r.vv_s.at[4], r.vv_r.at[6], xn).wait_send()
-
-    @pl.when(jnp.logical_not(root))
-    def _():
-        r.total_v[...] = jnp.zeros_like(r.total_v)
-        remote(r.v_send, r.v_in.at[index], r.vv_s.at[0], r.vv_r.at[index], home).wait_send()
-
-    ffn_end()
-
     def stack(src, row, n=6):
         return jnp.concatenate(
             [src[pl.ds(pl.multiple_of(row, 16), 16), 128 * j : 128 * j + 128] for j in range(n)], 0
@@ -1236,27 +1077,311 @@
         r.heads[g] = fl[0:32]
         go(sent, r.heads.at[g], r.after.at[g], r.head_s.at[g], r.head_r.at[g], preceding)
 
-    @pl.when(w1)
-    def _():
-        def pick(i):
-            m, t = i // 24, i % 24
-            return 96 * ((t % 12) // 3) + 16 * (3 * (t // 12) + t % 3) + m
-
-        perm = one_hot((384, 384), pick)
-
-        def body(i, carry):
-            tiles = jnp.concatenate([stack(r.nice_f.at[q], 16 * i) for q in range(4)], 0)
-            r.out_f[pl.ds(pl.multiple_of(384 * i, 128), 384)] = mm(perm, tiles).astype(BF)
-            return carry
-
-        lax.fori_loop(0, 12, body, 0)
-
-    @pl.when(jnp.logical_not(w1))
-    def _():
-        for q in range(4):
-            lay_flat(r.nice_f.at[q], r.out_f, 12, 1152 * q)
-
-    head_out(2, r.out_f)
+    def text_end():
+        d_text = r.dsum3[1] + rs_end(1, 1)
+        for i in range(2):
+            r.dfirst[64 * i + 32 : 64 * i + 64] = d_text[32 * i : 32 * i + 32]
+
+    def query_end():
+        keep.d_second = r.dsum3[0] + rs_end(1, 0)
+
+    def cross_back():
+        du2, dgain, dshift = norm_back(r.sum2[...], cross_v(3), keep.d_second)
+        r.vg[3, 8:9] = dgain
+        r.vg[3, 9:10] = dshift
+        low = keep.low2 = du2.astype(BF)
+        r.vg[3, 7:8] = rows_sum(low)
+        dca = mm_nt(low, r.wc[3584:4352]).astype(BF)
+        dcq = []
+        for i in range(2):
+            rows = slice(272 * i, 272 * i + 272)
+            mine = slice(32 * i, 32 * i + 32)
+            blocks = []
+            for g in range(3):
+                lanes = slice(256 * g, 256 * g + 256)
+                dq, dk, dv = attend_block_back(
+                    r.cq[mine, lanes], r.ck[rows, lanes], r.cv[rows, lanes], r.pc[i, g], dca[mine, lanes]
+                )
+                blocks.append(dq)
+                r.ck[rows, lanes] = dk
+                r.cv[rows, lanes] = dv
+            dcq.append(jnp.concatenate(blocks, 1))
+        dcq = keep.dcq = jnp.concatenate(dcq, 0)
+        r.vg[3, 5:6] = rows_sum(dcq)
+        r.vg[3, 6:7] = rows_sum(r.cv[...])
+        du = du2 + mm_nt(dcq, r.wc[0:768])
+        for i in range(2):
+            r.dfirst[64 * i : 64 * i + 32] = du[32 * i : 32 * i + 32]
+
+    def cross_grads():
+        drain(sent_w[1])
+        r.wc[3584:4352] = mm_tn(r.ca[...], keep.low2).astype(BF)
+        r.wc[0:768] = mm_tn(rows_of(r.first, 0).astype(BF), keep.dcq).astype(BF)
+        for j in range(11):
+            block = [r.feat[i, :, 128 * j : 128 * j + 128] for i in range(2)]
+            both = lambda d: mm_tn(block[0], d[0:257]) + mm_tn(block[1], d[272:529])
+            r.wc[768 + 128 * j : 896 + 128 * j] = both(r.ck).astype(BF)
+            r.wc[2176 + 128 * j : 2304 + 128 * j] = both(r.cv).astype(BF)
+
+    def self_back():
+        dsum1, dgain, dshift = norm_back(r.sum1[...], self_v(3), r.dfirst[...])
+        r.vg[3, 3:4] = dgain
+        r.vg[3, 4:5] = dshift
+        keep.dsum1 = dsum1
+        low = keep.low1 = dsum1.astype(BF)
+        r.vg[3, 2:3] = rows_sum(low)
+        da = mm_nt(low, r.ws[3]).astype(BF)
+        for i in range(2):
+            rows = slice(64 * i, 64 * i + 64)
+            for g in range(3):
+                lanes = slice(256 * g, 256 * g + 256)
+                dq, dk, dv = attend_block_back(
+                    r.q[rows, lanes], r.k[rows, lanes], r.v[rows, lanes], r.p[i, g], da[rows, lanes]
+                )
+                r.q[rows, lanes] = dq
+                r.k[rows, lanes] = dk
+                r.v[rows, lanes] = dv
+
+    def self_grads():
+        drain(sent_w[0])
+        r.vg[3, 0:1] = rows_sum(r.q[...])
+        r.vg[3, 1:2] = rows_sum(r.v[...])
+        total = keep.dsum1 + mm_nt(r.q[...], r.ws[0]) + mm_nt(r.k[...], r.ws[1]) + mm_nt(r.v[...], r.ws[2])
+        r.hgrad[...] = total.astype(BF)
+        r.ws[0] = mm_tn(r.hid[...], r.q[...]).astype(BF)
+        r.ws[1] = mm_tn(r.hid[...], r.k[...]).astype(BF)
+        r.ws[2] = mm_tn(r.hid[...], r.v[...]).astype(BF)
+        r.ws[3] = mm_tn(r.a[...], keep.low1).astype(BF)
+
+    index = 2 * y + c
+    home = device(x, z, 1, 1)
+
+    def vector_sums_out():
+        r.v_send[...] = r.vg[...].astype(BF)
+
+        @pl.when(jnp.logical_not(root))
+        def _():
+            remote(r.v_send, r.v_in.at[index], r.vv_s.at[0], r.vv_r.at[index], home).start()
+
+    def vector_sums_z():
+        @pl.when(root)
+        def _():
+            total = r.vg[...]
+            for i in range(3):
+                arrived(r.v_in.at[i], r.vv_r.at[i])
+                total = total + r.v_in[i].astype(F32)
+            r.v_z[...] = total.astype(BF)
+            for k in (1, 2, 3):
+                zz = (z + k) % 4
+                remote(r.v_z.at[zz], r.v_zin.at[k - 1], r.vv_s.at[k], r.vv_r.at[2 + k], device(x, zz, y, c)).start()
+
+    def vector_sums_x():
+        @pl.when(root)
+        def _():
+            total = r.v_z[z].astype(F32)
+            for k in (1, 2, 3):
+                arrived(r.v_zin.at[k - 1], r.vv_r.at[2 + k])
+                total = total + r.v_zin[k - 1].astype(F32)
+            r.v_x[...] = total.astype(BF)
+            remote(r.v_x, r.v_xin, r.vv_s.at[4], r.vv_r.at[6], xn).start()
+
+    def vector_sums_end():
+        @pl.when(root)
+        def _():
+            arrived(r.v_xin, r.vv_r.at[6])
+            r.total_v[...] = add(r.v_x[...], r.v_xin[...])
+            for k in (1, 2, 3):
+                zz = (z + k) % 4
+                remote(r.v_z.at[zz], r.v_zin.at[k - 1], r.vv_s.at[k], r.vv_r.at[2 + k], device(x, zz, y, c)).wait_send()
+            remote(r.v_x, r.v_xin, r.vv_s.at[4], r.vv_r.at[6], xn).wait_send()
+
+        @pl.when(jnp.logical_not(root))
+        def _():
+            r.total_v[...] = jnp.zeros_like(r.total_v)
+            remote(r.v_send, r.v_in.at[index], r.vv_s.at[0], r.vv_r.at[index], home).wait_send()
+
+    def flat_f():
+        @pl.when(w1)
+        def _():
+            def pick(i):
+                m, t = i // 24, i % 24
+                return 96 * ((t % 12) // 3) + 16 * (3 * (t // 12) + t % 3) + m
+
+            perm = one_hot((384, 384), pick)
+
+            def body(i, carry):
+                tiles = jnp.concatenate([stack(r.nice_f.at[q], 16 * i) for q in range(4)], 0)
+                r.out_f[pl.ds(pl.multiple_of(384 * i, 128), 384)] = mm(perm, tiles).astype(BF)
+                return carry
+
+            lax.fori_loop(0, 12, body, 0)
+
+        @pl.when(jnp.logical_not(w1))
+        def _():
+            for q in range(4):
+                lay_flat(r.nice_f.at[q], r.out_f, 12, 1152 * q)
+
+        head_out(2, r.out_f)
+
+    tail.start()
+    rows_s()
+    own_z(0)
+    own_y(0)
+    own_core(0)
+    vectors_out()
+    pad_rows()
+    rows_f()
+    gather_y(0, 0)
+    rows_c()
+    vectors_on()
+    own_y(1)
+    own_z(1)
+    gather_z(0, 0)
+    gather_z(0, 1)
+    own_y(2, 1)
+    gather_y(1, 0)
+    gather_z(0, 2)
+    gather_z(1, 1)
+    gather_y(0, 1)
+    own_core(1)
+    own_y(3, 0)
+    gather_y(0, 2)
+    own_y(5, 0)
+    own_z(2, 1)
+    own_y(5, 1)
+    own_z(3, 0)
+    gather_y(0, 3)
+    gather_z(1, 0)
+    own_z(4, 0)
+    other_z(0)
+    own_z(4, 1)
+    ffn_z(2, 2)
+    gather_z(1, 2)
+    gather_x(0)
+    own_y(3, 1)
+    gather_core(0, range(15))
+    gather_y(1, 2)
+    own_y(4, 0)
+    own_z(3, 1)
+    gather_y(1, 1)
+    vectors_in()
+    self_attention()
+    ffn_z(3, 1)
+    ffn_z(2, 3)
+    gather_y(1, 3)
+    gather_core(1, range(8))
+    ffn_z(4, 3)
+    ffn_z(4, 0)
+    other_z(1)
+    ffn_z(4, 1)
+    ffn_z(3, 2)
+    ffn_z(3, 3)
+    own_z(2, 0)
+    ffn_y(2, 3)
+    own_z(5, 1)
+    ag_start(0, 1)
+    own_y(4, 1)
+    image_rows(cols(x))
+    gather_x(1)
+    ffn_z(4, 2)
+    ffn_z(2, 1)
+    ffn_z(5, 0, other=True)
+    gather_core(1, range(8, 15))
+    own_z(5, 0)
+    image_rows(cols(1 - x))
+    ag_mid(0, 1)
+    cross_start()
+    cross_attention(0)
+    ffn_y(4, 3)
+    ffn_z(5, 3, other=True)
+    ffn_y(3, 3)
+    cross_attention(1)
+    cross_end()
+    ffn_z(5, 3)
+    ffn_z(5, 2)
+    ffn_z(5, 2, other=True)
+    own_y(2, 0)
+    ffn_y(3, 1)
+    ffn_y(4, 0)
+    ag_end(0, 1)
+    ag_start(0, 0)
+    ffn_y(2, 2)
+    ffn_z(3, 0)
+    ffn_y(4, 2)
+    ffn_y(3, 2)
+    ffn_forward_part(1)
+    rs_start(0, 1)
+    ffn_z(2, 0)
+    ag_mid(0, 0)
+    rs_mid(0, 1)
+    ffn_z(5, 1, other=True)
+    ffn_y(2, 1)
+    ffn_z(5, 0)
+    ffn_turn(1)
+    ag_start(1, 1)
+    ffn_y(3, 0)
+    ffn_y(4, 1)
+    ag_end(0, 0)
+    ffn_z(5, 1)
+    ffn_y(2, 0)
+    ffn_forward_part(0)
+    rs_start(0, 0)
+    ag_mid(1, 1)
+    rs_mid(0, 0)
+    ag_end(1, 1)
+    ffn_backward_part(1)
+    ffn_weight_grads(1)
+    ffn_sum_start(1)
+    ffn_turn(0)
+    ag_start(1, 0)
+    rs_start(1, 1)
+    ag_mid(1, 0)
+    rs_mid(1, 1)
+    ag_end(1, 0)
+    ffn_backward_part(0)
+    rs_start(1, 0)
+    ffn_weight_grads(0)
+    ffn_sum_start(0)
+    rs_mid(1, 0)
+    text_end()
+    query_end()
+    cross_back()
+    cross_grads()
+    sum_start(1, 0)
+    self_back()
+    self_grads()
+    vector_sums_out()
+    ffn_add(0)
+    ffn_add(3)
+    sum_start(0, 0)
+    sum_core(1, (0,))
+    ffn_sum_y(3)
+    ffn_sum_y(0)
+    sum_start(0, 1)
+    ffn_sum_y(2)
+    sum_core(0, (0,))
+    sum_start(1, 1)
+    ffn_sum_other()
+    vector_sums_z()
+    sum_core(1, (1,))
+    ffn_sum_y(1)
+    z_add_sum(2, r.yf.at[0], 0)
+    sum_core(0, (1,))
+    z_add_sum(2, r.yf.at[3], 3)
+    sum_mid(1, (0,))
+    ffn_sum_z()
+    sum_mid(0, (0,))
+    sum_mid(1, (1,))
+    sum_last(1)
+    sum_last(0)
+    vector_sums_x()
+    sum_z(1)
+    sum_z(0)
+    ffn_end()
+    flat_f()
+    vector_sums_end()
+    tail.wait_send()
+
     arrived(groups[1][5].at[:, cols(1 - x)], r.fi_r.at[1])
     lay_flat(r.nice_c, r.out_c, 17)
     head_out(1, r.out_c)

time: 244 us -> 231 us (0.947)
  Pallas kernels: 229 us -> 218 us
    pallas_call x1, Pallas kernels: 229 us -> 218 us  [layer(): pl.pallas_call(layer_kernel, out_shape=(jax.ShapeDtypeStruct((128, D), BF...]
where the time goes in v6:
time: 231 us; the launch traced here: 230 us
  Pallas kernels  218 us (94%)
  other arithmetic  5.45 us (2%)
  local copies, waits for them, and re-layouts  5.44 us (2%)
    pallas_call x1, Pallas kernels, layer(): pl.pallas_call(layer_kernel, out_shape=(jax.ShapeDtypeStruct((128, D), BF...  218 us
    reshape x3, other arithmetic, per_device_fast(): lax.dynamic_slice_in_dim(rows, back, flat.shape[0]).astype(F32).reshape(-1)  4.84 us

profile of v6, /device:TPU:0, one launch (start us, length us, event | category | flops | bytes accessed | tf_op | source)
XLA Modules:
  0.0 229.5 jit_solution(12804509063383717594)
XLA Ops:
  0.7 0.7 slice_bitcast_fusion
  1.4 0.7 slice_bitcast_fusion.2
  2.1 0.6 pad_maximum_fusion.refs_3_
  2.7 2.6 %copy.12.refs_6_ = bf16[2,257,1408]{2,1,0:T(8,128)(2,1)} copy(bf16[2,257,1408]{2,0,1:T(2,128)(2,1)} %param.9) | data formatting | bytes 2894848 | tf_op args[2]
  5.3 217.9 %shard_map.110 = (bf16[128,768]{1,0:T(8,128)(2,1)}, bf16[128,768]{1,0:T(8,128)(2,1)}, bf16[1184,128]{1,0:T(8,128)(2,1)}, bf16[1664,128]{1,0:T(8,128)(2,1)}, bf16[4640,128]{1,0:T(8,128)(2,1)}) custom-call(bf16[1154,128]{1,0:T(8,128)(2,1)} %bitcast.24, bf16[1634,128]{1,0:T(8,128)(2,1)} %bitcast.23, bf16[4614,128]{1,0:T(8,128)(2,1)} %bitcast.22, ...), custom_call_target="tpu_custom_call" | custom-call | tf_op jit(solution)/shard_map/pallas_call | solution.py:1423
  223.3 0.0 copy-start
  223.3 3.0 %bitcast_convert_fusion = f32[590592]{0:T(1024)} fusion(bf16[4640,128]{1,0:T(8,128)(2,1)} %get-tuple-element.14, s32[]{:T(128)S(6)} %select_n.24), kind=kLoop, calls=%fused_computation | loop fusion | flops 590592 | bytes 3543556 | tf_op jit(solution)/shard_map/reshape | solution.py:1446
  226.3 0.0 copy-start.1
  226.3 0.0 copy-start.3
  226.3 0.0 copy-done
  226.3 0.0 copy-start.2
  226.3 1.0 bitcast_convert_fusion.1
  227.3 0.0 copy-done.1
  227.3 0.9 bitcast_convert_fusion.2
  228.2 0.0 copy-done.3
  228.2 0.7 copy.15
  228.8 0.0 copy-done.2
  228.8 0.7 copy.16
Async XLA Ops:
  223.3 3.0 %copy-start = (bf16[1664,128]{1,0:T(8,128)(2,1)S(1)}, bf16[1664,128]{1,0:T(8,128)(2,1)}, u32[]{:S(2)}) copy-start(bf16[1664,128]{1,0:T(8,128)(2,1)} %get-tuple-element.13) | copy-start | bytes 1277956
  226.3 1.0 copy-start.1
  226.3 1.9 copy-start.3
  226.3 2.6 %copy-start.2 = (bf16[128,768]{1,0:T(8,128)(2,1)S(1)}, bf16[128,768]{1,0:T(8,128)(2,1)}, u32[]{:S(2)}) copy-start(bf16[128,768]{1,0:T(8,128)(2,1)} %get-tuple-element.11) | copy-start | bytes 589828

commit v7 on v6

--- a/solution.py
+++ b/solution.py
@@ -334,13 +334,6 @@
     return 2 * f, 2 * f, 6 * (f % 4) + jnp.where(f >= 8, 6, 0)
 
 
-def meet(devices):
-    barrier = pltpu.get_barrier_semaphore()
-    for d in devices:
-        pl.semaphore_signal(barrier, inc=1, device_id=d, device_id_type=MESH)
-    pl.semaphore_wait(barrier, len(devices))
-
-
 def remote(src, dst, send, recv, target):
     return pltpu.make_async_remote_copy(
         src_ref=src,
@@ -438,9 +431,9 @@
     return jnp.concatenate([ref[first : first + 32], ref[64 + first : 96 + first]], 0)
 
 
-SPLIT = 240
+SPLIT = 192
 REST = 384 - SPLIT
-X_FIRST = (False, True)
+X_FIRST = (True, False)
 SIDE = tuple((2, 4) if first else (4,) for first in X_FIRST)
 WIDTH = tuple(384 if first else 768 for first in X_FIRST)
 STREAMS = ((192, 384), (272, 384), (SPLIT, D), (REST, D), (REST, D))
@@ -453,6 +446,8 @@
     return dict(
         ws=b(4, D, D), wc=b(4352, D), wf=b(4, D, D), theirs=b(192, D), own_t=b(16, D), tb=b(4, 16, D), before=b(96, 128),
         tv=f(4, 16, D), vg=f(4, 16, D),
+        flat_c=b(1634, 128), flat_f=b(4614, 128), hid=b(128, D), feat=b(2, 257, E), cot=b(128, D), in_sem=dma(5),
+        tails=b(96, 128),
         q=b(128, D), k=b(128, D), v=b(128, D), a=b(128, D), p=f(2, 3, 256, 64),
         sum1=f(128, D), first=f(128, D), cq=b(64, D), ck=b(544, D), cv=b(544, D), ca=b(64, D),
         pc=f(2, 3, 128, 272), sum2=f(64, D), second=f(64, D),
@@ -475,7 +470,7 @@
 
 def layer_kernel(*refs):
     names = [
-        "flat_s", "flat_c", "flat_f", "tails", "lens", "hid", "feat", "cot",
+        "flat_s", "in_c", "in_f", "lens", "in_hid", "in_feat", "in_cot",
         "mixed", "hgrad", "out_s", "out_c", "out_f",
     ] + list(scratch())
     r = SimpleNamespace(**dict(zip(names, refs)))
@@ -485,7 +480,16 @@
     zdev = lambda d: device(x, (z + d) % 4, y, c)
     f = lax.axis_index("fsdp")
     following, preceding = (x, (f + 1) % 16), (x, (f + 15) % 16)
-    meet([core, xn, yn, diag, device(x, z, 1 - y, 1 - c), zdev(1), zdev(2), zdev(3), following, preceding])
+    loads = SimpleNamespace(**{
+        n: pltpu.make_async_copy(getattr(r, f"in_{n[-1]}" if n[:4] == "flat" else f"in_{n}"), getattr(r, n), r.in_sem.at[i])
+        for i, n in enumerate(("flat_c", "flat_f", "hid", "feat", "cot"))
+    })
+    for load in vars(loads).values():
+        load.start()
+    near = [core, xn, yn, diag, device(x, z, 1 - y, 1 - c), zdev(1), zdev(2), zdev(3), following, preceding]
+    barrier = pltpu.get_barrier_semaphore()
+    for d in near:
+        pl.semaphore_signal(barrier, inc=1, device_id=d, device_id_type=MESH)
     me = 2 * c + x
     cols = lambda h: pl.ds(pl.multiple_of(384 * h, 384), 384)
     root = jnp.logical_and(y == 1, c == 1)
@@ -643,16 +647,13 @@
     def first_window(g, flat, n):
         return jnp.concatenate([r.before[32 * g : 32 * g + 32], flat[0:n]], 0)
 
-    def lay_rows(g, flat, dst, n):
-        perm = to_rows(g)
-
+    def lay_rows(perm, flat, dst, n):
         def body(i, carry):
             window = flat[pl.ds(pl.multiple_of(96 * i - 32, 32), 128)]
             store_rows(dst, 16 * i, mm(perm, window).astype(BF))
             return carry
 
         lax.fori_loop(1, n, body, 0)
-        return perm
 
     tail_v = one_hot(
         (96, 96),
@@ -673,15 +674,10 @@
     )
     mine_s, mine_c = part(0, z, y, c, None), part(1, z, y, c, None)
 
-    def rows_s():
-        store_rows(r.own_t, 0, mm(tail_v, r.tails[...]).astype(BF))
-        perm = lay_rows(0, r.flat_s, mine_s, 12)
-        tail.wait_recv()
-        store_rows(mine_s, 0, mm(perm, first_window(0, r.flat_s, 96)).astype(BF))
-
-    def rows_c():
-        perm = lay_rows(1, r.flat_c, mine_c, 17)
-        store_rows(mine_c, 0, mm(perm, first_window(1, r.flat_c, 96)).astype(BF))
+    perm_sc = to_rows(0)
+
+    def rows_first(g, flat, dst):
+        store_rows(dst, 0, mm(perm_sc, first_window(g, flat, 96)).astype(BF))
 
     def rows_f():
         @pl.when(w1)
@@ -1200,6 +1196,11 @@
             r.total_v[...] = jnp.zeros_like(r.total_v)
             remote(r.v_send, r.v_in.at[index], r.vv_s.at[0], r.vv_r.at[index], home).wait_send()
 
+    def flat_sc(g, nice, out, n):
+        arrived(nice.at[:, cols(1 - x)], r.fi_r.at[g])
+        lay_flat(nice, out, n)
+        head_out(g, out)
+
     def flat_f():
         @pl.when(w1)
         def _():
@@ -1223,8 +1224,18 @@
 
         head_out(2, r.out_f)
 
+    lay_rows(perm_sc, r.flat_s, mine_s, 12)
+    loads.flat_c.wait()
+    loads.flat_f.wait()
+    r.tails[0:32] = r.flat_s[1122:1154]
+    r.tails[32:64] = r.flat_c[1602:1634]
+    r.tails[64:96] = r.flat_f[4582:4614]
+    pl.semaphore_wait(barrier, len(near))
     tail.start()
-    rows_s()
+    store_rows(r.own_t, 0, mm(tail_v, r.tails[...]).astype(BF))
+    lay_rows(perm_sc, r.flat_c, mine_c, 17)
+    tail.wait_recv()
+    rows_first(0, r.flat_s, mine_s)
     own_z(0)
     own_y(0)
     own_core(0)
@@ -1232,98 +1243,101 @@
     pad_rows()
     rows_f()
     gather_y(0, 0)
-    rows_c()
+    own_y(2, 0)
+    own_y(3, 1)
+    gather_z(0, 0)
+    rows_first(1, r.flat_c, mine_c)
     vectors_on()
+    own_z(1)
+    gather_z(0, 1)
+    gather_z(0, 2)
+    own_z(2, 0)
+    own_core(1)
+    own_y(2, 1)
     own_y(1)
-    own_z(1)
-    gather_z(0, 0)
-    gather_z(0, 1)
-    own_y(2, 1)
+    gather_y(0, 1)
+    gather_y(0, 3)
+    gather_y(0, 2)
+    own_z(5, 1)
+    gather_z(1, 1)
+    gather_z(1, 0)
+    gather_x(0)
+    gather_z(1, 2)
+    own_z(4, 0)
+    own_z(2, 1)
+    gather_y(1, 2)
+    own_y(5, 0)
     gather_y(1, 0)
-    gather_z(0, 2)
-    gather_z(1, 1)
-    gather_y(0, 1)
-    own_core(1)
+    ffn_z(2, 1)
+    ffn_z(2, 0)
+    ffn_z(5, 3)
+    gather_y(1, 1)
+    gather_core(0, range(15))
+    own_y(4, 1)
+    own_z(3, 1)
     own_y(3, 0)
-    gather_y(0, 2)
-    own_y(5, 0)
-    own_z(2, 1)
+    ffn_z(2, 2)
+    ffn_z(5, 2)
+    gather_y(1, 3)
+    own_z(3, 0)
+    own_y(4, 0)
+    other_z(0)
+    vectors_in()
+    loads.hid.wait()
+    self_attention()
     own_y(5, 1)
-    own_z(3, 0)
-    gather_y(0, 3)
-    gather_z(1, 0)
-    own_z(4, 0)
-    other_z(0)
+    ffn_z(3, 1)
+    ffn_z(3, 2)
     own_z(4, 1)
-    ffn_z(2, 2)
-    gather_z(1, 2)
-    gather_x(0)
-    own_y(3, 1)
-    gather_core(0, range(15))
-    gather_y(1, 2)
-    own_y(4, 0)
-    own_z(3, 1)
-    gather_y(1, 1)
-    vectors_in()
-    self_attention()
-    ffn_z(3, 1)
+    gather_core(1, range(8))
+    loads.feat.wait()
+    image_rows(cols(x))
+    ffn_z(3, 3)
     ffn_z(2, 3)
-    gather_y(1, 3)
-    gather_core(1, range(8))
+    other_z(1)
+    ag_start(0, 1)
+    ffn_z(4, 2)
+    gather_x(1)
     ffn_z(4, 3)
-    ffn_z(4, 0)
-    other_z(1)
-    ffn_z(4, 1)
-    ffn_z(3, 2)
-    ffn_z(3, 3)
-    own_z(2, 0)
-    ffn_y(2, 3)
-    own_z(5, 1)
-    ag_start(0, 1)
-    own_y(4, 1)
-    image_rows(cols(x))
-    gather_x(1)
-    ffn_z(4, 2)
-    ffn_z(2, 1)
-    ffn_z(5, 0, other=True)
+    ffn_z(3, 0)
     gather_core(1, range(8, 15))
+    ffn_y(3, 2)
+    ffn_z(5, 1, other=True)
     own_z(5, 0)
     image_rows(cols(1 - x))
+    ffn_z(4, 1)
     ag_mid(0, 1)
+    ffn_y(3, 3)
     cross_start()
     cross_attention(0)
-    ffn_y(4, 3)
-    ffn_z(5, 3, other=True)
-    ffn_y(3, 3)
     cross_attention(1)
     cross_end()
-    ffn_z(5, 3)
-    ffn_z(5, 2)
+    ffn_y(4, 2)
+    ffn_z(5, 3, other=True)
+    ag_start(0, 0)
+    ffn_z(4, 0)
+    ffn_y(2, 3)
+    ag_end(0, 1)
+    ffn_y(3, 1)
+    ffn_y(3, 0)
+    ffn_y(2, 2)
     ffn_z(5, 2, other=True)
-    own_y(2, 0)
-    ffn_y(3, 1)
-    ffn_y(4, 0)
-    ag_end(0, 1)
-    ag_start(0, 0)
-    ffn_y(2, 2)
-    ffn_z(3, 0)
-    ffn_y(4, 2)
-    ffn_y(3, 2)
+    ffn_y(2, 0)
+    ffn_y(4, 3)
     ffn_forward_part(1)
     rs_start(0, 1)
-    ffn_z(2, 0)
+    rs_mid(0, 1)
+    ffn_z(5, 0, other=True)
+    ffn_y(2, 1)
     ag_mid(0, 0)
-    rs_mid(0, 1)
-    ffn_z(5, 1, other=True)
-    ffn_y(2, 1)
-    ffn_z(5, 0)
+    loads.cot.wait()
     ffn_turn(1)
     ag_start(1, 1)
-    ffn_y(3, 0)
     ffn_y(4, 1)
+    ffn_y(4, 0)
+    ffn_z(5, 1)
     ag_end(0, 0)
-    ffn_z(5, 1)
-    ffn_y(2, 0)
+    ffn_z(5, 0)
     ffn_forward_part(0)
     rs_start(0, 0)
     ag_mid(1, 1)
@@ -1335,15 +1349,15 @@
     ffn_turn(0)
     ag_start(1, 0)
     rs_start(1, 1)
+    rs_mid(1, 1)
     ag_mid(1, 0)
-    rs_mid(1, 1)
     ag_end(1, 0)
     ffn_backward_part(0)
     rs_start(1, 0)
+    text_end()
+    rs_mid(1, 0)
     ffn_weight_grads(0)
     ffn_sum_start(0)
-    rs_mid(1, 0)
-    text_end()
     query_end()
     cross_back()
     cross_grads()
@@ -1351,43 +1365,38 @@
     self_back()
     self_grads()
     vector_sums_out()
+    sum_core(1, (0,))
+    sum_start(0, 0)
+    sum_start(0, 1)
+    ffn_sum_y(0)
+    sum_core(0, (0,))
+    ffn_add(3)
+    ffn_sum_y(3)
+    ffn_sum_y(1)
+    sum_core(0, (1,))
     ffn_add(0)
-    ffn_add(3)
-    sum_start(0, 0)
-    sum_core(1, (0,))
-    ffn_sum_y(3)
-    ffn_sum_y(0)
-    sum_start(0, 1)
     ffn_sum_y(2)
-    sum_core(0, (0,))
     sum_start(1, 1)
+    z_add_sum(2, r.yf.at[3], 3)
     ffn_sum_other()
     vector_sums_z()
+    sum_mid(0, (0,))
     sum_core(1, (1,))
-    ffn_sum_y(1)
     z_add_sum(2, r.yf.at[0], 0)
-    sum_core(0, (1,))
-    z_add_sum(2, r.yf.at[3], 3)
     sum_mid(1, (0,))
+    sum_last(1)
     ffn_sum_z()
-    sum_mid(0, (0,))
-    sum_mid(1, (1,))
-    sum_last(1)
+    sum_mid(0, (1,))
     sum_last(0)
     vector_sums_x()
     sum_z(1)
     sum_z(0)
     ffn_end()
     flat_f()
+    flat_sc(1, r.nice_c, r.out_c, 17)
+    flat_sc(0, r.nice_s, r.out_s, 12)
     vector_sums_end()
     tail.wait_send()
-
-    arrived(groups[1][5].at[:, cols(1 - x)], r.fi_r.at[1])
-    lay_flat(r.nice_c, r.out_c, 17)
-    head_out(1, r.out_c)
-    arrived(groups[0][5].at[:, cols(1 - x)], r.fi_r.at[0])
-    lay_flat(r.nice_s, r.out_s, 12)
-    head_out(0, r.out_s)
 
     vectors = stack(r.total_v, 0)
     end = (f == 15, f == 15, f % 4 == 3)
@@ -1418,7 +1427,7 @@
     drain(sent)
 
 
-def layer(flat_s, flat_c, flat_f, tails, lens, hid, feat, cot):
+def layer(flat_s, flat_c, flat_f, lens, hid, feat, cot):
     vm = pl.BlockSpec(memory_space=pltpu.VMEM)
     return pl.pallas_call(
         layer_kernel,
@@ -1427,20 +1436,19 @@
             jax.ShapeDtypeStruct((128, D), BF),
             *[jax.ShapeDtypeStruct((n, 128), BF) for n in (1184, 1664, 4640)],
         ),
-        in_specs=[vm] * 4 + [pl.BlockSpec(memory_space=pltpu.SMEM)] + [vm] * 3,
+        in_specs=[vm] + [pl.BlockSpec(memory_space=pl.ANY)] * 2 + [pl.BlockSpec(memory_space=pltpu.SMEM)] + [pl.BlockSpec(memory_space=pl.ANY)] * 3,
         out_specs=[vm] * 5,
         scratch_shapes=list(scratch().values()),
         compiler_params=pltpu.CompilerParams(
             collective_id=0, has_side_effects=True, vmem_limit_bytes=VMEM_BYTES
         ),
-    )(flat_s, flat_c, flat_f, tails, lens, hid, feat, cot)
+    )(flat_s, flat_c, flat_f, lens, hid, feat, cot)
 
 
 def per_device_fast(hidden, lengths, features, cotangent, self_params, cross_params, ffn_params):
     flats = [v.reshape(-1, 128) for v in (self_params, cross_params, ffn_params)]
-    tails = jnp.concatenate([v[-32:] for v in flats])
     mixed, hgrad, *grads = layer(
-        *flats, tails, lengths, hidden.reshape(128, D), features, cotangent.reshape(128, D)
+        *flats, lengths, hidden.reshape(128, D), features, cotangent.reshape(128, D)
     )
     outs = [
         lax.dynamic_slice_in_dim(rows, back, flat.shape[0]).astype(F32).reshape(-1)

time: 231 us -> 225 us (0.974)
  Pallas kernels: 218 us -> 212 us
    pallas_call x1, Pallas kernels: 218 us -> 212 us  [layer(): pl.pallas_call(layer_kernel, out_shape=(jax.ShapeDtypeStruct((128, D), BF...]
where the time goes in v7:
time: 225 us; the launch traced here: 221 us
  Pallas kernels  212 us (94%)
  other arithmetic  4.83 us (2%)
  local copies, waits for them, and re-layouts  4 us (2%)
    pallas_call x1, Pallas kernels, layer(): pl.pallas_call(layer_kernel, out_shape=(jax.ShapeDtypeStruct((128, D), BF...  212 us
    reshape x3, other arithmetic, per_device_fast(): lax.dynamic_slice_in_dim(rows, back, flat.shape[0]).astype(F32).reshape(-1)  4.83 us

profile of v7, /device:TPU:0, one launch (start us, length us, event | category | flops | bytes accessed | tf_op | source)
XLA Modules:
  0.0 221.3 jit_solution(1402393770988847559)
XLA Ops:
  0.7 2.6 %copy.12.refs_5_ = bf16[2,257,1408]{2,1,0:T(8,128)(2,1)} copy(bf16[2,257,1408]{2,0,1:T(2,128)(2,1)} %param.9) | data formatting | bytes 2894848 | tf_op args[2]
  3.3 211.8 %shard_map.110 = (bf16[128,768]{1,0:T(8,128)(2,1)}, bf16[128,768]{1,0:T(8,128)(2,1)}, bf16[1184,128]{1,0:T(8,128)(2,1)}, bf16[1664,128]{1,0:T(8,128)(2,1)}, bf16[4640,128]{1,0:T(8,128)(2,1)}) custom-call(bf16[1154,128]{1,0:T(8,128)(2,1)} %bitcast.18, bf16[1634,128]{1,0:T(8,128)(2,1)} %bitcast.17, bf16[4614,128]{1,0:T(8,128)(2,1)} %bitcast.16, s32[2]{0:T(128)} %refs_3_.1, ...), custom_call_target="tpu_custom_call" | custom-call | tf_op jit(solution)/shard_map/pallas_call | solution.py:1432
  215.1 0.0 copy-start
  215.1 3.0 %bitcast_convert_fusion = f32[590592]{0:T(1024)} fusion(bf16[4640,128]{1,0:T(8,128)(2,1)} %get-tuple-element.14, s32[]{:T(128)S(6)} %select_n.24), kind=kLoop, calls=%fused_computation | loop fusion | flops 590592 | bytes 3543556 | tf_op jit(solution)/shard_map/reshape | solution.py:1454
  218.1 0.0 copy-start.1
  218.1 0.0 copy-start.3
  218.1 0.0 copy-start.2
  218.1 0.0 copy-done
  218.1 1.0 bitcast_convert_fusion.1
  219.1 0.0 copy-done.1
  219.1 0.9 bitcast_convert_fusion.2
  220.0 0.0 copy-done.3
  220.0 0.7 copy.15
  220.6 0.0 copy-done.2
  220.6 0.7 copy.16
Async XLA Ops:
  215.1 3.0 %copy-start = (bf16[1664,128]{1,0:T(8,128)(2,1)S(1)}, bf16[1664,128]{1,0:T(8,128)(2,1)}, u32[]{:S(2)}) copy-start(bf16[1664,128]{1,0:T(8,128)(2,1)} %get-tuple-element.13) | copy-start | bytes 1277956
  218.1 1.0 copy-start.1
  218.1 1.9 copy-start.3
  218.1 2.6 %copy-start.2 = (bf16[128,768]{1,0:T(8,128)(2,1)S(1)}, bf16[128,768]{1,0:T(8,128)(2,1)}, u32[]{:S(2)}) copy-start(bf16[128,768]{1,0:T(8,128)(2,1)} %get-tuple-element.11) | copy-start | bytes 589828

commit v8 on v7

--- a/solution.py
+++ b/solution.py
@@ -383,12 +383,10 @@
 
 
 def gelu(v):
-    return 0.5 * v * (1.0 + jnp.tanh(GELU_A * (v + GELU_B * (v * v * v))))
-
-
-def gelu_slope(v):
-    t = jnp.tanh(GELU_A * (v + GELU_B * (v * v * v)))
-    return 0.5 * (1.0 + t) + 0.5 * v * (1.0 - t * t) * (GELU_A * (1.0 + 3.0 * GELU_B * (v * v)))
+    square = v * v
+    t = jnp.tanh(GELU_A * (v + GELU_B * (square * v)))
+    half = 0.5 + 0.5 * t
+    return v * half, half + 0.5 * v * (1.0 - t * t) * (GELU_A * (1.0 + 3.0 * GELU_B * square))
 
 
 def head_mask(h):
@@ -860,8 +858,9 @@
 
     def ffn_forward_part(b):
         rows = r.xg[0, b].reshape(256, D)
-        r.pre[b] = mm(rows, r.wf[2 * b]) + ffn_b1(b)
-        r.act[b] = gelu(r.pre[b]).astype(BF)
+        value, slope = gelu(mm(rows, r.wf[2 * b]) + ffn_b1(b))
+        r.act[b] = value.astype(BF)
+        r.pre[b] = slope
         r.part[b] = mm(r.act[b], r.wf[2 * b + 1]).reshape(4, 64, D)
 
     def ffn_turn(b):
@@ -880,27 +879,27 @@
         r.vg[2 * b + 1, 11:12] = dgain
         r.vg[2 * b + 1, 12:13] = dshift
 
-    def ffn_backward_part(b):
+    def ffn_back_hidden(b):
         up = r.xg[1, b].reshape(256, D)
-        r.dpre[b] = (mm_nt(up, r.wf[2 * b + 1]) * gelu_slope(r.pre[b])).astype(BF)
+        r.dpre[b] = (mm_nt(up, r.wf[2 * b + 1]) * r.pre[b]).astype(BF)
+
+    def ffn_back_rows(b):
         r.part[b] = mm_nt(r.dpre[b], r.wf[2 * b]).reshape(4, 64, D)
+
+    def ffn_grad_out(b):
+        drain(sent_f[b])
+        r.wf[2 * b + 1] = mm_tn(r.act[b], r.xg[1, b].reshape(256, D)).astype(BF)
+
+    def ffn_grad_in(b):
+        r.wf[2 * b] = mm_tn(r.xg[0, b].reshape(256, D), r.dpre[b]).astype(BF)
         db1 = rows_sum(r.dpre[b])
         for j in range(4):
             r.vg[2 * b, 10 + j : 11 + j] = jnp.where(j == me, db1, 0.0)
 
-    def ffn_weight_grads(b):
-        drain(sent_f[b])
-        rows = r.xg[0, b].reshape(256, D)
-        up = r.xg[1, b].reshape(256, D)
-        r.wf[2 * b] = mm_tn(rows, r.dpre[b]).astype(BF)
-        r.wf[2 * b + 1] = mm_tn(r.act[b], up).astype(BF)
-
-    def ffn_sum_start(b):
-        for p in (2 * b, 2 * b + 1):
-            go(sent, part_f(p, 1 - y, 0, SPLIT), r.yf.at[p], r.yy_s.at[2, p], r.yy_r.at[2, p], yn)
-        for p in (2 * b, 2 * b + 1):
-            for i, yy in ((4, 1 - y), (3, y)):
-                z_out_sum(i, part_f(p, yy, SPLIT, REST), p)
+    def ffn_sum_start(p):
+        go(sent, part_f(p, 1 - y, 0, SPLIT), r.yf.at[p], r.yy_s.at[2, p], r.yy_r.at[2, p], yn)
+        for i, yy in ((4, 1 - y), (3, y)):
+            z_out_sum(i, part_f(p, yy, SPLIT, REST), p)
 
     hop = jnp.where(z < 2, 1, 2)
 
@@ -1113,11 +1112,16 @@
         drain(sent_w[1])
         r.wc[3584:4352] = mm_tn(r.ca[...], keep.low2).astype(BF)
         r.wc[0:768] = mm_tn(rows_of(r.first, 0).astype(BF), keep.dcq).astype(BF)
+        last = lambda ref: jnp.concatenate([ref[0].astype(F32), ref[1].astype(F32), jnp.zeros((14, ref[0].shape[1]), F32)], 0).astype(BF)
+        rest = {n: last([d[256:257], d[528:529]]) for n, d in (("k", r.ck), ("v", r.cv))}
         for j in range(11):
-            block = [r.feat[i, :, 128 * j : 128 * j + 128] for i in range(2)]
-            both = lambda d: mm_tn(block[0], d[0:257]) + mm_tn(block[1], d[272:529])
-            r.wc[768 + 128 * j : 896 + 128 * j] = both(r.ck).astype(BF)
-            r.wc[2176 + 128 * j : 2304 + 128 * j] = both(r.cv).astype(BF)
+            lanes = slice(128 * j, 128 * j + 128)
+            tail_rows = last([r.feat[i, 256:257, lanes] for i in range(2)])
+            both = lambda d, n: (
+                mm_tn(r.feat[0, 0:256, lanes], d[0:256]) + mm_tn(r.feat[1, 0:256, lanes], d[272:528]) + mm_tn(tail_rows, rest[n])
+            )
+            r.wc[768 + 128 * j : 896 + 128 * j] = both(r.ck, "k").astype(BF)
+            r.wc[2176 + 128 * j : 2304 + 128 * j] = both(r.cv, "v").astype(BF)
 
     def self_back():
         dsum1, dgain, dshift = norm_back(r.sum1[...], self_v(3), r.dfirst[...])
@@ -1343,20 +1347,26 @@
     ag_mid(1, 1)
     rs_mid(0, 0)
     ag_end(1, 1)
-    ffn_backward_part(1)
-    ffn_weight_grads(1)
-    ffn_sum_start(1)
+    ffn_back_hidden(1)
+    ffn_back_rows(1)
+    ffn_grad_out(1)
+    ffn_grad_in(1)
+    ffn_sum_start(3)
+    ffn_sum_start(2)
     ffn_turn(0)
     ag_start(1, 0)
     rs_start(1, 1)
     rs_mid(1, 1)
     ag_mid(1, 0)
     ag_end(1, 0)
-    ffn_backward_part(0)
+    ffn_back_hidden(0)
+    ffn_back_rows(0)
     rs_start(1, 0)
     text_end()
     rs_mid(1, 0)
-    ffn_weight_grads(0)
+    ffn_grad_out(0)
+    ffn_grad_in(0)
+    ffn_sum_start(1)
     ffn_sum_start(0)
     query_end()
     cross_back()

time: 225 us -> 221 us (0.982)
  Pallas kernels: 212 us -> 208 us
    pallas_call x1, Pallas kernels: 212 us -> 208 us  [layer(): pl.pallas_call(layer_kernel, out_shape=(jax.ShapeDtypeStruct((128, D), BF...]
where the time goes in v8:
time: 221 us; the launch traced here: 218 us
  Pallas kernels  208 us (94%)
  other arithmetic  4.83 us (2%)
  local copies, waits for them, and re-layouts  4 us (2%)
    pallas_call x1, Pallas kernels, layer(): pl.pallas_call(layer_kernel, out_shape=(jax.ShapeDtypeStruct((128, D), BF...  208 us
    reshape x3, other arithmetic, per_device_fast(): lax.dynamic_slice_in_dim(rows, back, flat.shape[0]).astype(F32).reshape(-1)  4.83 us

profile of v8, /device:TPU:0, one launch (start us, length us, event | category | flops | bytes accessed | tf_op | source)
XLA Modules:
  0.0 217.6 jit_solution(9800765787823974439)
XLA Ops:
  0.7 2.6 %copy.12.refs_5_ = bf16[2,257,1408]{2,1,0:T(8,128)(2,1)} copy(bf16[2,257,1408]{2,0,1:T(2,128)(2,1)} %param.9) | data formatting | bytes 2894848 | tf_op args[2]
  3.3 208.1 %shard_map.110 = (bf16[128,768]{1,0:T(8,128)(2,1)}, bf16[128,768]{1,0:T(8,128)(2,1)}, bf16[1184,128]{1,0:T(8,128)(2,1)}, bf16[1664,128]{1,0:T(8,128)(2,1)}, bf16[4640,128]{1,0:T(8,128)(2,1)}) custom-call(bf16[1154,128]{1,0:T(8,128)(2,1)} %bitcast.18, bf16[1634,128]{1,0:T(8,128)(2,1)} %bitcast.17, bf16[4614,128]{1,0:T(8,128)(2,1)} %bitcast.16, s32[2]{0:T(128)} %refs_3_.1, ...), custom_call_target="tpu_custom_call" | custom-call | tf_op jit(solution)/shard_map/pallas_call | solution.py:1442
  211.4 0.0 copy-start
  211.4 3.0 %bitcast_convert_fusion = f32[590592]{0:T(1024)} fusion(bf16[4640,128]{1,0:T(8,128)(2,1)} %get-tuple-element.14, s32[]{:T(128)S(6)} %select_n.24), kind=kLoop, calls=%fused_computation | loop fusion | flops 590592 | bytes 3543556 | tf_op jit(solution)/shard_map/reshape | solution.py:1464
  214.4 0.0 copy-start.1
  214.4 0.0 copy-start.3
  214.4 0.0 copy-start.2
  214.4 0.0 copy-done
  214.4 1.0 bitcast_convert_fusion.1
  215.4 0.0 copy-done.1
  215.4 0.9 bitcast_convert_fusion.2
  216.3 0.0 copy-done.3
  216.3 0.7 copy.15
  216.9 0.0 copy-done.2
  216.9 0.7 copy.16
Async XLA Ops:
  211.4 3.0 %copy-start = (bf16[1664,128]{1,0:T(8,128)(2,1)S(1)}, bf16[1664,128]{1,0:T(8,128)(2,1)}, u32[]{:S(2)}) copy-start(bf16[1664,128]{1,0:T(8,128)(2,1)} %get-tuple-element.13) | copy-start | bytes 1277956
  214.4 1.0 copy-start.1
  214.4 1.9 copy-start.3
  214.4 2.6 %copy-start.2 = (bf16[128,768]{1,0:T(8,128)(2,1)S(1)}, bf16[128,768]{1,0:T(8,128)(2,1)}, u32[]{:S(2)}) copy-start(bf16[128,768]{1,0:T(8,128)(2,1)} %get-tuple-element.11) | copy-start | bytes 589828

commit v9 on v8

--- a/solution.py
+++ b/solution.py
@@ -545,7 +545,7 @@
         return sent_w[g] if g < 2 else sent_f[b]
 
     def z_out(src, dst, g, i, b=None):
-        for k in (2, 1, 3):
+        for k in (1, 3, 2):
             cond = both({1: z != 3, 2: None, 3: z != 0}[k], None if b is None else branch[b])
             go(sent_of(g, b), src, dst, r.gz_s.at[i, k], r.gz_r.at[i, k], zdev(k), cond)
 
@@ -1350,8 +1350,8 @@
     ffn_back_hidden(1)
     ffn_back_rows(1)
     ffn_grad_out(1)
+    ffn_sum_start(3)
     ffn_grad_in(1)
-    ffn_sum_start(3)
     ffn_sum_start(2)
     ffn_turn(0)
     ag_start(1, 0)
@@ -1365,8 +1365,8 @@
     text_end()
     rs_mid(1, 0)
     ffn_grad_out(0)
+    ffn_sum_start(1)
     ffn_grad_in(0)
-    ffn_sum_start(1)
     ffn_sum_start(0)
     query_end()
     cross_back()

time: 221 us -> 218 us (0.986)
  Pallas kernels: 208 us -> 205 us
    pallas_call x1, Pallas kernels: 208 us -> 205 us  [layer(): pl.pallas_call(layer_kernel, out_shape=(jax.ShapeDtypeStruct((128, D), BF...]
where the time goes in v9:
time: 218 us; the launch traced here: 215 us
  Pallas kernels  205 us (94%)
  other arithmetic  4.83 us (2%)
  local copies, waits for them, and re-layouts  4 us (2%)
    pallas_call x1, Pallas kernels, layer(): pl.pallas_call(layer_kernel, out_shape=(jax.ShapeDtypeStruct((128, D), BF...  205 us
    reshape x3, other arithmetic, per_device_fast(): lax.dynamic_slice_in_dim(rows, back, flat.shape[0]).astype(F32).reshape(-1)  4.83 us

profile of v9, /device:TPU:0, one launch (start us, length us, event | category | flops | bytes accessed | tf_op | source)
XLA Modules:
  0.0 214.9 jit_solution(5600806492197192950)
XLA Ops:
  0.7 2.6 %copy.12.refs_5_ = bf16[2,257,1408]{2,1,0:T(8,128)(2,1)} copy(bf16[2,257,1408]{2,0,1:T(2,128)(2,1)} %param.9) | data formatting | bytes 2894848 | tf_op args[2]
  3.3 205.4 %shard_map.110 = (bf16[128,768]{1,0:T(8,128)(2,1)}, bf16[128,768]{1,0:T(8,128)(2,1)}, bf16[1184,128]{1,0:T(8,128)(2,1)}, bf16[1664,128]{1,0:T(8,128)(2,1)}, bf16[4640,128]{1,0:T(8,128)(2,1)}) custom-call(bf16[1154,128]{1,0:T(8,128)(2,1)} %bitcast.18, bf16[1634,128]{1,0:T(8,128)(2,1)} %bitcast.17, bf16[4614,128]{1,0:T(8,128)(2,1)} %bitcast.16, s32[2]{0:T(128)} %refs_3_.1, ...), custom_call_target="tpu_custom_call" | custom-call | tf_op jit(solution)/shard_map/pallas_call | solution.py:1442
  208.7 0.0 copy-start
  208.7 3.0 %bitcast_convert_fusion = f32[590592]{0:T(1024)} fusion(bf16[4640,128]{1,0:T(8,128)(2,1)} %get-tuple-element.14, s32[]{:T(128)S(6)} %select_n.24), kind=kLoop, calls=%fused_computation | loop fusion | flops 590592 | bytes 3543556 | tf_op jit(solution)/shard_map/reshape | solution.py:1464
  211.7 0.0 copy-start.1
  211.7 0.0 copy-start.3
  211.7 0.0 copy-start.2
  211.7 0.0 copy-done
  211.7 1.0 bitcast_convert_fusion.1
  212.7 0.0 copy-done.1
  212.7 0.9 bitcast_convert_fusion.2
  213.5 0.0 copy-done.3
  213.5 0.7 copy.15
  214.2 0.0 copy-done.2
  214.2 0.7 copy.16
Async XLA Ops:
  208.7 3.0 %copy-start = (bf16[1664,128]{1,0:T(8,128)(2,1)S(1)}, bf16[1664,128]{1,0:T(8,128)(2,1)}, u32[]{:S(2)}) copy-start(bf16[1664,128]{1,0:T(8,128)(2,1)} %get-tuple-element.13) | copy-start | bytes 1277956
  211.7 1.0 copy-start.1
  211.7 1.9 copy-start.3
  211.7 2.6 %copy-start.2 = (bf16[128,768]{1,0:T(8,128)(2,1)S(1)}, bf16[128,768]{1,0:T(8,128)(2,1)}, u32[]{:S(2)}) copy-start(bf16[128,768]{1,0:T(8,128)(2,1)} %get-tuple-element.11) | copy-start | bytes 589828
